TPU v7x, 768 devices: a whole 4x8x12 slice. The times are simulated.
768 devices in a mesh: gx: 64 (over x, y, core), gy: 12 (over z).
Axes of the slice: x: 4, y: 8, z: 12, core: 2. Of those that a mesh axis runs over, the one named last changes fastest.
Arguments:
- right_side: float32 [3, 256, 96, 256], P(None, 'gx', 'gy'), may hold values from -24 to 24
- block_matrix: float32 [3, 3, 256, 96, 256], P(None, None, 'gx', 'gy'), may hold values from -1 to 8, as said below
- mobility: float32 [3, 256, 96, 256], P(None, 'gx', 'gy'), may hold values from 0.2 to 1
- trans: float32 [6, 256, 96, 256], P(None, 'gx', 'gy'), may hold values from 0.02 to 1
- active_mask: int32 [256, 96, 256], P('gx', 'gy'), may hold values 0 or 1
- cell_map: int32 [256, 96, 256], P('gx', 'gy'), may hold values from 0 to 63
- coarse_owner: int32 [64, 12], P('gx', 'gy'), may hold values from 0 to 11, each once within a row
- coarse_rows: float32 [49152, 768], P(('gx', 'gy')), may hold values from -0.109375 to 0.109375
Outputs:
- solution: float32 [3, 256, 96, 256], P(None, 'gx', 'gy')
Inputs may be any that keep to these rules, and one draw needn't show every extreme that they name: `coarse_owner`: each row holds every rank of 0 to 11 once. `block_matrix`: each cell's block has a positive diagonal, a positive first column, and is strictly diagonally dominant by rows.
All inputs are finite; a program needn't handle non-finite values. No bound on the sum of `active_mask` on one device may be relied on, other than what follows from the above.
Results may differ from a plain program's by a relative error of at most 0.0065.
Values sent between devices are 32-bit elements; how exact they have to be, the bound alone decides.
No kernel may reach another device: no remote copies, remote signals or barrier semaphores. Data moves between devices by JAX's collectives and lax.ppermute only.
A program may use at most 32 MiB of HBM per device.

v0:
```python
import jax
import jax.numpy as jnp
from jax import lax
from jax.sharding import PartitionSpec as P

SMOOTH = 2


damping = 0.8


def padded_2(cells, sides, width):
    for axis, dim in sides:
        count = lax.axis_size(axis)
        ends = count - 1
        head = lax.slice_in_dim(cells, 0, width, axis=dim)
        tail = lax.slice_in_dim(cells, cells.shape[dim] - width, cells.shape[dim], axis=dim)
        cells = jnp.concatenate(
            [
                lax.ppermute(tail, axis, [(i, (i + 1) % count) for i in range(ends)]),
                cells,
                lax.ppermute(head, axis, [((i + 1) % count, i) for i in range(ends)]),
            ],
            axis=dim,
        )
    return cells


def face_values(padded):
    centre = padded[..., 1:-1, 1:-1, :]
    zero_rim = jnp.zeros_like(centre[..., :1])
    return (
        padded[..., 2:, 1:-1, :],
        padded[..., :-2, 1:-1, :],
        padded[..., 1:-1, 2:, :],
        padded[..., 1:-1, :-2, :],
        jnp.concatenate([centre[..., 1:], zero_rim], -1),
        jnp.concatenate([zero_rim, centre[..., :-1]], -1),
    )


def neighbour_sum(padded, coefficients):
    neighbours = face_values(padded)
    running = coefficients[0] * neighbours[0]
    for side_index in range(1, 6):
        running = running + coefficients[side_index] * neighbours[side_index]
    return running


def faces(field_in):
    return padded_2(field_in, (("gx", 1), ("gy", 2)), 1)


def block_inverse(matrix, mask_float):
    entry = [
        [
            mask_float * matrix[row_index, col_index]
            + (1.0 - mask_float) * (1.0 if row_index == col_index else 0.0)
            for col_index in range(3)
        ]
        for row_index in range(3)
    ]
    cof_00 = entry[1][1] * entry[2][2] - entry[1][2] * entry[2][1]
    cof_01 = -(entry[1][0] * entry[2][2] - entry[1][2] * entry[2][0])
    cof_02 = entry[1][0] * entry[2][1] - entry[1][1] * entry[2][0]
    cof_10 = -(entry[0][1] * entry[2][2] - entry[0][2] * entry[2][1])
    cof_11 = entry[0][0] * entry[2][2] - entry[0][2] * entry[2][0]
    cof_12 = -(entry[0][0] * entry[2][1] - entry[0][1] * entry[2][0])
    cof_20 = entry[0][1] * entry[1][2] - entry[0][2] * entry[1][1]
    cof_21 = -(entry[0][0] * entry[1][2] - entry[0][2] * entry[1][0])
    cof_22 = entry[0][0] * entry[1][1] - entry[0][1] * entry[1][0]
    determinant = entry[0][0] * cof_00 + entry[0][1] * cof_01 + entry[0][2] * cof_02
    recip = 1.0 / determinant
    return jnp.stack(
        [
            jnp.stack([cof_00 * recip, cof_10 * recip, cof_20 * recip]),
            jnp.stack([cof_01 * recip, cof_11 * recip, cof_21 * recip]),
            jnp.stack([cof_02 * recip, cof_12 * recip, cof_22 * recip]),
        ]
    )


def on_device(
    right_side, block_matrix, mobility, trans, active_mask, cell_map, coarse_owner, coarse_rows
):
    highest = lax.Precision.HIGHEST
    mask_float = active_mask.astype(jnp.float32)
    mob_total = mobility[0] + mobility[1] + mobility[2]
    coupling = (mask_float * mob_total)[None] * trans
    diag_p = mask_float * (block_matrix[0, 0] + block_matrix[1, 0] + block_matrix[2, 0]) + (
        1.0 - mask_float
    )
    inv_diag = 1.0 / diag_p
    inverse = block_inverse(block_matrix, mask_float)
    aggregates = coarse_rows.shape[0]
    group_size = lax.axis_size("gy")
    onehot = (
        cell_map.reshape(-1)[None, :] == jnp.arange(aggregates, dtype=jnp.int32)[:, None]
    ).astype(jnp.float32)
    owner_pick = (jnp.arange(group_size, dtype=jnp.int32) == coarse_owner[0, 0]).astype(jnp.float32)

    def operate(field_in):
        neighbour = neighbour_sum(faces(mask_float[None] * field_in), trans)
        row_list = []
        for row_index in range(3):
            direct = (
                block_matrix[row_index, 0] * field_in[0]
                + block_matrix[row_index, 1] * field_in[1]
                + block_matrix[row_index, 2] * field_in[2]
            )
            flux_sum = neighbour[0] if row_index == 0 else neighbour[0] + neighbour[row_index]
            row_list.append(
                mask_float * (direct - mobility[row_index] * flux_sum)
                + (1.0 - mask_float) * field_in[row_index]
            )
        return jnp.stack(row_list)

    def precondition(residual_in):
        pressure_rhs = residual_in[0] + residual_in[1] + residual_in[2]
        coarse_local = jnp.dot(onehot, pressure_rhs.reshape(-1), precision=highest)
        coarse_all = lax.all_gather(coarse_local, "gy", axis=0, tiled=True)
        owned = jnp.dot(coarse_rows, coarse_all, precision=highest)
        returned = lax.all_gather(owned, "gy", axis=0, tiled=True).reshape(group_size, aggregates)
        own_values = jnp.dot(owner_pick, returned, precision=highest)
        pressure = jnp.dot(own_values, onehot, precision=highest).reshape(pressure_rhs.shape)
        for sweep_index in range(SMOOTH):
            padded = faces((mask_float * pressure)[None])[0]
            pressure = pressure + damping * inv_diag * (
                pressure_rhs - diag_p * pressure + neighbour_sum(padded, coupling)
            )
        neighbour = neighbour_sum(faces((mask_float * pressure)[None])[0], trans)
        second = []
        for row_index in range(3):
            applied = mask_float * (
                block_matrix[row_index, 0] * pressure - mobility[row_index] * neighbour
            )
            if row_index == 0:
                applied = applied + (1.0 - mask_float) * pressure
            second.append(residual_in[row_index] - applied)
        result = []
        for row_index in range(3):
            smoothed = (
                inverse[row_index, 0] * second[0]
                + inverse[row_index, 1] * second[1]
                + inverse[row_index, 2] * second[2]
            )
            result.append(pressure + smoothed if row_index == 0 else smoothed)
        return jnp.stack(result)

    first_z = precondition(right_side)
    first_w = operate(first_z)
    gram_one, proj_one = lax.psum(
        (jnp.sum(first_w * first_w), jnp.sum(first_w * right_side)), ("gx", "gy")
    )
    scaled = first_w * (1.0 / jnp.sqrt(gram_one + 1e-06))
    second_z = precondition(scaled)
    second_w = operate(second_z)
    gram_cross, gram_two, proj_two = lax.psum(
        (jnp.sum(first_w * second_w), jnp.sum(second_w * second_w), jnp.sum(second_w * right_side)),
        ("gx", "gy"),
    )
    determinant = gram_one * gram_two - gram_cross * gram_cross
    coeff_one = (gram_two * proj_one - gram_cross * proj_two) / determinant
    coeff_two = (gram_one * proj_two - gram_cross * proj_one) / determinant
    return coeff_one * first_z + coeff_two * second_z


def solution(mesh):
    in_specs = (
        P(None, "gx", "gy", None),
        P(None, None, "gx", "gy", None),
        P(None, "gx", "gy", None),
        P(None, "gx", "gy", None),
        P("gx", "gy", None),
        P("gx", "gy", None),
        P("gx", "gy"),
        P(("gx", "gy"), None),
    )
    out_specs = P(None, "gx", "gy", None)
    return jax.shard_map(
        on_device, mesh=mesh, in_specs=in_specs, out_specs=out_specs, check_vma=False
    )
```

profile of v0, /device:TPU:1, one launch (start us, length us, event | category | flops | bytes accessed | tf_op | source)
XLA Modules:
  0.0 481.8 jit_solution(516155254224907498)
XLA Ops:
  4.9 28.6 %all-reduce.16 = f32[768]{0:T(1024)S(1)} all-reduce(f32[768]{0:T(1024)S(1)} %dynamic-update-slice), channel_id=1, replica_groups=mesh['gx'=64,'gy'=12] {'gy'}, use_global_device_ids=true, to_apply=%add.16 | all-reduce | flops 768 | bytes 6144
  34.0 15.4 %all-reduce.17 = f32[768]{0:T(1024)S(1)} all-reduce(f32[768]{0:T(1024)S(1)} %dynamic-update-slice.1), channel_id=1, replica_groups=mesh['gx'=64,'gy'=12] {'gy'}, use_global_device_ids=true, to_apply=%add.17 | all-reduce | flops 768 | bytes 6144
  52.0 14.6 %collective-permute-start = (f32[1,1,8,256]{3,2,1,0:T(8,128)S(1)}, f32[1,1,8,256]{3,2,1,0:T(8,128)S(1)}, u32[]{:S(2)}, u32[]{:S(2)}) collective-permute-start(f32[1,1,8,256]{3,2,1,0:T(8,128)S(1)} %get-tuple-element.120), channel_id=1, source_target_pairs={{0,12},{12,24},{24,36},{36,48},{48,60},{60,72},{72,84},{84,96},{96... | collective-permute-start | bytes 24584 | tf_op jit(solution)/shard_map/ppermute | solution.py:20
  68.5 3.0 collective-permute-done.1
  71.5 3.6 collective-permute-start.2
  76.5 3.0 collective-permute-done.3
  79.8 3.4 collective-permute-start.4
  85.1 3.0 collective-permute-done.5
  91.1 3.0 collective-permute-done.7
  94.4 3.4 collective-permute-start.8
  99.7 3.0 collective-permute-done.9
  102.7 2.4 collective-permute-start.10
  106.5 3.1 collective-permute-done.11
  111.8 3.6 collective-permute-start.13
  117.7 4.0 collective-permute-start.15
  123.4 120.9 %psum.35 = f32[]{:T(128)} all-reduce(f32[]{:T(128)} %multiply_reduce_fusion.4), channel_id=1, replica_groups=mesh['gx'=64,'gy'=12] {'gx','gy'}, use_global_device_ids=true, to_apply=%region_1.0 | all-reduce | flops 1 | bytes 8 | tf_op jit(solution)/shard_map/psum | solution.py:152
  246.3 18.4 %all-reduce.18 = f32[768]{0:T(1024)S(1)} all-reduce(f32[768]{0:T(1024)S(1)} %dynamic-update-slice.2), channel_id=1, replica_groups=mesh['gx'=64,'gy'=12] {'gy'}, use_global_device_ids=true, to_apply=%add.18 | all-reduce | flops 768 | bytes 6144
  265.2 15.4 %all-reduce.19 = f32[768]{0:T(1024)S(1)} all-reduce(f32[768]{0:T(1024)S(1)} %dynamic-update-slice.3), channel_id=1, replica_groups=mesh['gx'=64,'gy'=12] {'gy'}, use_global_device_ids=true, to_apply=%add.19 | all-reduce | flops 768 | bytes 6144
  281.5 11.4 %collective-permute-start.16 = (f32[1,1,8,256]{3,2,1,0:T(8,128)S(1)}, f32[1,1,8,256]{3,2,1,0:T(8,128)S(1)}, u32[]{:S(2)}, u32[]{:S(2)}) collective-permute-start(f32[1,1,8,256]{3,2,1,0:T(8,128)S(1)} %get-tuple-element.104), channel_id=1, source_target_pairs={{0,12},{12,24},{24,36},{36,48},{48,60},{60,72},{72,84},{84,96},{96... | collective-permute-start | bytes 24584 | tf_op jit(solution)/shard_map/ppermute | solution.py:20
  292.9 3.1 collective-permute-start.17
  297.9 3.6 collective-permute-start.18
  302.8 3.4 collective-permute-done.19
  306.4 3.1 collective-permute-start.20
  311.4 3.0 collective-permute-done.21
  317.4 3.1 collective-permute-done.23
  320.7 3.4 collective-permute-start.24
  326.0 3.0 collective-permute-done.25
  329.0 3.5 collective-permute-start.26
  333.9 3.3 collective-permute-done.27
  339.4 3.6 collective-permute-start.29
  345.3 4.3 collective-permute-start.31
  351.3 122.3 %all-reduce.20 = (f32[]{:T(128)}, f32[]{:T(128)}, f32[]{:T(128)}, f32[]{:T(128)}) all-reduce(f32[]{:T(128)} %get-tuple-element.8, f32[]{:T(128)} %get-tuple-element.6, f32[]{:T(128)} %get-tuple-element.7, f32[]{:T(128)} %get-tuple-element.5), channel_id=1, replica_groups=mesh['gx'=64,'gy'=12] {'gx','gy'}, use_global_device_ids=true, to_apply=%region_9.0 | all-reduce | flops 4 | bytes 32 | tf_op jit(solution)/shard_map/psum | solution.py:158
  (137 shorter events, 45.5 us)
Async XLA Ops:
  52.0 16.5 %collective-permute-start = (f32[1,1,8,256]{3,2,1,0:T(8,128)S(1)}, f32[1,1,8,256]{3,2,1,0:T(8,128)S(1)}, u32[]{:S(2)}, u32[]{:S(2)}) collective-permute-start(f32[1,1,8,256]{3,2,1,0:T(8,128)S(1)} %get-tuple-element.120), channel_id=1, source_target_pairs={{0,12},{12,24},{24,36},{36,48},{48,60},{60,72},{72,84},{84,96},{96... | collective-permute-start | bytes 24584 | tf_op jit(solution)/shard_map/ppermute | solution.py:20
  66.6 5.0 %collective-permute-start.1 = (f32[1,1,8,256]{3,2,1,0:T(8,128)S(1)}, f32[1,1,8,256]{3,2,1,0:T(8,128)S(1)}, u32[]{:S(2)}, u32[]{:S(2)}) collective-permute-start(f32[1,1,8,256]{3,2,1,0:T(8,128)S(1)} %get-tuple-element.121), channel_id=1, source_target_pairs={{12,0},{24,12},{36,24},{48,36},{60,48},{72,60},{84,72},{96,84},{10... | collective-permute-start | bytes 24584 | tf_op jit(solution)/shard_map/ppermute | solution.py:22
  71.5 5.0 %collective-permute-start.2 = (f32[1,6,1,256]{3,2,1,0:T(1,128)S(1)}, f32[1,6,1,256]{3,2,1,0:T(1,128)S(1)}, u32[]{:S(2)}, u32[]{:S(2)}) collective-permute-start(f32[1,6,1,256]{3,2,1,0:T(1,128)S(1)} %get-tuple-element.98), channel_id=1, source_target_pairs={{0,1},{1,2},{2,3},{3,4},{4,5},{5,6},{6,7},{7,8},{8,9},{9,10},{10,1... | collective-permute-start | bytes 18440 | tf_op jit(solution)/shard_map/ppermute | solution.py:20
  75.2 4.4 collective-permute-start.3
  79.8 5.3 %collective-permute-start.4 = (f32[1,1,8,256]{3,2,1,0:T(8,128)S(1)}, f32[1,1,8,256]{3,2,1,0:T(8,128)S(1)}, u32[]{:S(2)}, u32[]{:S(2)}) collective-permute-start(f32[1,1,8,256]{3,2,1,0:T(8,128)S(1)} %get-tuple-element.118), channel_id=1, source_target_pairs={{0,12},{12,24},{24,36},{36,48},{48,60},{60,72},{72,84},{84,96},{96... | collective-permute-start | bytes 24584 | tf_op jit(solution)/shard_map/ppermute | solution.py:20
  83.2 5.0 %collective-permute-start.5 = (f32[1,1,8,256]{3,2,1,0:T(8,128)S(1)}, f32[1,1,8,256]{3,2,1,0:T(8,128)S(1)}, u32[]{:S(2)}, u32[]{:S(2)}) collective-permute-start(f32[1,1,8,256]{3,2,1,0:T(8,128)S(1)} %get-tuple-element.119), channel_id=1, source_target_pairs={{12,0},{24,12},{36,24},{48,36},{60,48},{72,60},{84,72},{96,84},{10... | collective-permute-start | bytes 24584 | tf_op jit(solution)/shard_map/ppermute | solution.py:22
  88.1 3.0 collective-permute-start.6
  89.8 4.4 collective-permute-start.7
  94.4 5.3 %collective-permute-start.8 = (f32[1,1,8,256]{3,2,1,0:T(8,128)S(1)}, f32[1,1,8,256]{3,2,1,0:T(8,128)S(1)}, u32[]{:S(2)}, u32[]{:S(2)}) collective-permute-start(f32[1,1,8,256]{3,2,1,0:T(8,128)S(1)} %get-tuple-element.114), channel_id=1, source_target_pairs={{0,12},{12,24},{24,36},{36,48},{48,60},{60,72},{72,84},{84,96},{96... | collective-permute-start | bytes 24584 | tf_op jit(solution)/shard_map/ppermute | solution.py:20
  97.7 5.0 %collective-permute-start.9 = (f32[1,1,8,256]{3,2,1,0:T(8,128)S(1)}, f32[1,1,8,256]{3,2,1,0:T(8,128)S(1)}, u32[]{:S(2)}, u32[]{:S(2)}) collective-permute-start(f32[1,1,8,256]{3,2,1,0:T(8,128)S(1)} %get-tuple-element.115), channel_id=1, source_target_pairs={{12,0},{24,12},{36,24},{48,36},{60,48},{72,60},{84,72},{96,84},{10... | collective-permute-start | bytes 24584 | tf_op jit(solution)/shard_map/ppermute | solution.py:22
  102.7 3.8 collective-permute-start.10
  105.2 4.4 collective-permute-start.11
  109.8 5.6 %collective-permute-start.12 = (f32[3,1,8,256]{3,2,1,0:T(8,128)S(1)}, f32[3,1,8,256]{3,2,1,0:T(8,128)S(1)}, u32[]{:S(2)}, u32[]{:S(2)}) collective-permute-start(f32[3,1,8,256]{3,2,1,0:T(8,128)S(1)} %get-tuple-element.73), channel_id=1, source_target_pairs={{12,0},{24,12},{36,24},{48,36},{60,48},{72,60},{84,72},{96,84},{10... | collective-permute-start | bytes 73736 | tf_op jit(solution)/shard_map/ppermute | solution.py:22
  111.8 4.6 collective-permute-start.13
  116.4 5.4 %collective-permute-start.14 = (f32[3,6,1,256]{3,2,1,0:T(1,128)S(1)}, f32[3,6,1,256]{3,2,1,0:T(1,128)S(1)}, u32[]{:S(2)}, u32[]{:S(2)}) collective-permute-start(f32[3,6,1,256]{3,2,1,0:T(1,128)S(1)} %get-tuple-element.56), channel_id=1, source_target_pairs={{1,0},{2,1},{3,2},{4,3},{5,4},{6,5},{7,6},{8,7},{9,8},{10,9},{11,1... | collective-permute-start | bytes 55304 | tf_op jit(solution)/shard_map/ppermute | solution.py:22
  117.7 4.9 %collective-permute-start.15 = (f32[3,6,1,256]{3,2,1,0:T(1,128)S(1)}, f32[3,6,1,256]{3,2,1,0:T(1,128)S(1)}, u32[]{:S(2)}, u32[]{:S(2)}) collective-permute-start(f32[3,6,1,256]{3,2,1,0:T(1,128)S(1)} %get-tuple-element.57), channel_id=1, source_target_pairs={{0,1},{1,2},{2,3},{3,4},{4,5},{5,6},{6,7},{7,8},{8,9},{9,10},{10,1... | collective-permute-start | bytes 55304 | tf_op jit(solution)/shard_map/ppermute | solution.py:20
  281.5 14.5 %collective-permute-start.16 = (f32[1,1,8,256]{3,2,1,0:T(8,128)S(1)}, f32[1,1,8,256]{3,2,1,0:T(8,128)S(1)}, u32[]{:S(2)}, u32[]{:S(2)}) collective-permute-start(f32[1,1,8,256]{3,2,1,0:T(8,128)S(1)} %get-tuple-element.104), channel_id=1, source_target_pairs={{0,12},{12,24},{24,36},{36,48},{48,60},{60,72},{72,84},{84,96},{96... | collective-permute-start | bytes 24584 | tf_op jit(solution)/shard_map/ppermute | solution.py:20
  292.9 5.0 %collective-permute-start.17 = (f32[1,1,8,256]{3,2,1,0:T(8,128)S(1)}, f32[1,1,8,256]{3,2,1,0:T(8,128)S(1)}, u32[]{:S(2)}, u32[]{:S(2)}) collective-permute-start(f32[1,1,8,256]{3,2,1,0:T(8,128)S(1)} %get-tuple-element.105), channel_id=1, source_target_pairs={{12,0},{24,12},{36,24},{48,36},{60,48},{72,60},{84,72},{96,84},{10... | collective-permute-start | bytes 24584 | tf_op jit(solution)/shard_map/ppermute | solution.py:22
  297.9 4.9 %collective-permute-start.18 = (f32[1,6,1,256]{3,2,1,0:T(1,128)S(1)}, f32[1,6,1,256]{3,2,1,0:T(1,128)S(1)}, u32[]{:S(2)}, u32[]{:S(2)}) collective-permute-start(f32[1,6,1,256]{3,2,1,0:T(1,128)S(1)} %get-tuple-element.92), channel_id=1, source_target_pairs={{0,1},{1,2},{2,3},{3,4},{4,5},{5,6},{6,7},{7,8},{8,9},{9,10},{10,1... | collective-permute-start | bytes 18440 | tf_op jit(solution)/shard_map/ppermute | solution.py:20
  301.5 4.7 collective-permute-start.19
  306.4 5.0 %collective-permute-start.20 = (f32[1,1,8,256]{3,2,1,0:T(8,128)S(1)}, f32[1,1,8,256]{3,2,1,0:T(8,128)S(1)}, u32[]{:S(2)}, u32[]{:S(2)}) collective-permute-start(f32[1,1,8,256]{3,2,1,0:T(8,128)S(1)} %get-tuple-element.102), channel_id=1, source_target_pairs={{0,12},{12,24},{24,36},{36,48},{48,60},{60,72},{72,84},{84,96},{96... | collective-permute-start | bytes 24584 | tf_op jit(solution)/shard_map/ppermute | solution.py:20
  309.5 5.0 %collective-permute-start.21 = (f32[1,1,8,256]{3,2,1,0:T(8,128)S(1)}, f32[1,1,8,256]{3,2,1,0:T(8,128)S(1)}, u32[]{:S(2)}, u32[]{:S(2)}) collective-permute-start(f32[1,1,8,256]{3,2,1,0:T(8,128)S(1)} %get-tuple-element.103), channel_id=1, source_target_pairs={{12,0},{24,12},{36,24},{48,36},{60,48},{72,60},{84,72},{96,84},{10... | collective-permute-start | bytes 24584 | tf_op jit(solution)/shard_map/ppermute | solution.py:22
  314.4 3.0 collective-permute-start.22
  316.1 4.4 collective-permute-start.23
  320.7 5.3 %collective-permute-start.24 = (f32[1,1,8,256]{3,2,1,0:T(8,128)S(1)}, f32[1,1,8,256]{3,2,1,0:T(8,128)S(1)}, u32[]{:S(2)}, u32[]{:S(2)}) collective-permute-start(f32[1,1,8,256]{3,2,1,0:T(8,128)S(1)} %get-tuple-element.100), channel_id=1, source_target_pairs={{0,12},{12,24},{24,36},{36,48},{48,60},{60,72},{72,84},{84,96},{96... | collective-permute-start | bytes 24584 | tf_op jit(solution)/shard_map/ppermute | solution.py:20
  324.1 5.0 %collective-permute-start.25 = (f32[1,1,8,256]{3,2,1,0:T(8,128)S(1)}, f32[1,1,8,256]{3,2,1,0:T(8,128)S(1)}, u32[]{:S(2)}, u32[]{:S(2)}) collective-permute-start(f32[1,1,8,256]{3,2,1,0:T(8,128)S(1)} %get-tuple-element.101), channel_id=1, source_target_pairs={{12,0},{24,12},{36,24},{48,36},{60,48},{72,60},{84,72},{96,84},{10... | collective-permute-start | bytes 24584 | tf_op jit(solution)/shard_map/ppermute | solution.py:22
  329.0 4.8 %collective-permute-start.26 = (f32[1,6,1,256]{3,2,1,0:T(1,128)S(1)}, f32[1,6,1,256]{3,2,1,0:T(1,128)S(1)}, u32[]{:S(2)}, u32[]{:S(2)}) collective-permute-start(f32[1,6,1,256]{3,2,1,0:T(1,128)S(1)} %get-tuple-element.88), channel_id=1, source_target_pairs={{0,1},{1,2},{2,3},{3,4},{4,5},{5,6},{6,7},{7,8},{8,9},{9,10},{10,1... | collective-permute-start | bytes 18440 | tf_op jit(solution)/shard_map/ppermute | solution.py:20
  332.6 4.7 collective-permute-start.27
  337.5 5.6 %collective-permute-start.28 = (f32[3,1,8,256]{3,2,1,0:T(8,128)S(1)}, f32[3,1,8,256]{3,2,1,0:T(8,128)S(1)}, u32[]{:S(2)}, u32[]{:S(2)}) collective-permute-start(f32[3,1,8,256]{3,2,1,0:T(8,128)S(1)} %get-tuple-element.61), channel_id=1, source_target_pairs={{12,0},{24,12},{36,24},{48,36},{60,48},{72,60},{84,72},{96,84},{10... | collective-permute-start | bytes 73736 | tf_op jit(solution)/shard_map/ppermute | solution.py:22
  339.4 4.6 collective-permute-start.29
  344.0 5.7 %collective-permute-start.30 = (f32[3,6,1,256]{3,2,1,0:T(1,128)S(1)}, f32[3,6,1,256]{3,2,1,0:T(1,128)S(1)}, u32[]{:S(2)}, u32[]{:S(2)}) collective-permute-start(f32[3,6,1,256]{3,2,1,0:T(1,128)S(1)} %get-tuple-element.54), channel_id=1, source_target_pairs={{1,0},{2,1},{3,2},{4,3},{5,4},{6,5},{7,6},{8,7},{9,8},{10,9},{11,1... | collective-permute-start | bytes 55304 | tf_op jit(solution)/shard_map/ppermute | solution.py:22
  345.3 5.1 %collective-permute-start.31 = (f32[3,6,1,256]{3,2,1,0:T(1,128)S(1)}, f32[3,6,1,256]{3,2,1,0:T(1,128)S(1)}, u32[]{:S(2)}, u32[]{:S(2)}) collective-permute-start(f32[3,6,1,256]{3,2,1,0:T(1,128)S(1)} %get-tuple-element.55), channel_id=1, source_target_pairs={{0,1},{1,2},{2,3},{3,4},{4,5},{5,6},{6,7},{7,8},{8,9},{9,10},{10,1... | collective-permute-start | bytes 55304 | tf_op jit(solution)/shard_map/ppermute | solution.py:20
  (6 other events, 65.5 us)
where the time goes:
time: 483 us; the launch traced here: 482 us
  blocking collectives  321 us (66%)
  starting transfers between devices  98.1 us (20%)
  waiting for transfers between devices  39.2 us (8%)
  between operations  10.3 us (2%)
    psum x1, blocking collectives, on_device(): lax.psum((jnp.sum(first_w * second_w), jnp.sum(second_w * second_w), jnp....  122 us
    psum x1, blocking collectives, on_device(): lax.psum((jnp.sum(first_w * first_w), jnp.sum(first_w * right_side)), ('g...  121 us
    unnamed x4, blocking collectives  77.8 us
    ppermute x16, starting transfers between devices, padded_2(): lax.ppermute(tail, axis, [(i, (i + 1) % count) for i in range(ends)])  71.2 us
    ppermute x16, waiting for transfers between devices, padded_2(): lax.ppermute(head, axis, [((i + 1) % count, i) for i in range(ends)])  35.8 us
    ppermute x16, starting transfers between devices, padded_2(): lax.ppermute(head, axis, [((i + 1) % count, i) for i in range(ends)])  26.9 us
  transfers between devices with their start and end apart: 32, of which 16 were waited for; matrix products, arithmetic and copies ran while one was open for 0% of the time, Pallas kernels for 0%

commit v1 on v0

--- a/solution.py
+++ b/solution.py
@@ -7,23 +7,6 @@
 
 
 damping = 0.8
-
-
-def padded_2(cells, sides, width):
-    for axis, dim in sides:
-        count = lax.axis_size(axis)
-        ends = count - 1
-        head = lax.slice_in_dim(cells, 0, width, axis=dim)
-        tail = lax.slice_in_dim(cells, cells.shape[dim] - width, cells.shape[dim], axis=dim)
-        cells = jnp.concatenate(
-            [
-                lax.ppermute(tail, axis, [(i, (i + 1) % count) for i in range(ends)]),
-                cells,
-                lax.ppermute(head, axis, [((i + 1) % count, i) for i in range(ends)]),
-            ],
-            axis=dim,
-        )
-    return cells
 
 
 def face_values(padded):
@@ -48,7 +31,24 @@
 
 
 def faces(field_in):
-    return padded_2(field_in, (("gx", 1), ("gy", 2)), 1)
+    received = []
+    for axis, dim in (("gx", 1), ("gy", 2)):
+        count = lax.axis_size(axis)
+        ends = count - 1
+        head = lax.slice_in_dim(field_in, 0, 1, axis=dim)
+        tail = lax.slice_in_dim(field_in, field_in.shape[dim] - 1, field_in.shape[dim], axis=dim)
+        received.append(lax.ppermute(tail, axis, [(i, i + 1) for i in range(ends)]))
+        received.append(lax.ppermute(head, axis, [(i + 1, i) for i in range(ends)]))
+    low_x, high_x, low_y, high_y = received
+    pad = [(0, 0), (1, 1), (0, 0), (0, 0)]
+    middle = jnp.concatenate([low_x, field_in, high_x], 1)
+    return jnp.concatenate([jnp.pad(low_y, pad), middle, jnp.pad(high_y, pad)], 2)
+
+
+def everyone(values, axis):
+    count = lax.axis_size(axis)
+    spread = jnp.broadcast_to(values[None, None], (count, 1) + values.shape)
+    return lax.all_to_all(spread, axis, 0, 0)[:, 0]
 
 
 def block_inverse(matrix, mask_float):
@@ -118,9 +118,9 @@
     def precondition(residual_in):
         pressure_rhs = residual_in[0] + residual_in[1] + residual_in[2]
         coarse_local = jnp.dot(onehot, pressure_rhs.reshape(-1), precision=highest)
-        coarse_all = lax.all_gather(coarse_local, "gy", axis=0, tiled=True)
+        coarse_all = everyone(coarse_local, "gy").reshape(-1)
         owned = jnp.dot(coarse_rows, coarse_all, precision=highest)
-        returned = lax.all_gather(owned, "gy", axis=0, tiled=True).reshape(group_size, aggregates)
+        returned = everyone(owned, "gy")
         own_values = jnp.dot(owner_pick, returned, precision=highest)
         pressure = jnp.dot(own_values, onehot, precision=highest).reshape(pressure_rhs.shape)
         for sweep_index in range(SMOOTH):
@@ -149,16 +149,20 @@
 
     first_z = precondition(right_side)
     first_w = operate(first_z)
-    gram_one, proj_one = lax.psum(
-        (jnp.sum(first_w * first_w), jnp.sum(first_w * right_side)), ("gx", "gy")
+    second_z = precondition(first_w)
+    second_w = operate(second_z)
+    sums = jnp.stack(
+        [
+            jnp.sum(first_w * first_w),
+            jnp.sum(first_w * second_w),
+            jnp.sum(second_w * second_w),
+            jnp.sum(first_w * right_side),
+            jnp.sum(second_w * right_side),
+        ]
     )
-    scaled = first_w * (1.0 / jnp.sqrt(gram_one + 1e-06))
-    second_z = precondition(scaled)
-    second_w = operate(second_z)
-    gram_cross, gram_two, proj_two = lax.psum(
-        (jnp.sum(first_w * second_w), jnp.sum(second_w * second_w), jnp.sum(second_w * right_side)),
-        ("gx", "gy"),
-    )
+    sums = jnp.sum(everyone(sums, "gx"), 0)
+    sums = jnp.sum(everyone(sums, "gy"), 0)
+    gram_one, gram_cross, gram_two, proj_one, proj_two = [sums[i] for i in range(5)]
     determinant = gram_one * gram_two - gram_cross * gram_cross
     coeff_one = (gram_two * proj_one - gram_cross * proj_two) / determinant
     coeff_two = (gram_one * proj_two - gram_cross * proj_one) / determinant

time: 483 us -> 248 us (0.51)
  blocking collectives: 321 us -> 75.7 us
  starting transfers between devices: 98.1 us -> 105 us
    psum x2 -> x0, blocking collectives: 243 us -> none  [the longest x1 122 us: on_device(): lax.psum((jnp.sum(first_w * second_w), jnp.sum(second_w * second_w), jnp....]
    unnamed x4 -> x0, blocking collectives: 77.8 us -> none
    all_to_all x0 -> x4, blocking collectives: none -> 75.7 us  [everyone(): return lax.all_to_all(spread, axis, 0, 0)[:, 0]]
    all_to_all x0 -> x2, starting transfers between devices: none -> 19.2 us  [everyone(): return lax.all_to_all(spread, axis, 0, 0)[:, 0]]
    all_to_all x0 -> x2, waiting for transfers between devices: none -> 16.8 us  [everyone(): return lax.all_to_all(spread, axis, 0, 0)[:, 0]]
    ppermute x32, waiting for transfers between devices: 39.2 us -> 24.8 us  [the longest x16 24.8 us: faces(): received.append(lax.ppermute(head, axis, [(i + 1, i) for i in range(ends)]))]
    ppermute x32, starting transfers between devices: 98.1 us -> 86.1 us  [the longest x16 59.9 us: faces(): received.append(lax.ppermute(tail, axis, [(i, i + 1) for i in range(ends)]))]
  transfers between devices with their start and end apart: 32 -> 34, of which waited for: 16 -> 10; matrix products, arithmetic and copies ran while one was open for 0% -> 0% of each run, Pallas kernels for 0% -> 0%
where the time goes in v1:
time: 248 us; the launch traced here: 247 us
  starting transfers between devices  105 us (42%)
  blocking collectives  75.7 us (31%)
  waiting for transfers between devices  41.6 us (17%)
  between operations  9.37 us (4%)
  local copies, waits for them, and re-layouts  7.19 us (3%)
  matrix products  4.24 us (2%)
  other arithmetic  3.57 us (1%)
    all_to_all x4, blocking collectives, everyone(): return lax.all_to_all(spread, axis, 0, 0)[:, 0]  75.7 us
    ppermute x16, starting transfers between devices, faces(): received.append(lax.ppermute(tail, axis, [(i, i + 1) for i in range(ends)]))  59.9 us
    ppermute x16, starting transfers between devices, faces(): received.append(lax.ppermute(head, axis, [(i + 1, i) for i in range(ends)]))  26.2 us
    ppermute x16, waiting for transfers between devices, faces(): received.append(lax.ppermute(head, axis, [(i + 1, i) for i in range(ends)]))  24.8 us
    all_to_all x2, starting transfers between devices, everyone(): return lax.all_to_all(spread, axis, 0, 0)[:, 0]  19.2 us
    all_to_all x2, waiting for transfers between devices, everyone(): return lax.all_to_all(spread, axis, 0, 0)[:, 0]  16.8 us
  transfers between devices with their start and end apart: 34, of which 10 were waited for; matrix products, arithmetic and copies ran while one was open for 0% of the time, Pallas kernels for 0%

profile of v1, /device:TPU:1, one launch (start us, length us, event | category | flops | bytes accessed | tf_op | source)
XLA Modules:
  0.0 247.0 jit_solution(234397567216175947)
XLA Ops:
  3.3 15.7 %all-to-all-start = ((f32[12,1,64]{2,1,0:T(1,128)}), f32[12,1,64]{2,1,0:T(1,128)S(1)}, u32[]{:S(2)}, u32[]{:S(2)}) async-start(f32[12,1,64]{2,1,0:T(1,128)} %broadcast_in_dim.24), calls=%async_computation | async-start | bytes 12288 | tf_op jit(solution)/shard_map/all_to_all | solution.py:51
  19.1 8.8 %all-to-all-done = f32[12,1,64]{2,1,0:T(1,128)S(1)} async-done(((f32[12,1,64]{2,1,0:T(1,128)}), f32[12,1,64]{2,1,0:T(1,128)S(1)}, u32[]{:S(2)}, u32[]{:S(2)}) %all-to-all-start) | async-done | bytes 3104 | tf_op jit(solution)/shard_map/all_to_all | solution.py:51
  28.9 3.5 %all-to-all-start.1 = ((f32[12,1,64]{2,1,0:T(1,128)}), f32[12,1,64]{2,1,0:T(1,128)S(1)}, u32[]{:S(2)}, u32[]{:S(2)}) async-start(f32[12,1,64]{2,1,0:T(1,128)} %broadcast_in_dim.25), calls=%async_computation.1 | async-start | bytes 12288 | tf_op jit(solution)/shard_map/all_to_all | solution.py:51
  33.1 8.0 %all-to-all-done.1 = f32[12,1,64]{2,1,0:T(1,128)S(1)} async-done(((f32[12,1,64]{2,1,0:T(1,128)}), f32[12,1,64]{2,1,0:T(1,128)S(1)}, u32[]{:S(2)}, u32[]{:S(2)}) %all-to-all-start.1) | async-done | bytes 3104 | tf_op jit(solution)/shard_map/all_to_all | solution.py:51
  42.1 2.2 collective-permute-start
  45.6 6.6 %collective-permute-start.1 = (f32[1,1,8,256]{3,2,1,0:T(8,128)S(1)}, f32[1,1,8,256]{3,2,1,0:T(8,128)S(1)}, u32[]{:S(2)}, u32[]{:S(2)}) collective-permute-start(f32[1,1,8,256]{3,2,1,0:T(8,128)S(1)} %get-tuple-element.111), channel_id=1, source_target_pairs={{0,12},{12,24},{24,36},{36,48},{48,60},{60,72},{72,84},{84,96},{96... | collective-permute-start | bytes 24584 | tf_op jit(solution)/shard_map/ppermute | solution.py:40
  54.3 2.9 %collective-permute-done.2 = f32[1,1,8,256]{3,2,1,0:T(8,128)S(1)} collective-permute-done((f32[1,1,8,256]{3,2,1,0:T(8,128)S(1)}, f32[1,1,8,256]{3,2,1,0:T(8,128)S(1)}, u32[]{:S(2)}, u32[]{:S(2)}) %collective-permute-start.2) | collective-permute-done | bytes 8224 | tf_op jit(solution)/shard_map/ppermute | solution.py:41
  57.4 4.3 %collective-permute-start.4 = (f32[1,4,1,256]{3,2,1,0:T(1,128)S(1)}, f32[1,4,1,256]{3,2,1,0:T(1,128)S(1)}, u32[]{:S(2)}, u32[]{:S(2)}) collective-permute-start(f32[1,4,1,256]{3,2,1,0:T(1,128)S(1)} %get-tuple-element.109), channel_id=1, source_target_pairs={{0,1},{1,2},{2,3},{3,4},{4,5},{5,6},{6,7},{7,8},{8,9},{9,10},{10,1... | collective-permute-start | bytes 12296 | tf_op jit(solution)/shard_map/ppermute | solution.py:40
  63.0 2.2 collective-permute-start.5
  67.4 2.8 %collective-permute-done.6 = f32[1,1,8,256]{3,2,1,0:T(8,128)S(1)} collective-permute-done((f32[1,1,8,256]{3,2,1,0:T(8,128)S(1)}, f32[1,1,8,256]{3,2,1,0:T(8,128)S(1)}, u32[]{:S(2)}, u32[]{:S(2)}) %collective-permute-start.6) | collective-permute-done | bytes 8224 | tf_op jit(solution)/shard_map/ppermute | solution.py:41
  70.4 4.3 %collective-permute-start.8 = (f32[1,4,1,256]{3,2,1,0:T(1,128)S(1)}, f32[1,4,1,256]{3,2,1,0:T(1,128)S(1)}, u32[]{:S(2)}, u32[]{:S(2)}) collective-permute-start(f32[1,4,1,256]{3,2,1,0:T(1,128)S(1)} %get-tuple-element.103), channel_id=1, source_target_pairs={{0,1},{1,2},{2,3},{3,4},{4,5},{5,6},{6,7},{7,8},{8,9},{9,10},{10,1... | collective-permute-start | bytes 12296 | tf_op jit(solution)/shard_map/ppermute | solution.py:40
  76.0 2.2 collective-permute-start.9
  80.4 2.8 %collective-permute-done.10 = f32[1,1,8,256]{3,2,1,0:T(8,128)S(1)} collective-permute-done((f32[1,1,8,256]{3,2,1,0:T(8,128)S(1)}, f32[1,1,8,256]{3,2,1,0:T(8,128)S(1)}, u32[]{:S(2)}, u32[]{:S(2)}) %collective-permute-start.10) | collective-permute-done | bytes 8224 | tf_op jit(solution)/shard_map/ppermute | solution.py:41
  84.8 4.9 %collective-permute-start.15 = (f32[3,4,1,256]{3,2,1,0:T(1,128)S(1)}, f32[3,4,1,256]{3,2,1,0:T(1,128)S(1)}, u32[]{:S(2)}, u32[]{:S(2)}) collective-permute-start(f32[3,4,1,256]{3,2,1,0:T(1,128)S(1)} %get-tuple-element.70), channel_id=1, source_target_pairs={{0,1},{1,2},{2,3},{3,4},{4,5},{5,6},{6,7},{7,8},{8,9},{9,10},{10,1... | collective-permute-start | bytes 36872 | tf_op jit(solution)/shard_map/ppermute | solution.py:40
  89.7 2.2 collective-permute-start.13
  94.1 3.7 %collective-permute-done.12 = f32[3,1,8,256]{3,2,1,0:T(8,128)S(1)} collective-permute-done((f32[3,1,8,256]{3,2,1,0:T(8,128)S(1)}, f32[3,1,8,256]{3,2,1,0:T(8,128)S(1)}, u32[]{:S(2)}, u32[]{:S(2)}) %collective-permute-start.12) | collective-permute-done | bytes 24608 | tf_op jit(solution)/shard_map/ppermute | solution.py:41
  99.1 16.1 %all_to_all.30 = f32[12,1,64]{2,1,0:T(1,128)S(1)} all-to-all(f32[12,1,64]{2,1,0:T(1,128)S(1)} %broadcast_in_dim.29), channel_id=1, replica_groups=mesh['gx'=64,'gy'=12] {'gy'}, dimensions={0} | all-to-all | bytes 6144 | tf_op jit(solution)/shard_map/all_to_all | solution.py:51
  115.6 11.4 %all_to_all.31 = f32[12,1,64]{2,1,0:T(1,128)S(1)} all-to-all(f32[12,1,64]{2,1,0:T(1,128)S(1)} %broadcast_in_dim.30), channel_id=1, replica_groups=mesh['gx'=64,'gy'=12] {'gy'}, dimensions={0} | all-to-all | bytes 6144 | tf_op jit(solution)/shard_map/all_to_all | solution.py:51
  127.9 4.5 %collective-permute-start.17 = (f32[1,1,8,256]{3,2,1,0:T(8,128)S(1)}, f32[1,1,8,256]{3,2,1,0:T(8,128)S(1)}, u32[]{:S(2)}, u32[]{:S(2)}) collective-permute-start(f32[1,1,8,256]{3,2,1,0:T(8,128)S(1)} %get-tuple-element.95), channel_id=1, source_target_pairs={{0,12},{12,24},{24,36},{36,48},{48,60},{60,72},{72,84},{84,96},{96... | collective-permute-start | bytes 24584 | tf_op jit(solution)/shard_map/ppermute | solution.py:40
  134.4 2.2 collective-permute-start.16
  137.9 3.0 %collective-permute-done.19 = f32[1,4,1,256]{3,2,1,0:T(1,128)S(1)} collective-permute-done((f32[1,4,1,256]{3,2,1,0:T(1,128)S(1)}, f32[1,4,1,256]{3,2,1,0:T(1,128)S(1)}, u32[]{:S(2)}, u32[]{:S(2)}) %collective-permute-start.19) | collective-permute-done | bytes 4128 | tf_op jit(solution)/shard_map/ppermute | solution.py:41
  141.1 5.1 %collective-permute-start.21 = (f32[1,1,8,256]{3,2,1,0:T(8,128)S(1)}, f32[1,1,8,256]{3,2,1,0:T(8,128)S(1)}, u32[]{:S(2)}, u32[]{:S(2)}) collective-permute-start(f32[1,1,8,256]{3,2,1,0:T(8,128)S(1)} %get-tuple-element.91), channel_id=1, source_target_pairs={{0,12},{12,24},{24,36},{36,48},{48,60},{60,72},{72,84},{84,96},{96... | collective-permute-start | bytes 24584 | tf_op jit(solution)/shard_map/ppermute | solution.py:40
  151.6 3.0 %collective-permute-done.23 = f32[1,4,1,256]{3,2,1,0:T(1,128)S(1)} collective-permute-done((f32[1,4,1,256]{3,2,1,0:T(1,128)S(1)}, f32[1,4,1,256]{3,2,1,0:T(1,128)S(1)}, u32[]{:S(2)}, u32[]{:S(2)}) %collective-permute-start.23) | collective-permute-done | bytes 4128 | tf_op jit(solution)/shard_map/ppermute | solution.py:41
  154.9 5.1 %collective-permute-start.25 = (f32[1,1,8,256]{3,2,1,0:T(8,128)S(1)}, f32[1,1,8,256]{3,2,1,0:T(8,128)S(1)}, u32[]{:S(2)}, u32[]{:S(2)}) collective-permute-start(f32[1,1,8,256]{3,2,1,0:T(8,128)S(1)} %get-tuple-element.87), channel_id=1, source_target_pairs={{0,12},{12,24},{24,36},{36,48},{48,60},{60,72},{72,84},{84,96},{96... | collective-permute-start | bytes 24584 | tf_op jit(solution)/shard_map/ppermute | solution.py:40
  161.9 2.6 %collective-permute-start.24 = (f32[1,4,1,256]{3,2,1,0:T(1,128)S(1)}, f32[1,4,1,256]{3,2,1,0:T(1,128)S(1)}, u32[]{:S(2)}, u32[]{:S(2)}) collective-permute-start(f32[1,4,1,256]{3,2,1,0:T(1,128)S(1)} %get-tuple-element.89), channel_id=1, source_target_pairs={{0,1},{1,2},{2,3},{3,4},{4,5},{5,6},{6,7},{7,8},{8,9},{9,10},{10,1... | collective-permute-start | bytes 12296 | tf_op jit(solution)/shard_map/ppermute | solution.py:40
  165.8 3.3 %collective-permute-done.27 = f32[1,4,1,256]{3,2,1,0:T(1,128)S(1)} collective-permute-done((f32[1,4,1,256]{3,2,1,0:T(1,128)S(1)}, f32[1,4,1,256]{3,2,1,0:T(1,128)S(1)}, u32[]{:S(2)}, u32[]{:S(2)}) %collective-permute-start.27) | collective-permute-done | bytes 4128 | tf_op jit(solution)/shard_map/ppermute | solution.py:41
  170.8 4.0 %collective-permute-start.31 = (f32[3,4,1,256]{3,2,1,0:T(1,128)S(1)}, f32[3,4,1,256]{3,2,1,0:T(1,128)S(1)}, u32[]{:S(2)}, u32[]{:S(2)}) collective-permute-start(f32[3,4,1,256]{3,2,1,0:T(1,128)S(1)} %get-tuple-element.56), channel_id=1, source_target_pairs={{0,1},{1,2},{2,3},{3,4},{4,5},{5,6},{6,7},{7,8},{8,9},{9,10},{10,1... | collective-permute-start | bytes 36872 | tf_op jit(solution)/shard_map/ppermute | solution.py:40
  174.8 5.4 %collective-permute-start.29 = (f32[3,1,8,256]{3,2,1,0:T(8,128)S(1)}, f32[3,1,8,256]{3,2,1,0:T(8,128)S(1)}, u32[]{:S(2)}, u32[]{:S(2)}) collective-permute-start(f32[3,1,8,256]{3,2,1,0:T(8,128)S(1)} %get-tuple-element.57), channel_id=1, source_target_pairs={{0,12},{12,24},{24,36},{36,48},{48,60},{60,72},{72,84},{84,96},{96... | collective-permute-start | bytes 73736 | tf_op jit(solution)/shard_map/ppermute | solution.py:40
  182.2 3.1 %collective-permute-done.28 = f32[3,1,8,256]{3,2,1,0:T(8,128)S(1)} collective-permute-done((f32[3,1,8,256]{3,2,1,0:T(8,128)S(1)}, f32[3,1,8,256]{3,2,1,0:T(8,128)S(1)}, u32[]{:S(2)}, u32[]{:S(2)}) %collective-permute-start.28) | collective-permute-done | bytes 24608 | tf_op jit(solution)/shard_map/ppermute | solution.py:41
  186.2 3.3 %stack.147 = f32[5]{0:T(128)S(1)} concatenate(f32[1]{0:T(128)} %bitcast.70, f32[1]{0:T(128)} %bitcast.92, f32[1]{0:T(128)} %bitcast.93, f32[1]{0:T(128)} %bitcast.94, f32[1]{0:T(128)} %bitcast.95), dimensions={0} | concatenate | bytes 40 | tf_op jit(solution)/shard_map/stack | solution.py:154
  189.5 31.9 %all_to_all.32 = f32[64,1,5]{2,1,0:T(1,128)S(1)} all-to-all(f32[64,1,5]{2,1,0:T(1,128)S(1)} %broadcast_in_dim.68), channel_id=1, replica_groups=mesh['gx'=64,'gy'=12] {'gx'}, dimensions={0} | all-to-all | bytes 2560 | tf_op jit(solution)/shard_map/all_to_all | solution.py:51
  221.5 16.3 %all_to_all.33 = f32[12,1,5]{2,1,0:T(1,128)S(1)} all-to-all(f32[12,1,5]{2,1,0:T(1,128)S(1)} %broadcast_in_dim.69), channel_id=1, replica_groups=mesh['gx'=64,'gy'=12] {'gy'}, dimensions={0} | all-to-all | bytes 480 | tf_op jit(solution)/shard_map/all_to_all | solution.py:51
  (136 shorter events, 40.1 us)
Async XLA Ops:
  3.3 24.6 %all-to-all-start = ((f32[12,1,64]{2,1,0:T(1,128)}), f32[12,1,64]{2,1,0:T(1,128)S(1)}, u32[]{:S(2)}, u32[]{:S(2)}) async-start(f32[12,1,64]{2,1,0:T(1,128)} %broadcast_in_dim.24), calls=%async_computation | async-start | bytes 12288 | tf_op jit(solution)/shard_map/all_to_all | solution.py:51
  28.9 12.2 %all-to-all-start.1 = ((f32[12,1,64]{2,1,0:T(1,128)}), f32[12,1,64]{2,1,0:T(1,128)S(1)}, u32[]{:S(2)}, u32[]{:S(2)}) async-start(f32[12,1,64]{2,1,0:T(1,128)} %broadcast_in_dim.25), calls=%async_computation.1 | async-start | bytes 12288 | tf_op jit(solution)/shard_map/all_to_all | solution.py:51
  42.1 12.1 %collective-permute-start = (f32[1,4,1,256]{3,2,1,0:T(1,128)S(1)}, f32[1,4,1,256]{3,2,1,0:T(1,128)S(1)}, u32[]{:S(2)}, u32[]{:S(2)}) collective-permute-start(f32[1,4,1,256]{3,2,1,0:T(1,128)S(1)} %get-tuple-element.113), channel_id=1, source_target_pairs={{0,1},{1,2},{2,3},{3,4},{4,5},{5,6},{6,7},{7,8},{8,9},{9,10},{10,1... | collective-permute-start | bytes 12296 | tf_op jit(solution)/shard_map/ppermute | solution.py:40
  44.3 10.0 %collective-permute-start.3 = (f32[1,4,1,256]{3,2,1,0:T(1,128)S(1)}, f32[1,4,1,256]{3,2,1,0:T(1,128)S(1)}, u32[]{:S(2)}, u32[]{:S(2)}) collective-permute-start(f32[1,4,1,256]{3,2,1,0:T(1,128)S(1)} %get-tuple-element.114), channel_id=1, source_target_pairs={{1,0},{2,1},{3,2},{4,3},{5,4},{6,5},{7,6},{8,7},{9,8},{10,9},{11,1... | collective-permute-start | bytes 12296 | tf_op jit(solution)/shard_map/ppermute | solution.py:41
  45.6 8.7 %collective-permute-start.1 = (f32[1,1,8,256]{3,2,1,0:T(8,128)S(1)}, f32[1,1,8,256]{3,2,1,0:T(8,128)S(1)}, u32[]{:S(2)}, u32[]{:S(2)}) collective-permute-start(f32[1,1,8,256]{3,2,1,0:T(8,128)S(1)} %get-tuple-element.111), channel_id=1, source_target_pairs={{0,12},{12,24},{24,36},{36,48},{48,60},{60,72},{72,84},{84,96},{96... | collective-permute-start | bytes 24584 | tf_op jit(solution)/shard_map/ppermute | solution.py:40
  52.2 5.0 %collective-permute-start.2 = (f32[1,1,8,256]{3,2,1,0:T(8,128)S(1)}, f32[1,1,8,256]{3,2,1,0:T(8,128)S(1)}, u32[]{:S(2)}, u32[]{:S(2)}) collective-permute-start(f32[1,1,8,256]{3,2,1,0:T(8,128)S(1)} %get-tuple-element.112), channel_id=1, source_target_pairs={{12,0},{24,12},{36,24},{48,36},{60,48},{72,60},{84,72},{96,84},{10... | collective-permute-start | bytes 24584 | tf_op jit(solution)/shard_map/ppermute | solution.py:41
  57.4 9.9 %collective-permute-start.4 = (f32[1,4,1,256]{3,2,1,0:T(1,128)S(1)}, f32[1,4,1,256]{3,2,1,0:T(1,128)S(1)}, u32[]{:S(2)}, u32[]{:S(2)}) collective-permute-start(f32[1,4,1,256]{3,2,1,0:T(1,128)S(1)} %get-tuple-element.109), channel_id=1, source_target_pairs={{0,1},{1,2},{2,3},{3,4},{4,5},{5,6},{6,7},{7,8},{8,9},{9,10},{10,1... | collective-permute-start | bytes 12296 | tf_op jit(solution)/shard_map/ppermute | solution.py:40
  61.7 5.7 %collective-permute-start.7 = (f32[1,4,1,256]{3,2,1,0:T(1,128)S(1)}, f32[1,4,1,256]{3,2,1,0:T(1,128)S(1)}, u32[]{:S(2)}, u32[]{:S(2)}) collective-permute-start(f32[1,4,1,256]{3,2,1,0:T(1,128)S(1)} %get-tuple-element.110), channel_id=1, source_target_pairs={{1,0},{2,1},{3,2},{4,3},{5,4},{6,5},{7,6},{8,7},{9,8},{10,9},{11,1... | collective-permute-start | bytes 12296 | tf_op jit(solution)/shard_map/ppermute | solution.py:41
  63.0 4.4 %collective-permute-start.5 = (f32[1,1,8,256]{3,2,1,0:T(8,128)S(1)}, f32[1,1,8,256]{3,2,1,0:T(8,128)S(1)}, u32[]{:S(2)}, u32[]{:S(2)}) collective-permute-start(f32[1,1,8,256]{3,2,1,0:T(8,128)S(1)} %get-tuple-element.107), channel_id=1, source_target_pairs={{0,12},{12,24},{24,36},{36,48},{48,60},{60,72},{72,84},{84,96},{96... | collective-permute-start | bytes 24584 | tf_op jit(solution)/shard_map/ppermute | solution.py:40
  65.2 5.0 %collective-permute-start.6 = (f32[1,1,8,256]{3,2,1,0:T(8,128)S(1)}, f32[1,1,8,256]{3,2,1,0:T(8,128)S(1)}, u32[]{:S(2)}, u32[]{:S(2)}) collective-permute-start(f32[1,1,8,256]{3,2,1,0:T(8,128)S(1)} %get-tuple-element.108), channel_id=1, source_target_pairs={{12,0},{24,12},{36,24},{48,36},{60,48},{72,60},{84,72},{96,84},{10... | collective-permute-start | bytes 24584 | tf_op jit(solution)/shard_map/ppermute | solution.py:41
  70.4 9.9 %collective-permute-start.8 = (f32[1,4,1,256]{3,2,1,0:T(1,128)S(1)}, f32[1,4,1,256]{3,2,1,0:T(1,128)S(1)}, u32[]{:S(2)}, u32[]{:S(2)}) collective-permute-start(f32[1,4,1,256]{3,2,1,0:T(1,128)S(1)} %get-tuple-element.103), channel_id=1, source_target_pairs={{0,1},{1,2},{2,3},{3,4},{4,5},{5,6},{6,7},{7,8},{8,9},{9,10},{10,1... | collective-permute-start | bytes 12296 | tf_op jit(solution)/shard_map/ppermute | solution.py:40
  74.7 5.7 %collective-permute-start.11 = (f32[1,4,1,256]{3,2,1,0:T(1,128)S(1)}, f32[1,4,1,256]{3,2,1,0:T(1,128)S(1)}, u32[]{:S(2)}, u32[]{:S(2)}) collective-permute-start(f32[1,4,1,256]{3,2,1,0:T(1,128)S(1)} %get-tuple-element.104), channel_id=1, source_target_pairs={{1,0},{2,1},{3,2},{4,3},{5,4},{6,5},{7,6},{8,7},{9,8},{10,9},{11,1... | collective-permute-start | bytes 12296 | tf_op jit(solution)/shard_map/ppermute | solution.py:41
  76.0 4.4 %collective-permute-start.9 = (f32[1,1,8,256]{3,2,1,0:T(8,128)S(1)}, f32[1,1,8,256]{3,2,1,0:T(8,128)S(1)}, u32[]{:S(2)}, u32[]{:S(2)}) collective-permute-start(f32[1,1,8,256]{3,2,1,0:T(8,128)S(1)} %get-tuple-element.101), channel_id=1, source_target_pairs={{0,12},{12,24},{24,36},{36,48},{48,60},{60,72},{72,84},{84,96},{96... | collective-permute-start | bytes 24584 | tf_op jit(solution)/shard_map/ppermute | solution.py:40
  78.2 5.0 %collective-permute-start.10 = (f32[1,1,8,256]{3,2,1,0:T(8,128)S(1)}, f32[1,1,8,256]{3,2,1,0:T(8,128)S(1)}, u32[]{:S(2)}, u32[]{:S(2)}) collective-permute-start(f32[1,1,8,256]{3,2,1,0:T(8,128)S(1)} %get-tuple-element.102), channel_id=1, source_target_pairs={{12,0},{24,12},{36,24},{48,36},{60,48},{72,60},{84,72},{96,84},{10... | collective-permute-start | bytes 24584 | tf_op jit(solution)/shard_map/ppermute | solution.py:41
  83.5 10.6 %collective-permute-start.14 = (f32[3,4,1,256]{3,2,1,0:T(1,128)S(1)}, f32[3,4,1,256]{3,2,1,0:T(1,128)S(1)}, u32[]{:S(2)}, u32[]{:S(2)}) collective-permute-start(f32[3,4,1,256]{3,2,1,0:T(1,128)S(1)} %get-tuple-element.69), channel_id=1, source_target_pairs={{1,0},{2,1},{3,2},{4,3},{5,4},{6,5},{7,6},{8,7},{9,8},{10,9},{11,1... | collective-permute-start | bytes 36872 | tf_op jit(solution)/shard_map/ppermute | solution.py:41
  84.8 9.3 %collective-permute-start.15 = (f32[3,4,1,256]{3,2,1,0:T(1,128)S(1)}, f32[3,4,1,256]{3,2,1,0:T(1,128)S(1)}, u32[]{:S(2)}, u32[]{:S(2)}) collective-permute-start(f32[3,4,1,256]{3,2,1,0:T(1,128)S(1)} %get-tuple-element.70), channel_id=1, source_target_pairs={{0,1},{1,2},{2,3},{3,4},{4,5},{5,6},{6,7},{7,8},{8,9},{9,10},{10,1... | collective-permute-start | bytes 36872 | tf_op jit(solution)/shard_map/ppermute | solution.py:40
  89.7 4.5 %collective-permute-start.13 = (f32[3,1,8,256]{3,2,1,0:T(8,128)S(1)}, f32[3,1,8,256]{3,2,1,0:T(8,128)S(1)}, u32[]{:S(2)}, u32[]{:S(2)}) collective-permute-start(f32[3,1,8,256]{3,2,1,0:T(8,128)S(1)} %get-tuple-element.71), channel_id=1, source_target_pairs={{0,12},{12,24},{24,36},{36,48},{48,60},{60,72},{72,84},{84,96},{96... | collective-permute-start | bytes 73736 | tf_op jit(solution)/shard_map/ppermute | solution.py:40
  91.9 5.9 %collective-permute-start.12 = (f32[3,1,8,256]{3,2,1,0:T(8,128)S(1)}, f32[3,1,8,256]{3,2,1,0:T(8,128)S(1)}, u32[]{:S(2)}, u32[]{:S(2)}) collective-permute-start(f32[3,1,8,256]{3,2,1,0:T(8,128)S(1)} %get-tuple-element.72), channel_id=1, source_target_pairs={{12,0},{24,12},{36,24},{48,36},{60,48},{72,60},{84,72},{96,84},{10... | collective-permute-start | bytes 73736 | tf_op jit(solution)/shard_map/ppermute | solution.py:41
  127.9 13.0 %collective-permute-start.17 = (f32[1,1,8,256]{3,2,1,0:T(8,128)S(1)}, f32[1,1,8,256]{3,2,1,0:T(8,128)S(1)}, u32[]{:S(2)}, u32[]{:S(2)}) collective-permute-start(f32[1,1,8,256]{3,2,1,0:T(8,128)S(1)} %get-tuple-element.95), channel_id=1, source_target_pairs={{0,12},{12,24},{24,36},{36,48},{48,60},{60,72},{72,84},{84,96},{96... | collective-permute-start | bytes 24584 | tf_op jit(solution)/shard_map/ppermute | solution.py:40
  132.4 8.5 %collective-permute-start.18 = (f32[1,1,8,256]{3,2,1,0:T(8,128)S(1)}, f32[1,1,8,256]{3,2,1,0:T(8,128)S(1)}, u32[]{:S(2)}, u32[]{:S(2)}) collective-permute-start(f32[1,1,8,256]{3,2,1,0:T(8,128)S(1)} %get-tuple-element.96), channel_id=1, source_target_pairs={{12,0},{24,12},{36,24},{48,36},{60,48},{72,60},{84,72},{96,84},{10... | collective-permute-start | bytes 24584 | tf_op jit(solution)/shard_map/ppermute | solution.py:41
  136.6 4.4 %collective-permute-start.19 = (f32[1,4,1,256]{3,2,1,0:T(1,128)S(1)}, f32[1,4,1,256]{3,2,1,0:T(1,128)S(1)}, u32[]{:S(2)}, u32[]{:S(2)}) collective-permute-start(f32[1,4,1,256]{3,2,1,0:T(1,128)S(1)} %get-tuple-element.98), channel_id=1, source_target_pairs={{1,0},{2,1},{3,2},{4,3},{5,4},{6,5},{7,6},{8,7},{9,8},{10,9},{11,1... | collective-permute-start | bytes 12296 | tf_op jit(solution)/shard_map/ppermute | solution.py:41
  141.1 13.5 %collective-permute-start.21 = (f32[1,1,8,256]{3,2,1,0:T(8,128)S(1)}, f32[1,1,8,256]{3,2,1,0:T(8,128)S(1)}, u32[]{:S(2)}, u32[]{:S(2)}) collective-permute-start(f32[1,1,8,256]{3,2,1,0:T(8,128)S(1)} %get-tuple-element.91), channel_id=1, source_target_pairs={{0,12},{12,24},{24,36},{36,48},{48,60},{60,72},{72,84},{84,96},{96... | collective-permute-start | bytes 24584 | tf_op jit(solution)/shard_map/ppermute | solution.py:40
  146.2 8.5 %collective-permute-start.22 = (f32[1,1,8,256]{3,2,1,0:T(8,128)S(1)}, f32[1,1,8,256]{3,2,1,0:T(8,128)S(1)}, u32[]{:S(2)}, u32[]{:S(2)}) collective-permute-start(f32[1,1,8,256]{3,2,1,0:T(8,128)S(1)} %get-tuple-element.92), channel_id=1, source_target_pairs={{12,0},{24,12},{36,24},{48,36},{60,48},{72,60},{84,72},{96,84},{10... | collective-permute-start | bytes 24584 | tf_op jit(solution)/shard_map/ppermute | solution.py:41
  150.3 4.4 %collective-permute-start.23 = (f32[1,4,1,256]{3,2,1,0:T(1,128)S(1)}, f32[1,4,1,256]{3,2,1,0:T(1,128)S(1)}, u32[]{:S(2)}, u32[]{:S(2)}) collective-permute-start(f32[1,4,1,256]{3,2,1,0:T(1,128)S(1)} %get-tuple-element.94), channel_id=1, source_target_pairs={{1,0},{2,1},{3,2},{4,3},{5,4},{6,5},{7,6},{8,7},{9,8},{10,9},{11,1... | collective-permute-start | bytes 12296 | tf_op jit(solution)/shard_map/ppermute | solution.py:41
  154.9 14.3 %collective-permute-start.25 = (f32[1,1,8,256]{3,2,1,0:T(8,128)S(1)}, f32[1,1,8,256]{3,2,1,0:T(8,128)S(1)}, u32[]{:S(2)}, u32[]{:S(2)}) collective-permute-start(f32[1,1,8,256]{3,2,1,0:T(8,128)S(1)} %get-tuple-element.87), channel_id=1, source_target_pairs={{0,12},{12,24},{24,36},{36,48},{48,60},{60,72},{72,84},{84,96},{96... | collective-permute-start | bytes 24584 | tf_op jit(solution)/shard_map/ppermute | solution.py:40
  160.0 9.2 %collective-permute-start.26 = (f32[1,1,8,256]{3,2,1,0:T(8,128)S(1)}, f32[1,1,8,256]{3,2,1,0:T(8,128)S(1)}, u32[]{:S(2)}, u32[]{:S(2)}) collective-permute-start(f32[1,1,8,256]{3,2,1,0:T(8,128)S(1)} %get-tuple-element.88), channel_id=1, source_target_pairs={{12,0},{24,12},{36,24},{48,36},{60,48},{72,60},{84,72},{96,84},{10... | collective-permute-start | bytes 24584 | tf_op jit(solution)/shard_map/ppermute | solution.py:41
  161.9 3.9 %collective-permute-start.24 = (f32[1,4,1,256]{3,2,1,0:T(1,128)S(1)}, f32[1,4,1,256]{3,2,1,0:T(1,128)S(1)}, u32[]{:S(2)}, u32[]{:S(2)}) collective-permute-start(f32[1,4,1,256]{3,2,1,0:T(1,128)S(1)} %get-tuple-element.89), channel_id=1, source_target_pairs={{0,1},{1,2},{2,3},{3,4},{4,5},{5,6},{6,7},{7,8},{8,9},{9,10},{10,1... | collective-permute-start | bytes 12296 | tf_op jit(solution)/shard_map/ppermute | solution.py:40
  164.5 4.6 %collective-permute-start.27 = (f32[1,4,1,256]{3,2,1,0:T(1,128)S(1)}, f32[1,4,1,256]{3,2,1,0:T(1,128)S(1)}, u32[]{:S(2)}, u32[]{:S(2)}) collective-permute-start(f32[1,4,1,256]{3,2,1,0:T(1,128)S(1)} %get-tuple-element.90), channel_id=1, source_target_pairs={{1,0},{2,1},{3,2},{4,3},{5,4},{6,5},{7,6},{8,7},{9,8},{10,9},{11,1... | collective-permute-start | bytes 12296 | tf_op jit(solution)/shard_map/ppermute | solution.py:41
  169.5 12.7 %collective-permute-start.30 = (f32[3,4,1,256]{3,2,1,0:T(1,128)S(1)}, f32[3,4,1,256]{3,2,1,0:T(1,128)S(1)}, u32[]{:S(2)}, u32[]{:S(2)}) collective-permute-start(f32[3,4,1,256]{3,2,1,0:T(1,128)S(1)} %get-tuple-element.55), channel_id=1, source_target_pairs={{1,0},{2,1},{3,2},{4,3},{5,4},{6,5},{7,6},{8,7},{9,8},{10,9},{11,1... | collective-permute-start | bytes 36872 | tf_op jit(solution)/shard_map/ppermute | solution.py:41
  170.8 11.4 %collective-permute-start.31 = (f32[3,4,1,256]{3,2,1,0:T(1,128)S(1)}, f32[3,4,1,256]{3,2,1,0:T(1,128)S(1)}, u32[]{:S(2)}, u32[]{:S(2)}) collective-permute-start(f32[3,4,1,256]{3,2,1,0:T(1,128)S(1)} %get-tuple-element.56), channel_id=1, source_target_pairs={{0,1},{1,2},{2,3},{3,4},{4,5},{5,6},{6,7},{7,8},{8,9},{9,10},{10,1... | collective-permute-start | bytes 36872 | tf_op jit(solution)/shard_map/ppermute | solution.py:40
  174.8 7.4 %collective-permute-start.29 = (f32[3,1,8,256]{3,2,1,0:T(8,128)S(1)}, f32[3,1,8,256]{3,2,1,0:T(8,128)S(1)}, u32[]{:S(2)}, u32[]{:S(2)}) collective-permute-start(f32[3,1,8,256]{3,2,1,0:T(8,128)S(1)} %get-tuple-element.57), channel_id=1, source_target_pairs={{0,12},{12,24},{24,36},{36,48},{48,60},{60,72},{72,84},{84,96},{96... | collective-permute-start | bytes 73736 | tf_op jit(solution)/shard_map/ppermute | solution.py:40
  180.1 5.1 %collective-permute-start.28 = (f32[3,1,8,256]{3,2,1,0:T(8,128)S(1)}, f32[3,1,8,256]{3,2,1,0:T(8,128)S(1)}, u32[]{:S(2)}, u32[]{:S(2)}) collective-permute-start(f32[3,1,8,256]{3,2,1,0:T(8,128)S(1)} %get-tuple-element.58), channel_id=1, source_target_pairs={{12,0},{24,12},{36,24},{48,36},{60,48},{72,60},{84,72},{96,84},{10... | collective-permute-start | bytes 73736 | tf_op jit(solution)/shard_map/ppermute | solution.py:41
  (8 other events, 91.6 us)

commit v2 on v0

v2 whole, which is shorter than its diff:
```python
import functools

import jax
import jax.numpy as jnp
from jax import lax
from jax.experimental import pallas as pl
from jax.experimental.pallas import tpu as pltpu
from jax.sharding import PartitionSpec as P

DAMPING = 0.8
F32 = jnp.float32
XO = 4
ROWS = 8
NC = 64

X_FIELD, X_VEM, X_CORNER, X_CELL13, X_CELL2, X_COARSE, X_TILES = 4, 28, 37, 45, 46, 47, 49
Y_FIELD, Y_VEM, Y_TILES = 2, 18, 23
X2_S, X2_COARSE, X2_TILES = 3, 6, 8
Y2_V, Y2_TILES = 4, 6
Y2_PLACES = (0, 1, 2, 3, 4, 5, 10, 11)


def row_index():
    return lax.broadcasted_iota(jnp.int32, (ROWS, 256), 0)


def turned(tile, by):
    return pltpu.roll(tile, by, axis=0)


def put(ref, index, tile):
    ref[8 * index : 8 * index + 8, :] = tile


def get(ref, index):
    return ref[8 * index : 8 * index + 8, :]


class Own:
    def __init__(self, place, block_ref, mobility_ref, mask_ref):
        self.mask = mask = mask_ref[place].astype(F32)
        self.rest = rest = 1.0 - mask
        self.block = [[block_ref[c, j, place] for j in range(3)] for c in range(3)]
        self.mobility = [mobility_ref[c, place] for c in range(3)]
        e = [
            [mask * self.block[c][j] + rest if c == j else mask * self.block[c][j] for j in range(3)]
            for c in range(3)
        ]
        cof = [
            [
                e[(c + 1) % 3][(j + 1) % 3] * e[(c + 2) % 3][(j + 2) % 3]
                - e[(c + 1) % 3][(j + 2) % 3] * e[(c + 2) % 3][(j + 1) % 3]
                for j in range(3)
            ]
            for c in range(3)
        ]
        recip = 1.0 / (e[0][0] * cof[0][0] + e[0][1] * cof[0][1] + e[0][2] * cof[0][2])
        self.inverse = [[cof[j][c] * recip for j in range(3)] for c in range(3)]
        self.entry = e
        self.scale = DAMPING * mask / (mask * (self.block[0][0] + self.block[1][0] + self.block[2][0]) + rest)

    def solve(self, vector):
        i = self.inverse
        return [i[c][0] * vector[0] + i[c][1] * vector[1] + i[c][2] * vector[2] for c in range(3)]

    def kappa(self):
        return self.scale * (self.mobility[0] + self.mobility[1] + self.mobility[2])

    def of_pressure(self):
        column = self.solve([self.entry[j][0] for j in range(3)])
        return [1.0 - column[0], -column[1], -column[2]]

    def of_flux(self):
        return self.solve([self.mask * self.mobility[j] for j in range(3)])


def cell_code(place, mask_ref, cell_ref):
    return jnp.where(mask_ref[place] > 0, cell_ref[place], -1).astype(F32)


def coarse_sums(cell_ref, of_row):
    wanted = lax.broadcasted_iota(jnp.int32, (NC, 256), 0)
    total = jnp.zeros((NC, 256), F32)
    for place in range(XO):
        cells, values = cell_ref[place], of_row(place)
        for row in range(ROWS):
            here = jnp.broadcast_to(cells[row : row + 1], (NC, 256)) == wanted
            total = total + jnp.where(here, jnp.broadcast_to(values[row : row + 1], (NC, 256)), 0.0)
    return jnp.sum(total[:, :128] + total[:, 128:], axis=1, keepdims=True)


def coarse_terms(sums, columns_ref, terms_ref, group):
    lane = lax.broadcasted_iota(jnp.int32, (NC // 2, 128), 1)
    weights = jnp.where(
        lane < NC,
        jnp.broadcast_to(sums[: NC // 2], (NC // 2, 128)),
        jnp.broadcast_to(sums[NC // 2 :], (NC // 2, 128)),
    )
    result = jnp.zeros(terms_ref.shape, F32)
    for j in range(group):
        terms_ref[j : j + 1, :] = columns_ref[j, NC // 2 : NC // 2 + 1, :]
    owners = terms_ref[...]
    for j in range(group):
        line = jnp.sum(columns_ref[j, : NC // 2, :] * weights, axis=0, keepdims=True)
        line = line + pltpu.roll(line, NC, axis=1)
        result = result + jnp.where(owners == float(j), jnp.broadcast_to(line, result.shape), 0.0)
    return result


def shifted_lanes(tile):
    lane = lax.broadcasted_iota(jnp.int32, (ROWS, 256), 1)
    after = jnp.where(lane < 255, pltpu.roll(tile, 255, axis=1), 0.0)
    before = jnp.where(lane > 0, pltpu.roll(tile, 1, axis=1), 0.0)
    return after, before


def flux(field, trans, place, tiles):
    own, halo = field(place, 0), field(place, 1)
    inner = row_index() < 7
    outer = row_index() > 0
    own_up, halo_up, own_down, halo_down = turned(own, 7), turned(halo, 7), turned(own, 1), turned(halo, 1)
    result = []
    for tile in tiles:
        if tile == 0:
            up, down = jnp.where(inner, own_up, halo_up), jnp.where(outer, own_down, halo_down)
        else:
            up, down = jnp.where(inner, halo_up, own_up), jnp.where(outer, halo_down, own_down)
        after, before = shifted_lanes(halo if tile else own)
        total = trans(0, place, tile) * field((place + 1) % 12, tile)
        total = total + trans(1, place, tile) * field((place + 11) % 12, tile)
        total = total + trans(2, place, tile) * up
        total = total + trans(3, place, tile) * down
        total = total + trans(4, place, tile) * after
        total = total + trans(5, place, tile) * before
        result.append(total)
    return result


def paired(tiles, to_next):
    first, second = tiles
    low = row_index() < 4
    if to_next:
        return jnp.where(low, turned(first, 4), second)
    return jnp.where(low, first, turned(second, 4))


def halo_tile(next_pair, previous_pair, which):
    low = row_index() < 4
    if which == 0:
        return jnp.where(low, next_pair, turned(previous_pair, 4))
    return jnp.where(low, turned(next_pair, 4), previous_pair)


def pack_kernel(
    group, owner_ref, rows_ref, right_ref, block_ref, mobility_ref, trans_ref, mask_ref, cell_ref,
    columns_ref, up_ref, down_ref, field_ref,
):
    lane = lax.broadcasted_iota(jnp.int32, (NC // 2, 128), 1)
    owner = jnp.full((8, 128), owner_ref[0, 0], jnp.int32).astype(F32)
    for pair in range(group // 2):
        part = rows_ref[:, 128 * pair : 128 * pair + 128]
        flipped = jnp.concatenate([part, part], axis=0).T
        for odd in range(2):
            block = flipped[NC * odd : NC * odd + NC]
            columns_ref[2 * pair + odd, : NC // 2, :] = jnp.where(lane < NC, block[: NC // 2], block[NC // 2 :])
            columns_ref[2 * pair + odd, NC // 2 :, :] = owner
    for out_ref in (up_ref, down_ref):
        out_ref[8 * Y_TILES - 4 :, :] = jnp.zeros((4, 256), F32)
    for half in range(2):
        cells, fields = [], []
        for place in (2 * half, 2 * half + 1):
            own = Own(place, block_ref, mobility_ref, mask_ref)
            cells.append(cell_code(place, mask_ref, cell_ref))
            right = [right_ref[c, place] for c in range(3)]
            fields.append(
                [trans_ref[face, place] for face in range(6)]
                + [own.kappa(), own.scale * (right[0] + right[1] + right[2])]
            )
            vem = [own.mask * v for v in own.solve(right)] + own.of_pressure() + own.of_flux()
            for f in range(9):
                field_ref[...] = vem[f]
                spot = 8 * Y_VEM + 4 * f + place
                up_ref[spot : spot + 1, :] = field_ref[7:8, :]
                down_ref[spot : spot + 1, :] = field_ref[0:1, :]
        for out_ref, to_next in ((up_ref, True), (down_ref, False)):
            put(out_ref, half, paired(cells, to_next))
            for k in range(8):
                put(out_ref, Y_FIELD + 2 * k + half, paired([fields[0][k], fields[1][k]], to_next))


def y_halo(next_ref, previous_ref, index, place):
    at = index + place // 2
    return halo_tile(get(next_ref, at), get(previous_ref, at), place % 2)


def sides_kernel(
    group, right_ref, block_ref, mobility_ref, trans_ref, mask_ref, cell_ref, columns_ref, yn_ref, yp_ref,
    fore_ref, back_ref, terms_ref, scratch_ref,
):
    row = row_index()
    middle = (row == 3) | (row == 4)
    outs = (fore_ref, lambda d: 4 - d), (back_ref, lambda d: d - 1)
    for place in range(XO):
        own = Own(place, block_ref, mobility_ref, mask_ref)
        right = [right_ref[c, place] for c in range(3)]
        cells = cell_code(place, mask_ref, cell_ref)
        kappa, source = own.kappa(), own.scale * (right[0] + right[1] + right[2])
        for out_ref, at in outs:
            distance = next(d for d in range(1, 5) if at(d) == place)
            put(out_ref, distance - 1, cells)
            if distance < 4:
                for k in range(8):
                    value = trans_ref[k, place] if k < 6 else (kappa if k == 6 else source)
                    put(out_ref, X_FIELD + 3 * k + distance - 1, value)
            if distance == 1:
                vem = [own.mask * v for v in own.solve(right)] + own.of_pressure() + own.of_flux()
                for f in range(9):
                    put(out_ref, X_VEM + f, vem[f])
    for out_ref, at in outs:
        for k in range(8):
            near, far = [y_halo(yn_ref, yp_ref, Y_FIELD + 2 * k, at(d)) for d in (1, 2)]
            put(out_ref, X_CORNER + k, jnp.where(middle, turned(far, 4), near))
        near, mid, far = [y_halo(yn_ref, yp_ref, 0, at(d)) for d in (1, 2, 3)]
        put(out_ref, X_CELL13, jnp.where(middle, turned(far, 4), near))
        put(out_ref, X_CELL2, mid)
    sums = coarse_sums(cell_ref, lambda i: right_ref[0, i] + right_ref[1, i] + right_ref[2, i])
    terms = coarse_terms(sums, columns_ref, scratch_ref, group)
    terms_ref[...] = terms
    for out_ref, _ in outs:
        out_ref[8 * X_COARSE :, :128] = terms
        out_ref[8 * X_COARSE :, 128:] = jnp.zeros((16, 128), F32)


def write_slots(group, slots_ref, three):
    lane = lax.broadcasted_iota(jnp.int32, (1, 128), 1)
    zero = jnp.zeros((1, 128), F32)
    for b in range(group):
        slots_ref[b, 6:8, :] = jnp.zeros((2, 128), F32)
        for i, line in enumerate(three):
            after = line(b + 1) if b + 1 < group else zero
            before = line(b - 1) if b > 0 else zero
            slots_ref[b, i : i + 1, :] = line(b)
            slots_ref[b, 3 + i : 4 + i, :] = jnp.where(lane < NC, after, before)


def three_groups(terms_ref, next_ref, previous_ref, start):
    return (
        lambda b: terms_ref[b : b + 1, :],
        lambda b: next_ref[start + b : start + b + 1, :128],
        lambda b: previous_ref[start + b : start + b + 1, :128],
    )


def slots_kernel(group, terms_ref, next_ref, previous_ref, slots_ref):
    write_slots(group, slots_ref, three_groups(terms_ref, next_ref, previous_ref, 0))


def forward_kernel(group, terms_ref, source_ref, solved_ref, next_ref, previous_ref, slots_ref, up_ref, down_ref):
    write_slots(group, slots_ref, three_groups(terms_ref, next_ref, previous_ref, 8 * X2_COARSE))

    def source(place):
        if place < 4:
            return source_ref[place]
        return get(next_ref, X2_S + place - 4) if place < 8 else get(previous_ref, X2_S + 11 - place)

    for out_ref, to_next in ((up_ref, True), (down_ref, False)):
        for half in range(4):
            put(out_ref, half, paired([source(Y2_PLACES[2 * half]), source(Y2_PLACES[2 * half + 1])], to_next))
        out_ref[8 * Y2_TILES - 4 :, :] = jnp.zeros((4, 256), F32)
        edge = 7 if to_next else 0
        for f in range(3):
            for place in range(XO):
                spot = 8 * Y2_V + 4 * f + place
                out_ref[spot : spot + 1, :] = solved_ref[f, place, edge : edge + 1, :]


class Fields:
    def __init__(self, trans_ref, xn_ref, xp_ref, yn_ref, yp_ref, own):
        self.trans_ref, self.x, self.y, self.own = trans_ref, (xn_ref, xp_ref), (yn_ref, yp_ref), own

    def side(self, place):
        return (self.x[0], place - 3) if place < 8 else (self.x[1], 12 - place)

    def field(self, k, place, tile):
        if place < 4:
            if tile:
                return y_halo(self.y[0], self.y[1], Y_FIELD + 2 * k, place)
            return self.trans_ref[k, place] if k < 6 else self.own(k, place)
        ref, d = self.side(place)
        if tile == 0:
            return get(ref, X_FIELD + 3 * k + d - 1)
        corner = get(ref, X_CORNER + k)
        return corner if d == 1 else turned(corner, 4)

    def trans(self, face, place, tile):
        return self.field(face, place, tile)

    def cells(self, place, tile, own_cells):
        if place < 4:
            return y_halo(self.y[0], self.y[1], 0, place) if tile else own_cells(place)
        ref, d = self.side(place)
        if tile == 0:
            return get(ref, d - 1)
        if d == 2:
            return get(ref, X_CELL2)
        corner = get(ref, X_CELL13)
        return corner if d == 1 else turned(corner, 4)

    def vem(self, f, place, tile):
        if tile == 0:
            return get(self.x[0] if place == 4 else self.x[1], X_VEM + f)
        return edge_rows(self.y[0], self.y[1], 8 * Y_VEM + 4 * f + place)


def edge_rows(next_ref, previous_ref, spot):
    after = jnp.broadcast_to(next_ref[spot : spot + 1, :], (ROWS, 256))
    before = jnp.broadcast_to(previous_ref[spot : spot + 1, :], (ROWS, 256))
    return jnp.where(row_index() < 4, after, before)


def picked(coarse, code, tile, group):
    index = jnp.maximum(code, 0.0).astype(jnp.int32)
    if tile:
        index = index + jnp.where(row_index() < 4, 0, NC)
    line = 3 * tile + group
    table = jnp.broadcast_to(coarse[line : line + 1, :], (ROWS, 128))
    found = [jnp.take_along_axis(table, index[:, 128 * h : 128 * h + 128], axis=1) for h in range(2)]
    return jnp.where(code >= 0.0, jnp.concatenate(found, axis=1), 0.0)


def application(group, fields, slots_ref, own_cells, source, solved, owns, p_ref, q_ref, z_ref, zo_ref, w_ref):
    coarse = slots_ref[0]
    for b in range(1, group):
        coarse = coarse + slots_ref[b]
    for place in range(12):
        for tile in range(2):
            if tile and place in (7, 8):
                continue
            code = fields.cells(place, tile, own_cells)
            p_ref[2 * place + tile] = picked(coarse, code, tile, (place >= 4) + (place >= 8))

    def sweep(from_ref, to_ref, both, single):
        def pressure(place, tile):
            return from_ref[2 * place + tile]

        for place in both + single:
            tiles = (0, 1) if place in both else (0,)
            for tile, total in zip(tiles, flux(pressure, fields.trans, place, tiles), strict=True):
                to_ref[2 * place + tile] = (
                    (1.0 - DAMPING) * pressure(place, tile)
                    + source(place, tile)
                    + fields.field(6, place, tile) * total
                )

    sweep(p_ref, q_ref, (0, 1, 2, 3, 4, 5, 10, 11), (6, 9))
    sweep(q_ref, p_ref, (0, 1, 2, 3, 4, 11), (5, 10))

    def pressure(place, tile):
        return p_ref[2 * place + tile]

    for place in (0, 1, 2, 3, 4, 11):
        tiles = (0, 1) if place < 4 else (0,)
        for tile, total in zip(tiles, flux(pressure, fields.trans, place, tiles), strict=True):
            p = pressure(place, tile)
            inside = place < 4 and tile == 0
            if inside:
                own = owns(place)
                e, m = own.of_pressure(), own.of_flux()
            else:
                e, m = ([fields.vem(3 * part + c, place, tile) for c in range(3)] for part in (1, 2))
            v = solved(place, tile)
            for c in range(3):
                z = v[c] + e[c] * p + m[c] * total
                if inside:
                    zo_ref[c, place] = z
                    z = own.mask * z
                z_ref[c, 2 * place + tile] = z
    for place in range(4):
        own = owns(place)
        fluxes = [flux(lambda i, t, c=c: z_ref[c, 2 * i + t], fields.trans, place, (0,))[0] for c in range(3)]
        z = [zo_ref[c, place] for c in range(3)]
        for c in range(3):
            direct = own.block[c][0] * z[0] + own.block[c][1] * z[1] + own.block[c][2] * z[2]
            total = fluxes[0] if c == 0 else fluxes[0] + fluxes[c]
            w_ref[c, place] = own.mask * (direct - own.mobility[c] * total) + own.rest * z[c]


def first_kernel(
    group, right_ref, block_ref, mobility_ref, trans_ref, mask_ref, cell_ref, columns_ref,
    xn_ref, xp_ref, yn_ref, yp_ref, slots_ref,
    zo_ref, w_ref, fore_ref, back_ref, terms_ref, source_ref, solved_ref,
    p_ref, q_ref, z_ref, scratch_ref, kappa_ref,
):
    def owns(place):
        return Own(place, block_ref, mobility_ref, mask_ref)

    def right(place):
        return [right_ref[c, place] for c in range(3)]

    for place in range(4):
        own = owns(place)
        r = right(place)
        kappa_ref[place] = own.kappa()
        source_ref[place] = own.scale * (r[0] + r[1] + r[2])
        v = own.solve(r)
        for c in range(3):
            solved_ref[c, place] = v[c]
    fields = Fields(
        trans_ref, xn_ref, xp_ref, yn_ref, yp_ref,
        lambda k, place: kappa_ref[place] if k == 6 else source_ref[place],
    )

    def solved(place, tile):
        if place < 4 and tile == 0:
            return [solved_ref[c, place] for c in range(3)]
        return [fields.vem(c, place, tile) for c in range(3)]

    application(
        group, fields, slots_ref, lambda place: cell_code(place, mask_ref, cell_ref),
        lambda place, tile: fields.field(7, place, tile), solved, owns, p_ref, q_ref, z_ref, zo_ref, w_ref,
    )
    for place in range(4):
        own = owns(place)
        w = [w_ref[c, place] for c in range(3)]
        source = own.scale * (w[0] + w[1] + w[2])
        v = [own.mask * part for part in own.solve(w)]
        source_ref[place] = source
        for c in range(3):
            solved_ref[c, place] = v[c]
        for out_ref, distance in ((fore_ref, 4 - place), (back_ref, place + 1)):
            if distance < 4:
                put(out_ref, X2_S + distance - 1, source)
            if distance == 1:
                for c in range(3):
                    put(out_ref, c, v[c])
    sums = coarse_sums(cell_ref, lambda i: w_ref[0, i] + w_ref[1, i] + w_ref[2, i])
    terms = coarse_terms(sums, columns_ref, scratch_ref, group)
    terms_ref[...] = terms
    for out_ref in (fore_ref, back_ref):
        out_ref[8 * X2_COARSE :, :128] = terms
        out_ref[8 * X2_COARSE :, 128:] = jnp.zeros((16, 128), F32)


def second_kernel(
    group, right_ref, block_ref, mobility_ref, trans_ref, mask_ref, cell_ref,
    xn_ref, xp_ref, yn_ref, yp_ref, slots_ref, w1_ref, source_ref, xn2_ref, xp2_ref, yn2_ref, yp2_ref,
    zo_ref, sums_ref,
    w_ref, p_ref, q_ref, z_ref, kappa_ref,
):
    def owns(place):
        return Own(place, block_ref, mobility_ref, mask_ref)

    for place in range(4):
        kappa_ref[place] = owns(place).kappa()
    fields = Fields(trans_ref, xn_ref, xp_ref, yn_ref, yp_ref, lambda k, place: kappa_ref[place])

    def source(place, tile):
        if tile:
            at = Y2_PLACES.index(place)
            return halo_tile(get(yn2_ref, at // 2), get(yp2_ref, at // 2), at % 2)
        if place < 4:
            return source_ref[place]
        return get(xn2_ref, X2_S + place - 4) if place < 8 else get(xp2_ref, X2_S + 11 - place)

    def solved(place, tile):
        if tile:
            return [edge_rows(yn2_ref, yp2_ref, 8 * Y2_V + 4 * c + place) for c in range(3)]
        if place < 4:
            return owns(place).solve([w1_ref[c, place] for c in range(3)])
        return [get(xn2_ref if place == 4 else xp2_ref, c) for c in range(3)]

    application(
        group, fields, slots_ref, lambda place: cell_code(place, mask_ref, cell_ref),
        source, solved, owns, p_ref, q_ref, z_ref, zo_ref, w_ref,
    )
    lane = lax.broadcasted_iota(jnp.int32, (1, 128), 1)
    totals = [jnp.zeros((ROWS, 256), F32) for _ in range(5)]
    for place in range(4):
        for c in range(3):
            a, b, r = w1_ref[c, place], w_ref[c, place], right_ref[c, place]
            for i, term in enumerate((a * a, a * b, b * b, a * r, b * r)):
                totals[i] = totals[i] + term
    line = jnp.zeros((1, 128), F32)
    for i in range(5):
        value = jnp.sum(jnp.sum(totals[i], axis=0, keepdims=True), axis=1, keepdims=True)
        line = line + jnp.where(lane == i, jnp.broadcast_to(value, (1, 128)), 0.0)
    sums_ref[...] = jnp.broadcast_to(line[None], sums_ref.shape)


def regroup_kernel(parts_ref, sums_ref):
    line = jnp.sum(parts_ref[...], axis=0)
    sums_ref[...] = jnp.broadcast_to(line[None], sums_ref.shape)


def combine_kernel(parts_ref, z1_ref, z2_ref, out_ref):
    line = jnp.sum(parts_ref[...], axis=0)
    g11, g12, g22, h1, h2 = [line[:, i : i + 1] for i in range(5)]
    determinant = g11 * g22 - g12 * g12
    c1 = jnp.broadcast_to((g22 * h1 - g12 * h2) / determinant, (ROWS, 256))
    c2 = jnp.broadcast_to((g11 * h2 - g12 * h1) / determinant, (ROWS, 256))
    for c in range(3):
        for place in range(XO):
            out_ref[c, place] = c1 * z1_ref[c, place] + c2 * z2_ref[c, place]


def call(kernel, outs, scratch, *args, smem=0):
    vmem = pl.BlockSpec(memory_space=pltpu.VMEM)
    return pl.pallas_call(
        kernel,
        out_shape=[jax.ShapeDtypeStruct(shape, F32) for shape in outs],
        in_specs=[pl.BlockSpec(memory_space=pltpu.SMEM)] * smem + [vmem] * (len(args) - smem),
        out_specs=[vmem] * len(outs),
        scratch_shapes=[pltpu.VMEM(shape, F32) for shape in scratch],
        compiler_params=pltpu.CompilerParams(vmem_limit_bytes=40 * 2**20),
    )(*args)


def send(values, axis, step):
    count = lax.axis_size(axis)
    pairs = [(i, i + step) for i in range(count) if 0 <= i + step < count]
    return lax.ppermute(values, axis, pairs)


def on_device(
    right_side, block_matrix, mobility, trans, active_mask, cell_map, coarse_owner, coarse_rows
):
    group = lax.axis_size("gy")
    line = lax.axis_size("gx")
    local = (right_side, block_matrix, mobility, trans, active_mask, cell_map)
    field = (3, XO, ROWS, 256)
    columns, up, down = call(
        functools.partial(pack_kernel, group),
        [(group, 40, 128), (8 * Y_TILES, 256), (8 * Y_TILES, 256)],
        [(ROWS, 256)],
        coarse_owner, coarse_rows, *local,
        smem=1,
    )
    columns = lax.all_to_all(columns, "gy", 0, 0)
    y_previous, y_next = send(up, "gy", 1), send(down, "gy", -1)
    fore, back, terms = call(
        functools.partial(sides_kernel, group),
        [(8 * X_TILES, 256), (8 * X_TILES, 256), (16, 128)],
        [(16, 128)],
        *local, columns, y_next, y_previous,
    )
    x_previous, x_next = send(fore, "gx", 1), send(back, "gx", -1)
    (slots,) = call(
        functools.partial(slots_kernel, group),
        [(group, 8, 128)],
        [],
        terms, x_next[8 * X_COARSE :], x_previous[8 * X_COARSE :],
    )
    slots = lax.all_to_all(slots, "gy", 0, 0)
    halos = (x_next, x_previous, y_next, y_previous)
    work = [(24, ROWS, 256), (24, ROWS, 256), (3, 24, ROWS, 256)]
    first_z, first_w, fore, back, terms, source, solved = call(
        functools.partial(first_kernel, group),
        [field, field, (8 * X2_TILES, 256), (8 * X2_TILES, 256), (16, 128), (XO, ROWS, 256), field],
        work + [(16, 128), (XO, ROWS, 256)],
        *local, columns, *halos, slots,
    )
    x2_previous, x2_next = send(fore, "gx", 1), send(back, "gx", -1)
    slots, up, down = call(
        functools.partial(forward_kernel, group),
        [(group, 8, 128), (8 * Y2_TILES, 256), (8 * Y2_TILES, 256)],
        [],
        terms, source, solved, x2_next, x2_previous,
    )
    slots = lax.all_to_all(slots, "gy", 0, 0)
    y2_previous, y2_next = send(up, "gy", 1), send(down, "gy", -1)
    second_z, sums = call(
        functools.partial(second_kernel, group),
        [field, (line, 1, 128)],
        [field] + work + [(XO, ROWS, 256)],
        *local, *halos, slots, first_w, source, x2_next, x2_previous, y2_next, y2_previous,
    )
    sums = lax.all_to_all(sums, "gx", 0, 0)
    (sums,) = call(regroup_kernel, [(group, 1, 128)], [], sums)
    sums = lax.all_to_all(sums, "gy", 0, 0)
    return call(combine_kernel, [field], [], sums, first_z, second_z)[0]


def solution(mesh):
    in_specs = (
        P(None, "gx", "gy", None),
        P(None, None, "gx", "gy", None),
        P(None, "gx", "gy", None),
        P(None, "gx", "gy", None),
        P("gx", "gy", None),
        P("gx", "gy", None),
        P("gx", "gy"),
        P(("gx", "gy"), None),
    )
    out_specs = P(None, "gx", "gy", None)
    return jax.shard_map(
        on_device, mesh=mesh, in_specs=in_specs, out_specs=out_specs, check_vma=False
    )
```

time: 483 us -> 135 us (0.28)
  blocking collectives: 321 us -> 55.6 us
  starting transfers between devices: 98.1 us -> 47.3 us
  waiting for transfers between devices: 39.2 us -> 18.6 us
  between operations: 10.3 us -> 0.84 us
  Pallas kernels: 0 us -> 5.32 us
    psum x2 -> x0, blocking collectives: 243 us -> none  [the longest x1 122 us: on_device(): lax.psum((jnp.sum(first_w * second_w), jnp.sum(second_w * second_w), jnp....]
    unnamed x4 -> x0, blocking collectives: 77.8 us -> none
    ppermute x32 -> x8, starting transfers between devices: 98.1 us -> 28 us  [send(): return lax.ppermute(values, axis, pairs)]
    all_to_all x0 -> x3, blocking collectives: none -> 55.6 us  [the longest x1 23.9 us: on_device(): sums = lax.all_to_all(sums, 'gx', 0, 0)]
    ppermute x32 -> x8, waiting for transfers between devices: 39.2 us -> 15.5 us  [send(): return lax.ppermute(values, axis, pairs)]
    all_to_all x0 -> x2, starting transfers between devices: none -> 19.3 us  [the longest x1 15.8 us: on_device(): columns = lax.all_to_all(columns, 'gy', 0, 0)]
    pallas_call x0 -> x8, Pallas kernels: none -> 5.32 us  [call(): pl.pallas_call(kernel, out_shape=[jax.ShapeDtypeStruct(shape, F32) for sh...]
  transfers between devices with their start and end apart: 32 -> 10, of which waited for: 16 -> 6; matrix products, arithmetic and copies ran while one was open for 0% -> 0% of each run, Pallas kernels for 0% -> 0%
where the time goes in v2:
time: 135 us; the launch traced here: 134 us
  blocking collectives  55.6 us (41%)
  starting transfers between devices  47.3 us (35%)
  waiting for transfers between devices  18.6 us (14%)
  local copies, waits for them, and re-layouts  6.13 us (5%)
  Pallas kernels  5.32 us (4%)
    ppermute x8, starting transfers between devices, send(): return lax.ppermute(values, axis, pairs)  28 us
    all_to_all x1, blocking collectives, on_device(): sums = lax.all_to_all(sums, 'gx', 0, 0)  23.9 us
    all_to_all x1, blocking collectives, on_device(): sums = lax.all_to_all(sums, 'gy', 0, 0)  16.6 us
    all_to_all x1, starting transfers between devices, on_device(): columns = lax.all_to_all(columns, 'gy', 0, 0)  15.8 us
    ppermute x8, waiting for transfers between devices, send(): return lax.ppermute(values, axis, pairs)  15.5 us
    all_to_all x1, blocking collectives, on_device(): slots = lax.all_to_all(slots, 'gy', 0, 0)  15 us
    unnamed x26, local copies, waits for them, and re-layouts  6.13 us
    pallas_call x8, Pallas kernels, call(): pl.pallas_call(kernel, out_shape=[jax.ShapeDtypeStruct(shape, F32) for sh...  5.32 us
  transfers between devices with their start and end apart: 10, of which 6 were waited for; matrix products, arithmetic and copies ran while one was open for 0% of the time, Pallas kernels for 0%

profile of v2, /device:TPU:1, one launch (start us, length us, event | category | flops | bytes accessed | tf_op | source)
XLA Modules:
  0.0 133.8 jit_solution(4255138870833868301)
XLA Ops:
  0.7 1.0 copy-done
  1.6 0.9 copy-done.2
  2.5 0.9 copy-done.4
  3.4 0.9 copy-done.6
  4.3 0.8 copy-done.8
  5.1 0.8 copy-done.10
  5.8 0.9 copy-done.12
  6.8 1.0 shard_map.82
  7.7 15.8 %all-to-all-start = ((f32[12,40,128]{2,1,0:T(8,128)}), f32[12,40,128]{2,1,0:T(8,128)S(1)}, u32[]{:S(2)}, u32[]{:S(2)}) async-start(f32[12,40,128]{2,1,0:T(8,128)} %get-tuple-element.23), calls=%async_computation | async-start | bytes 491520 | tf_op jit(solution)/shard_map/all_to_all | solution.py:538
  23.6 1.3 collective-permute-start
  24.9 4.0 %collective-permute-start.1 = (f32[184,256]{1,0:T(8,128)S(1)}, f32[184,256]{1,0:T(8,128)S(1)}, u32[]{:S(2)}, u32[]{:S(2)}) collective-permute-start(f32[184,256]{1,0:T(8,128)S(1)} %get-tuple-element.25), channel_id=1, source_target_pairs={{0,1},{1,2},{2,3},{3,4},{4,5},{5,6},{6,7},{7,8},{8,9},{9,10},{10,1... | collective-permute-start | bytes 565256 | tf_op jit(solution)/shard_map/ppermute | solution.py:521
  28.9 8.2 %collective-permute-done.yn_ref = f32[184,256]{1,0:T(8,128)S(1)} collective-permute-done((f32[184,256]{1,0:T(8,128)S(1)}, f32[184,256]{1,0:T(8,128)S(1)}, u32[]{:S(2)}, u32[]{:S(2)}) %collective-permute-start) | collective-permute-done | bytes 188448 | tf_op jit(solution)/shard_map/ppermute | solution.py:521
  37.2 0.5 shard_map.83
  37.7 6.4 %collective-permute-start.2 = (f32[392,256]{1,0:T(8,128)S(1)}, f32[392,256]{1,0:T(8,128)S(1)}, u32[]{:S(2)}, u32[]{:S(2)}) collective-permute-start(f32[392,256]{1,0:T(8,128)S(1)} %get-tuple-element.26), channel_id=1, source_target_pairs={{12,0},{24,12},{36,24},{48,36},{60,48},{72,60},{84,72},{96,84},{10... | collective-permute-start | bytes 1204232 | tf_op jit(solution)/shard_map/ppermute | solution.py:521
  44.1 3.1 %collective-permute-start.3 = (f32[392,256]{1,0:T(8,128)S(1)}, f32[392,256]{1,0:T(8,128)S(1)}, u32[]{:S(2)}, u32[]{:S(2)}) collective-permute-start(f32[392,256]{1,0:T(8,128)S(1)} %get-tuple-element.27), channel_id=1, source_target_pairs={{0,12},{12,24},{24,36},{36,48},{48,60},{60,72},{72,84},{84,96},{96... | collective-permute-start | bytes 1204232 | tf_op jit(solution)/shard_map/ppermute | solution.py:521
  47.2 3.6 %collective-permute-done.2.xn_ref = f32[392,256]{1,0:T(8,128)S(1)} collective-permute-done((f32[392,256]{1,0:T(8,128)S(1)}, f32[392,256]{1,0:T(8,128)S(1)}, u32[]{:S(2)}, u32[]{:S(2)}) %collective-permute-start.2) | collective-permute-done | bytes 401440 | tf_op jit(solution)/shard_map/ppermute | solution.py:521
  50.8 1.2 collective-permute-done.3.xp_ref
  52.0 15.0 %all_to_all.25.slots_ref = f32[12,8,128]{2,1,0:T(8,128)S(1)} all-to-all(f32[12,8,128]{2,1,0:T(8,128)S(1)} %shard_map.84), channel_id=1, replica_groups=mesh['gx'=64,'gy'=12] {'gy'}, dimensions={0} | all-to-all | bytes 98304 | tf_op jit(solution)/shard_map/all_to_all | solution.py:553
  67.0 1.3 shard_map.85
  68.4 1.9 %collective-permute-start.4 = (f32[64,256]{1,0:T(8,128)S(1)}, f32[64,256]{1,0:T(8,128)S(1)}, u32[]{:S(2)}, u32[]{:S(2)}) collective-permute-start(f32[64,256]{1,0:T(8,128)S(1)} %get-tuple-element.32), channel_id=1, source_target_pairs={{12,0},{24,12},{36,24},{48,36},{60,48},{72,60},{84,72},{96,84},{10... | collective-permute-start | bytes 196616 | tf_op jit(solution)/shard_map/ppermute | solution.py:521
  70.3 6.0 %collective-permute-start.5 = (f32[64,256]{1,0:T(8,128)S(1)}, f32[64,256]{1,0:T(8,128)S(1)}, u32[]{:S(2)}, u32[]{:S(2)}) collective-permute-start(f32[64,256]{1,0:T(8,128)S(1)} %get-tuple-element.33), channel_id=1, source_target_pairs={{0,12},{12,24},{24,36},{36,48},{48,60},{60,72},{72,84},{84,96},{96... | collective-permute-start | bytes 196616 | tf_op jit(solution)/shard_map/ppermute | solution.py:521
  76.3 1.3 collective-permute-done.5.previous_ref.xp2_ref
  77.6 0.7 shard_map.86
  78.3 3.5 %all-to-all-start.2 = ((f32[12,8,128]{2,1,0:T(8,128)}), f32[12,8,128]{2,1,0:T(8,128)S(1)}, u32[]{:S(2)}, u32[]{:S(2)}) async-start(f32[12,8,128]{2,1,0:T(8,128)} %get-tuple-element.34), calls=%async_computation.2 | async-start | bytes 98304 | tf_op jit(solution)/shard_map/all_to_all | solution.py:569
  81.8 1.3 collective-permute-start.6
  83.1 4.0 %collective-permute-start.7 = (f32[48,256]{1,0:T(8,128)S(1)}, f32[48,256]{1,0:T(8,128)S(1)}, u32[]{:S(2)}, u32[]{:S(2)}) collective-permute-start(f32[48,256]{1,0:T(8,128)S(1)} %get-tuple-element.37), channel_id=1, source_target_pairs={{0,1},{1,2},{2,3},{3,4},{4,5},{5,6},{6,7},{7,8},{8,9},{9,10},{10,1... | collective-permute-start | bytes 147464 | tf_op jit(solution)/shard_map/ppermute | solution.py:521
  87.1 1.1 collective-permute-done.7.yp2_ref
  88.2 3.2 %all-to-all-done.2.slots_ref = f32[12,8,128]{2,1,0:T(8,128)S(1)} async-done(((f32[12,8,128]{2,1,0:T(8,128)}), f32[12,8,128]{2,1,0:T(8,128)S(1)}, u32[]{:S(2)}, u32[]{:S(2)}) %all-to-all-start.2) | async-done | bytes 49184 | tf_op jit(solution)/shard_map/all_to_all | solution.py:569
  91.4 0.9 shard_map.87
  92.3 23.9 %all_to_all.26.parts_ref = f32[64,1,128]{2,1,0:T(1,128)S(1)} all-to-all(f32[64,1,128]{2,1,0:T(1,128)S(1)} %get-tuple-element.38), channel_id=1, replica_groups=mesh['gx'=64,'gy'=12] {'gx'}, dimensions={0} | all-to-all | bytes 65536 | tf_op jit(solution)/shard_map/all_to_all | solution.py:577
  116.3 16.6 %all_to_all.27.parts_ref = f32[12,1,128]{2,1,0:T(1,128)S(1)} all-to-all(f32[12,1,128]{2,1,0:T(1,128)S(1)} %shard_map.88), channel_id=1, replica_groups=mesh['gx'=64,'gy'=12] {'gy'}, dimensions={0} | all-to-all | bytes 12288 | tf_op jit(solution)/shard_map/all_to_all | solution.py:579
  132.9 0.9 shard_map.89
  (27 shorter events, 0.2 us)
Async XLA Ops:
  0.7 1.0 copy-start
  1.6 0.9 copy-start.2
  2.5 0.9 copy-start.4
  3.4 0.9 copy-start.6
  4.3 0.8 copy-start.8
  5.1 0.8 copy-start.10
  5.8 0.9 copy-start.12
  6.8 30.4 %copy-start.5 = (f32[3,4,8,256]{3,2,1,0:T(8,128)S(1)}, f32[3,4,8,256]{3,2,1,0:T(8,128)}, u32[]{:S(2)}) copy-start(f32[3,4,8,256]{3,2,1,0:T(8,128)} %right_ref.7) | copy-start | bytes 294916
  6.8 30.4 %copy-start.7 = (f32[3,4,8,256]{3,2,1,0:T(8,128)S(1)}, f32[3,4,8,256]{3,2,1,0:T(8,128)}, u32[]{:S(2)}) copy-start(f32[3,4,8,256]{3,2,1,0:T(8,128)} %mobility_ref.7) | copy-start | bytes 294916
  6.8 30.4 %copy-start.9 = (s32[4,8,256]{2,1,0:T(8,128)S(1)}, s32[4,8,256]{2,1,0:T(8,128)}, u32[]{:S(2)}) copy-start(s32[4,8,256]{2,1,0:T(8,128)} %mask_ref.7) | copy-start | bytes 98308
  6.8 30.4 %copy-start.11 = (s32[4,8,256]{2,1,0:T(8,128)S(1)}, s32[4,8,256]{2,1,0:T(8,128)}, u32[]{:S(2)}) copy-start(s32[4,8,256]{2,1,0:T(8,128)} %cell_ref.7) | copy-start | bytes 98308
  7.7 29.4 %copy-start.1 = (f32[3,3,4,8,256]{4,3,2,1,0:T(8,128)S(1)}, f32[3,3,4,8,256]{4,3,2,1,0:T(8,128)}, u32[]{:S(2)}) copy-start(f32[3,3,4,8,256]{4,3,2,1,0:T(8,128)} %block_ref.7) | copy-start | bytes 884740
  7.7 29.4 %copy-start.3 = (f32[6,4,8,256]{3,2,1,0:T(8,128)S(1)}, f32[6,4,8,256]{3,2,1,0:T(8,128)}, u32[]{:S(2)}) copy-start(f32[6,4,8,256]{3,2,1,0:T(8,128)} %trans_ref.7) | copy-start | bytes 589828
  7.7 29.4 %all-to-all-start = ((f32[12,40,128]{2,1,0:T(8,128)}), f32[12,40,128]{2,1,0:T(8,128)S(1)}, u32[]{:S(2)}, u32[]{:S(2)}) async-start(f32[12,40,128]{2,1,0:T(8,128)} %get-tuple-element.23), calls=%async_computation | async-start | bytes 491520 | tf_op jit(solution)/shard_map/all_to_all | solution.py:538
  23.6 13.5 %collective-permute-start = (f32[184,256]{1,0:T(8,128)S(1)}, f32[184,256]{1,0:T(8,128)S(1)}, u32[]{:S(2)}, u32[]{:S(2)}) collective-permute-start(f32[184,256]{1,0:T(8,128)S(1)} %get-tuple-element.24), channel_id=1, source_target_pairs={{1,0},{2,1},{3,2},{4,3},{5,4},{6,5},{7,6},{8,7},{9,8},{10,9},{11,1... | collective-permute-start | bytes 565256 | tf_op jit(solution)/shard_map/ppermute | solution.py:521
  24.9 12.2 %collective-permute-start.1 = (f32[184,256]{1,0:T(8,128)S(1)}, f32[184,256]{1,0:T(8,128)S(1)}, u32[]{:S(2)}, u32[]{:S(2)}) collective-permute-start(f32[184,256]{1,0:T(8,128)S(1)} %get-tuple-element.25), channel_id=1, source_target_pairs={{0,1},{1,2},{2,3},{3,4},{4,5},{5,6},{6,7},{7,8},{8,9},{9,10},{10,1... | collective-permute-start | bytes 565256 | tf_op jit(solution)/shard_map/ppermute | solution.py:521
  37.7 13.1 %collective-permute-start.2 = (f32[392,256]{1,0:T(8,128)S(1)}, f32[392,256]{1,0:T(8,128)S(1)}, u32[]{:S(2)}, u32[]{:S(2)}) collective-permute-start(f32[392,256]{1,0:T(8,128)S(1)} %get-tuple-element.26), channel_id=1, source_target_pairs={{12,0},{24,12},{36,24},{48,36},{60,48},{72,60},{84,72},{96,84},{10... | collective-permute-start | bytes 1204232 | tf_op jit(solution)/shard_map/ppermute | solution.py:521
  44.1 7.9 %collective-permute-start.3 = (f32[392,256]{1,0:T(8,128)S(1)}, f32[392,256]{1,0:T(8,128)S(1)}, u32[]{:S(2)}, u32[]{:S(2)}) collective-permute-start(f32[392,256]{1,0:T(8,128)S(1)} %get-tuple-element.27), channel_id=1, source_target_pairs={{0,12},{12,24},{24,36},{36,48},{48,60},{60,72},{72,84},{84,96},{96... | collective-permute-start | bytes 1204232 | tf_op jit(solution)/shard_map/ppermute | solution.py:521
  68.4 7.9 %collective-permute-start.4 = (f32[64,256]{1,0:T(8,128)S(1)}, f32[64,256]{1,0:T(8,128)S(1)}, u32[]{:S(2)}, u32[]{:S(2)}) collective-permute-start(f32[64,256]{1,0:T(8,128)S(1)} %get-tuple-element.32), channel_id=1, source_target_pairs={{12,0},{24,12},{36,24},{48,36},{60,48},{72,60},{84,72},{96,84},{10... | collective-permute-start | bytes 196616 | tf_op jit(solution)/shard_map/ppermute | solution.py:521
  70.3 7.3 %collective-permute-start.5 = (f32[64,256]{1,0:T(8,128)S(1)}, f32[64,256]{1,0:T(8,128)S(1)}, u32[]{:S(2)}, u32[]{:S(2)}) collective-permute-start(f32[64,256]{1,0:T(8,128)S(1)} %get-tuple-element.33), channel_id=1, source_target_pairs={{0,12},{12,24},{24,36},{36,48},{48,60},{60,72},{72,84},{84,96},{96... | collective-permute-start | bytes 196616 | tf_op jit(solution)/shard_map/ppermute | solution.py:521
  78.3 13.1 %all-to-all-start.2 = ((f32[12,8,128]{2,1,0:T(8,128)}), f32[12,8,128]{2,1,0:T(8,128)S(1)}, u32[]{:S(2)}, u32[]{:S(2)}) async-start(f32[12,8,128]{2,1,0:T(8,128)} %get-tuple-element.34), calls=%async_computation.2 | async-start | bytes 98304 | tf_op jit(solution)/shard_map/all_to_all | solution.py:569
  81.8 5.3 %collective-permute-start.6 = (f32[48,256]{1,0:T(8,128)S(1)}, f32[48,256]{1,0:T(8,128)S(1)}, u32[]{:S(2)}, u32[]{:S(2)}) collective-permute-start(f32[48,256]{1,0:T(8,128)S(1)} %get-tuple-element.36), channel_id=1, source_target_pairs={{1,0},{2,1},{3,2},{4,3},{5,4},{6,5},{7,6},{8,7},{9,8},{10,9},{11,1... | collective-permute-start | bytes 147464 | tf_op jit(solution)/shard_map/ppermute | solution.py:521
  83.1 5.2 %collective-permute-start.7 = (f32[48,256]{1,0:T(8,128)S(1)}, f32[48,256]{1,0:T(8,128)S(1)}, u32[]{:S(2)}, u32[]{:S(2)}) collective-permute-start(f32[48,256]{1,0:T(8,128)S(1)} %get-tuple-element.37), channel_id=1, source_target_pairs={{0,1},{1,2},{2,3},{3,4},{4,5},{5,6},{6,7},{7,8},{8,9},{9,10},{10,1... | collective-permute-start | bytes 147464 | tf_op jit(solution)/shard_map/ppermute | solution.py:521

commit v3 on v2

--- a/solution.py
+++ b/solution.py
@@ -152,9 +152,18 @@
 
 
 def pack_kernel(
-    group, owner_ref, rows_ref, right_ref, block_ref, mobility_ref, trans_ref, mask_ref, cell_ref,
-    columns_ref, up_ref, down_ref, field_ref,
+    group, owner_ref, rows_hbm, right_hbm, block_hbm, mobility_hbm, trans_hbm, mask_hbm, cell_hbm,
+    columns_ref, up_ref, down_ref,
+    field_ref, rows_ref, right_ref, block_ref, mobility_ref, trans_ref, mask_ref, cell_ref, sems,
 ):
+    pairs = (
+        (rows_hbm, rows_ref), (block_hbm, block_ref), (right_hbm, right_ref), (mobility_hbm, mobility_ref),
+        (trans_hbm, trans_ref), (mask_hbm, mask_ref), (cell_hbm, cell_ref),
+    )
+    copies = [pltpu.make_async_copy(a, b, sems.at[i]) for i, (a, b) in enumerate(pairs)]
+    for copy in copies:
+        copy.start()
+    copies[0].wait()
     lane = lax.broadcasted_iota(jnp.int32, (NC // 2, 128), 1)
     owner = jnp.full((8, 128), owner_ref[0, 0], jnp.int32).astype(F32)
     for pair in range(group // 2):
@@ -164,6 +173,8 @@
             block = flipped[NC * odd : NC * odd + NC]
             columns_ref[2 * pair + odd, : NC // 2, :] = jnp.where(lane < NC, block[: NC // 2], block[NC // 2 :])
             columns_ref[2 * pair + odd, NC // 2 :, :] = owner
+    for copy in copies[1:]:
+        copy.wait()
     for out_ref in (up_ref, down_ref):
         out_ref[8 * Y_TILES - 4 :, :] = jnp.zeros((4, 256), F32)
     for half in range(2):
@@ -503,14 +514,14 @@
             out_ref[c, place] = c1 * z1_ref[c, place] + c2 * z2_ref[c, place]
 
 
-def call(kernel, outs, scratch, *args, smem=0):
+def call(kernel, outs, scratch, *args, smem=0, space=pltpu.VMEM):
     vmem = pl.BlockSpec(memory_space=pltpu.VMEM)
     return pl.pallas_call(
         kernel,
         out_shape=[jax.ShapeDtypeStruct(shape, F32) for shape in outs],
-        in_specs=[pl.BlockSpec(memory_space=pltpu.SMEM)] * smem + [vmem] * (len(args) - smem),
+        in_specs=[pl.BlockSpec(memory_space=pltpu.SMEM)] * smem + [pl.BlockSpec(memory_space=space)] * (len(args) - smem),
         out_specs=[vmem] * len(outs),
-        scratch_shapes=[pltpu.VMEM(shape, F32) for shape in scratch],
+        scratch_shapes=[pltpu.VMEM(shape, F32) if isinstance(shape, tuple) else shape for shape in scratch],
         compiler_params=pltpu.CompilerParams(vmem_limit_bytes=40 * 2**20),
     )(*args)
 
@@ -531,9 +542,11 @@
     columns, up, down = call(
         functools.partial(pack_kernel, group),
         [(group, 40, 128), (8 * Y_TILES, 256), (8 * Y_TILES, 256)],
-        [(ROWS, 256)],
-        coarse_owner, coarse_rows, *local,
-        smem=1,
+        [(ROWS, 256), coarse_rows.shape]
+        + [pltpu.VMEM(arg.shape, arg.dtype) for arg in local]
+        + [pltpu.SemaphoreType.DMA((7,))],
+        coarse_owner, *[pltpu.with_memory_space_constraint(arg, pltpu.HBM) for arg in (coarse_rows, *local)],
+        smem=1, space=pltpu.HBM,
     )
     columns = lax.all_to_all(columns, "gy", 0, 0)
     y_previous, y_next = send(up, "gy", 1), send(down, "gy", -1)

time: 135 us -> 129 us (0.956)
  local copies, waits for them, and re-layouts: 6.13 us -> 0.03 us
    unnamed x26 -> x12, local copies, waits for them, and re-layouts: 6.13 us -> 0.03 us
where the time goes in v3:
time: 129 us
  blocking collectives  55.6 us (43%)
  starting transfers between devices  47.3 us (37%)
  waiting for transfers between devices  18.6 us (14%)
  Pallas kernels  6.37 us (5%)
    ppermute x8, starting transfers between devices, send(): return lax.ppermute(values, axis, pairs)  28 us
    all_to_all x1, blocking collectives, on_device(): sums = lax.all_to_all(sums, 'gx', 0, 0)  23.9 us
    all_to_all x1, blocking collectives, on_device(): sums = lax.all_to_all(sums, 'gy', 0, 0)  16.6 us
    all_to_all x1, starting transfers between devices, on_device(): columns = lax.all_to_all(columns, 'gy', 0, 0)  15.8 us
    ppermute x8, waiting for transfers between devices, send(): return lax.ppermute(values, axis, pairs)  15.5 us
    all_to_all x1, blocking collectives, on_device(): slots = lax.all_to_all(slots, 'gy', 0, 0)  15 us
    pallas_call x8, Pallas kernels, call(): pl.pallas_call(kernel, out_shape=[jax.ShapeDtypeStruct(shape, F32) for sh...  6.37 us
    all_to_all x1, starting transfers between devices, on_device(): slots = lax.all_to_all(slots, 'gy', 0, 0)  3.5 us
  transfers between devices with their start and end apart: 10, of which 6 were waited for; matrix products, arithmetic and copies ran while one was open for 0% of the time, Pallas kernels for 0%

profile of v3, /device:TPU:1, one launch (start us, length us, event | category | flops | bytes accessed | tf_op | source)
XLA Modules:
  0.0 128.8 jit_solution(7621222735921785644)
XLA Ops:
  0.7 2.0 %shard_map.82 = (f32[12,40,128]{2,1,0:T(8,128)}, f32[184,256]{1,0:T(8,128)S(1)}, f32[184,256]{1,0:T(8,128)S(1)}) custom-call(s32[1,1]{1,0:T(1,128)S(6)} %copy.9.owner_ref, f32[64,768]{1,0:T(8,128)} %rows_hbm.1, f32[3,4,8,256]{3,2,1,0:T(8,128)} %right_ref.5, f32[3,3,4,8,256]{4,3,2,1,0:T(8,128)} %block_ref.5, f32[3,4,8,256]{3,2,1,0:T(8,128)} %mobility_ref.5, ...), custom_call_target="tpu_custom_call" | custom-call | tf_op jit(solution)/shard_map/pallas_call | solution.py:519
  2.7 0.0 copy-start
  2.7 0.0 copy-start.1
  2.7 15.8 %all-to-all-start = ((f32[12,40,128]{2,1,0:T(8,128)}), f32[12,40,128]{2,1,0:T(8,128)S(1)}, u32[]{:S(2)}, u32[]{:S(2)}) async-start(f32[12,40,128]{2,1,0:T(8,128)} %get-tuple-element.23), calls=%async_computation | async-start | bytes 491520 | tf_op jit(solution)/shard_map/all_to_all | solution.py:551
  18.6 1.3 %collective-permute-start = (f32[184,256]{1,0:T(8,128)S(1)}, f32[184,256]{1,0:T(8,128)S(1)}, u32[]{:S(2)}, u32[]{:S(2)}) collective-permute-start(f32[184,256]{1,0:T(8,128)S(1)} %get-tuple-element.24), channel_id=1, source_target_pairs={{1,0},{2,1},{3,2},{4,3},{5,4},{6,5},{7,6},{8,7},{9,8},{10,9},{11,1... | collective-permute-start | bytes 565256 | tf_op jit(solution)/shard_map/ppermute | solution.py:532
  19.9 4.0 %collective-permute-start.1 = (f32[184,256]{1,0:T(8,128)S(1)}, f32[184,256]{1,0:T(8,128)S(1)}, u32[]{:S(2)}, u32[]{:S(2)}) collective-permute-start(f32[184,256]{1,0:T(8,128)S(1)} %get-tuple-element.25), channel_id=1, source_target_pairs={{0,1},{1,2},{2,3},{3,4},{4,5},{5,6},{6,7},{7,8},{8,9},{9,10},{10,1... | collective-permute-start | bytes 565256 | tf_op jit(solution)/shard_map/ppermute | solution.py:532
  23.9 8.2 %collective-permute-done.yn_ref = f32[184,256]{1,0:T(8,128)S(1)} collective-permute-done((f32[184,256]{1,0:T(8,128)S(1)}, f32[184,256]{1,0:T(8,128)S(1)}, u32[]{:S(2)}, u32[]{:S(2)}) %collective-permute-start) | collective-permute-done | bytes 188448 | tf_op jit(solution)/shard_map/ppermute | solution.py:532
  32.1 0.0 collective-permute-done.1.yp_ref
  32.1 0.0 all-to-all-done.columns_ref
  32.2 0.5 shard_map.83
  32.7 6.4 %collective-permute-start.2 = (f32[392,256]{1,0:T(8,128)S(1)}, f32[392,256]{1,0:T(8,128)S(1)}, u32[]{:S(2)}, u32[]{:S(2)}) collective-permute-start(f32[392,256]{1,0:T(8,128)S(1)} %get-tuple-element.26), channel_id=1, source_target_pairs={{12,0},{24,12},{36,24},{48,36},{60,48},{72,60},{84,72},{96,84},{10... | collective-permute-start | bytes 1204232 | tf_op jit(solution)/shard_map/ppermute | solution.py:532
  39.1 3.1 %collective-permute-start.3 = (f32[392,256]{1,0:T(8,128)S(1)}, f32[392,256]{1,0:T(8,128)S(1)}, u32[]{:S(2)}, u32[]{:S(2)}) collective-permute-start(f32[392,256]{1,0:T(8,128)S(1)} %get-tuple-element.27), channel_id=1, source_target_pairs={{0,12},{12,24},{24,36},{36,48},{48,60},{60,72},{72,84},{84,96},{96... | collective-permute-start | bytes 1204232 | tf_op jit(solution)/shard_map/ppermute | solution.py:532
  42.2 3.6 %collective-permute-done.2.xn_ref = f32[392,256]{1,0:T(8,128)S(1)} collective-permute-done((f32[392,256]{1,0:T(8,128)S(1)}, f32[392,256]{1,0:T(8,128)S(1)}, u32[]{:S(2)}, u32[]{:S(2)}) %collective-permute-start.2) | collective-permute-done | bytes 401440 | tf_op jit(solution)/shard_map/ppermute | solution.py:532
  45.8 1.2 collective-permute-done.3.xp_ref
  47.0 15.0 %all_to_all.25.slots_ref = f32[12,8,128]{2,1,0:T(8,128)S(1)} all-to-all(f32[12,8,128]{2,1,0:T(8,128)S(1)} %shard_map.84), channel_id=1, replica_groups=mesh['gx'=64,'gy'=12] {'gy'}, dimensions={0} | all-to-all | bytes 98304 | tf_op jit(solution)/shard_map/all_to_all | solution.py:566
  62.0 1.3 %shard_map.85 = (f32[3,4,8,256]{3,2,1,0:T(8,128)S(1)}, f32[3,4,8,256]{3,2,1,0:T(8,128)S(1)}, f32[64,256]{1,0:T(8,128)S(1)}, f32[64,256]{1,0:T(8,128)S(1)}, f32[1...) custom-call(f32[3,4,8,256]{3,2,1,0:T(8,128)S(1)} %copy-done.2, ...), custom_call_target="tpu_custom_call" | custom-call | tf_op jit(solution)/shard_map/pallas_call | solution.py:519
  63.3 1.9 %collective-permute-start.4 = (f32[64,256]{1,0:T(8,128)S(1)}, f32[64,256]{1,0:T(8,128)S(1)}, u32[]{:S(2)}, u32[]{:S(2)}) collective-permute-start(f32[64,256]{1,0:T(8,128)S(1)} %get-tuple-element.32), channel_id=1, source_target_pairs={{12,0},{24,12},{36,24},{48,36},{60,48},{72,60},{84,72},{96,84},{10... | collective-permute-start | bytes 196616 | tf_op jit(solution)/shard_map/ppermute | solution.py:532
  65.3 6.0 %collective-permute-start.5 = (f32[64,256]{1,0:T(8,128)S(1)}, f32[64,256]{1,0:T(8,128)S(1)}, u32[]{:S(2)}, u32[]{:S(2)}) collective-permute-start(f32[64,256]{1,0:T(8,128)S(1)} %get-tuple-element.33), channel_id=1, source_target_pairs={{0,12},{12,24},{24,36},{36,48},{48,60},{60,72},{72,84},{84,96},{96... | collective-permute-start | bytes 196616 | tf_op jit(solution)/shard_map/ppermute | solution.py:532
  71.3 0.0 collective-permute-done.4.next_ref.xn2_ref
  71.3 1.3 %collective-permute-done.5.previous_ref.xp2_ref = f32[64,256]{1,0:T(8,128)S(1)} collective-permute-done((f32[64,256]{1,0:T(8,128)S(1)}, f32[64,256]{1,0:T(8,128)S(1)}, u32[]{:S(2)}, u32[]{:S(2)}) %collective-permute-start.5) | collective-permute-done | bytes 65568 | tf_op jit(solution)/shard_map/ppermute | solution.py:532
  72.6 0.7 shard_map.86
  73.2 3.5 %all-to-all-start.2 = ((f32[12,8,128]{2,1,0:T(8,128)}), f32[12,8,128]{2,1,0:T(8,128)S(1)}, u32[]{:S(2)}, u32[]{:S(2)}) async-start(f32[12,8,128]{2,1,0:T(8,128)} %get-tuple-element.34), calls=%async_computation.2 | async-start | bytes 98304 | tf_op jit(solution)/shard_map/all_to_all | solution.py:582
  76.8 1.3 %collective-permute-start.6 = (f32[48,256]{1,0:T(8,128)S(1)}, f32[48,256]{1,0:T(8,128)S(1)}, u32[]{:S(2)}, u32[]{:S(2)}) collective-permute-start(f32[48,256]{1,0:T(8,128)S(1)} %get-tuple-element.36), channel_id=1, source_target_pairs={{1,0},{2,1},{3,2},{4,3},{5,4},{6,5},{7,6},{8,7},{9,8},{10,9},{11,1... | collective-permute-start | bytes 147464 | tf_op jit(solution)/shard_map/ppermute | solution.py:532
  78.1 4.0 %collective-permute-start.7 = (f32[48,256]{1,0:T(8,128)S(1)}, f32[48,256]{1,0:T(8,128)S(1)}, u32[]{:S(2)}, u32[]{:S(2)}) collective-permute-start(f32[48,256]{1,0:T(8,128)S(1)} %get-tuple-element.37), channel_id=1, source_target_pairs={{0,1},{1,2},{2,3},{3,4},{4,5},{5,6},{6,7},{7,8},{8,9},{9,10},{10,1... | collective-permute-start | bytes 147464 | tf_op jit(solution)/shard_map/ppermute | solution.py:532
  82.0 0.0 collective-permute-done.6.yn2_ref
  82.1 1.1 collective-permute-done.7.yp2_ref
  83.2 3.2 %all-to-all-done.2.slots_ref = f32[12,8,128]{2,1,0:T(8,128)S(1)} async-done(((f32[12,8,128]{2,1,0:T(8,128)}), f32[12,8,128]{2,1,0:T(8,128)S(1)}, u32[]{:S(2)}, u32[]{:S(2)}) %all-to-all-start.2) | async-done | bytes 49184 | tf_op jit(solution)/shard_map/all_to_all | solution.py:582
  86.4 0.9 shard_map.87
  87.3 23.9 %all_to_all.26.parts_ref = f32[64,1,128]{2,1,0:T(1,128)S(1)} all-to-all(f32[64,1,128]{2,1,0:T(1,128)S(1)} %get-tuple-element.38), channel_id=1, replica_groups=mesh['gx'=64,'gy'=12] {'gx'}, dimensions={0} | all-to-all | bytes 65536 | tf_op jit(solution)/shard_map/all_to_all | solution.py:590
  111.2 0.1 shard_map.88
  111.3 16.6 %all_to_all.27.parts_ref = f32[12,1,128]{2,1,0:T(1,128)S(1)} all-to-all(f32[12,1,128]{2,1,0:T(1,128)S(1)} %shard_map.88), channel_id=1, replica_groups=mesh['gx'=64,'gy'=12] {'gy'}, dimensions={0} | all-to-all | bytes 12288 | tf_op jit(solution)/shard_map/all_to_all | solution.py:592
  127.9 0.9 shard_map.89
  (13 shorter events, 0.0 us)
Async XLA Ops:
  0.7 31.5 %copy-start.2 = (f32[3,4,8,256]{3,2,1,0:T(8,128)S(1)}, f32[3,4,8,256]{3,2,1,0:T(8,128)}, u32[]{:S(2)}) copy-start(f32[3,4,8,256]{3,2,1,0:T(8,128)} %right_ref.5) | copy-start | bytes 294916
  0.7 31.5 %copy-start.3 = (f32[3,4,8,256]{3,2,1,0:T(8,128)S(1)}, f32[3,4,8,256]{3,2,1,0:T(8,128)}, u32[]{:S(2)}) copy-start(f32[3,4,8,256]{3,2,1,0:T(8,128)} %mobility_ref.5) | copy-start | bytes 294916
  0.7 31.5 %copy-start.4 = (s32[4,8,256]{2,1,0:T(8,128)S(1)}, s32[4,8,256]{2,1,0:T(8,128)}, u32[]{:S(2)}) copy-start(s32[4,8,256]{2,1,0:T(8,128)} %mask_ref.5) | copy-start | bytes 98308
  0.7 31.5 %copy-start.5 = (s32[4,8,256]{2,1,0:T(8,128)S(1)}, s32[4,8,256]{2,1,0:T(8,128)}, u32[]{:S(2)}) copy-start(s32[4,8,256]{2,1,0:T(8,128)} %cell_ref.5) | copy-start | bytes 98308
  2.7 29.5 %copy-start = (f32[3,3,4,8,256]{4,3,2,1,0:T(8,128)S(1)}, f32[3,3,4,8,256]{4,3,2,1,0:T(8,128)}, u32[]{:S(2)}) copy-start(f32[3,3,4,8,256]{4,3,2,1,0:T(8,128)} %block_ref.5) | copy-start | bytes 884740
  2.7 29.5 %copy-start.1 = (f32[6,4,8,256]{3,2,1,0:T(8,128)S(1)}, f32[6,4,8,256]{3,2,1,0:T(8,128)}, u32[]{:S(2)}) copy-start(f32[6,4,8,256]{3,2,1,0:T(8,128)} %trans_ref.5) | copy-start | bytes 589828
  2.7 29.4 %all-to-all-start = ((f32[12,40,128]{2,1,0:T(8,128)}), f32[12,40,128]{2,1,0:T(8,128)S(1)}, u32[]{:S(2)}, u32[]{:S(2)}) async-start(f32[12,40,128]{2,1,0:T(8,128)} %get-tuple-element.23), calls=%async_computation | async-start | bytes 491520 | tf_op jit(solution)/shard_map/all_to_all | solution.py:551
  18.6 13.5 %collective-permute-start = (f32[184,256]{1,0:T(8,128)S(1)}, f32[184,256]{1,0:T(8,128)S(1)}, u32[]{:S(2)}, u32[]{:S(2)}) collective-permute-start(f32[184,256]{1,0:T(8,128)S(1)} %get-tuple-element.24), channel_id=1, source_target_pairs={{1,0},{2,1},{3,2},{4,3},{5,4},{6,5},{7,6},{8,7},{9,8},{10,9},{11,1... | collective-permute-start | bytes 565256 | tf_op jit(solution)/shard_map/ppermute | solution.py:532
  19.9 12.2 %collective-permute-start.1 = (f32[184,256]{1,0:T(8,128)S(1)}, f32[184,256]{1,0:T(8,128)S(1)}, u32[]{:S(2)}, u32[]{:S(2)}) collective-permute-start(f32[184,256]{1,0:T(8,128)S(1)} %get-tuple-element.25), channel_id=1, source_target_pairs={{0,1},{1,2},{2,3},{3,4},{4,5},{5,6},{6,7},{7,8},{8,9},{9,10},{10,1... | collective-permute-start | bytes 565256 | tf_op jit(solution)/shard_map/ppermute | solution.py:532
  32.7 13.1 %collective-permute-start.2 = (f32[392,256]{1,0:T(8,128)S(1)}, f32[392,256]{1,0:T(8,128)S(1)}, u32[]{:S(2)}, u32[]{:S(2)}) collective-permute-start(f32[392,256]{1,0:T(8,128)S(1)} %get-tuple-element.26), channel_id=1, source_target_pairs={{12,0},{24,12},{36,24},{48,36},{60,48},{72,60},{84,72},{96,84},{10... | collective-permute-start | bytes 1204232 | tf_op jit(solution)/shard_map/ppermute | solution.py:532
  39.1 7.9 %collective-permute-start.3 = (f32[392,256]{1,0:T(8,128)S(1)}, f32[392,256]{1,0:T(8,128)S(1)}, u32[]{:S(2)}, u32[]{:S(2)}) collective-permute-start(f32[392,256]{1,0:T(8,128)S(1)} %get-tuple-element.27), channel_id=1, source_target_pairs={{0,12},{12,24},{24,36},{36,48},{48,60},{60,72},{72,84},{84,96},{96... | collective-permute-start | bytes 1204232 | tf_op jit(solution)/shard_map/ppermute | solution.py:532
  63.3 7.9 %collective-permute-start.4 = (f32[64,256]{1,0:T(8,128)S(1)}, f32[64,256]{1,0:T(8,128)S(1)}, u32[]{:S(2)}, u32[]{:S(2)}) collective-permute-start(f32[64,256]{1,0:T(8,128)S(1)} %get-tuple-element.32), channel_id=1, source_target_pairs={{12,0},{24,12},{36,24},{48,36},{60,48},{72,60},{84,72},{96,84},{10... | collective-permute-start | bytes 196616 | tf_op jit(solution)/shard_map/ppermute | solution.py:532
  65.3 7.3 %collective-permute-start.5 = (f32[64,256]{1,0:T(8,128)S(1)}, f32[64,256]{1,0:T(8,128)S(1)}, u32[]{:S(2)}, u32[]{:S(2)}) collective-permute-start(f32[64,256]{1,0:T(8,128)S(1)} %get-tuple-element.33), channel_id=1, source_target_pairs={{0,12},{12,24},{24,36},{36,48},{48,60},{60,72},{72,84},{84,96},{96... | collective-permute-start | bytes 196616 | tf_op jit(solution)/shard_map/ppermute | solution.py:532
  73.2 13.1 %all-to-all-start.2 = ((f32[12,8,128]{2,1,0:T(8,128)}), f32[12,8,128]{2,1,0:T(8,128)S(1)}, u32[]{:S(2)}, u32[]{:S(2)}) async-start(f32[12,8,128]{2,1,0:T(8,128)} %get-tuple-element.34), calls=%async_computation.2 | async-start | bytes 98304 | tf_op jit(solution)/shard_map/all_to_all | solution.py:582
  76.8 5.3 %collective-permute-start.6 = (f32[48,256]{1,0:T(8,128)S(1)}, f32[48,256]{1,0:T(8,128)S(1)}, u32[]{:S(2)}, u32[]{:S(2)}) collective-permute-start(f32[48,256]{1,0:T(8,128)S(1)} %get-tuple-element.36), channel_id=1, source_target_pairs={{1,0},{2,1},{3,2},{4,3},{5,4},{6,5},{7,6},{8,7},{9,8},{10,9},{11,1... | collective-permute-start | bytes 147464 | tf_op jit(solution)/shard_map/ppermute | solution.py:532
  78.1 5.2 %collective-permute-start.7 = (f32[48,256]{1,0:T(8,128)S(1)}, f32[48,256]{1,0:T(8,128)S(1)}, u32[]{:S(2)}, u32[]{:S(2)}) collective-permute-start(f32[48,256]{1,0:T(8,128)S(1)} %get-tuple-element.37), channel_id=1, source_target_pairs={{0,1},{1,2},{2,3},{3,4},{4,5},{5,6},{6,7},{7,8},{8,9},{9,10},{10,1... | collective-permute-start | bytes 147464 | tf_op jit(solution)/shard_map/ppermute | solution.py:532

commit v4 on v3

--- a/solution.py
+++ b/solution.py
@@ -13,8 +13,9 @@
 ROWS = 8
 NC = 64
 
-X_FIELD, X_VEM, X_CORNER, X_CELL13, X_CELL2, X_COARSE, X_TILES = 4, 28, 37, 45, 46, 47, 49
-Y_FIELD, Y_VEM, Y_TILES = 2, 18, 23
+X_FIELD, X_VEM, X_TILES = 4, 28, 37
+C_CELL13, C_CELL2, C_COARSE, C_TILES = 8, 9, 10, 12
+Y_FIELD, Y_LAST, Y_TILES = 2, 18, 19
 X2_S, X2_COARSE, X2_TILES = 3, 6, 8
 Y2_V, Y2_TILES = 4, 6
 Y2_PLACES = (0, 1, 2, 3, 4, 5, 10, 11)
@@ -153,7 +154,7 @@
 
 def pack_kernel(
     group, owner_ref, rows_hbm, right_hbm, block_hbm, mobility_hbm, trans_hbm, mask_hbm, cell_hbm,
-    columns_ref, up_ref, down_ref,
+    columns_ref, up_ref, down_ref, fore_ref, back_ref,
     field_ref, rows_ref, right_ref, block_ref, mobility_ref, trans_ref, mask_ref, cell_ref, sems,
 ):
     pairs = (
@@ -178,7 +179,7 @@
     for out_ref in (up_ref, down_ref):
         out_ref[8 * Y_TILES - 4 :, :] = jnp.zeros((4, 256), F32)
     for half in range(2):
-        cells, fields = [], []
+        cells, fields, edges = [], [], []
         for place in (2 * half, 2 * half + 1):
             own = Own(place, block_ref, mobility_ref, mask_ref)
             cells.append(cell_code(place, mask_ref, cell_ref))
@@ -188,15 +189,26 @@
                 + [own.kappa(), own.scale * (right[0] + right[1] + right[2])]
             )
             vem = [own.mask * v for v in own.solve(right)] + own.of_pressure() + own.of_flux()
-            for f in range(9):
-                field_ref[...] = vem[f]
-                spot = 8 * Y_VEM + 4 * f + place
-                up_ref[spot : spot + 1, :] = field_ref[7:8, :]
-                down_ref[spot : spot + 1, :] = field_ref[0:1, :]
+            for out_ref, distance in ((fore_ref, 4 - place), (back_ref, place + 1)):
+                put(out_ref, distance - 1, cells[-1])
+                if distance < 4:
+                    for k in range(8):
+                        put(out_ref, X_FIELD + 3 * k + distance - 1, fields[-1][k])
+                if distance == 1:
+                    for f in range(9):
+                        put(out_ref, X_VEM + f, vem[f])
+            edges.append(vem)
         for out_ref, to_next in ((up_ref, True), (down_ref, False)):
             put(out_ref, half, paired(cells, to_next))
+            free = row_index() % 4 == (0 if to_next else 3)
             for k in range(8):
-                put(out_ref, Y_FIELD + 2 * k + half, paired([fields[0][k], fields[1][k]], to_next))
+                edge = [turned(edges[0][k], 1 if to_next else 3), turned(edges[1][k], 5 if to_next else 7)]
+                both = jnp.where(row_index() < 4, edge[0], edge[1])
+                put(out_ref, Y_FIELD + 2 * k + half, jnp.where(free, both, paired([fields[0][k], fields[1][k]], to_next)))
+            for i in range(2):
+                field_ref[...] = edges[i][8]
+                spot = 8 * Y_LAST + 2 * half + i
+                out_ref[spot : spot + 1, :] = field_ref[7:8, :] if to_next else field_ref[0:1, :]
 
 
 def y_halo(next_ref, previous_ref, index, place):
@@ -205,41 +217,23 @@
 
 
 def sides_kernel(
-    group, right_ref, block_ref, mobility_ref, trans_ref, mask_ref, cell_ref, columns_ref, yn_ref, yp_ref,
+    group, right_ref, cell_ref, columns_ref, yn_ref, yp_ref,
     fore_ref, back_ref, terms_ref, scratch_ref,
 ):
     row = row_index()
     middle = (row == 3) | (row == 4)
-    outs = (fore_ref, lambda d: 4 - d), (back_ref, lambda d: d - 1)
-    for place in range(XO):
-        own = Own(place, block_ref, mobility_ref, mask_ref)
-        right = [right_ref[c, place] for c in range(3)]
-        cells = cell_code(place, mask_ref, cell_ref)
-        kappa, source = own.kappa(), own.scale * (right[0] + right[1] + right[2])
-        for out_ref, at in outs:
-            distance = next(d for d in range(1, 5) if at(d) == place)
-            put(out_ref, distance - 1, cells)
-            if distance < 4:
-                for k in range(8):
-                    value = trans_ref[k, place] if k < 6 else (kappa if k == 6 else source)
-                    put(out_ref, X_FIELD + 3 * k + distance - 1, value)
-            if distance == 1:
-                vem = [own.mask * v for v in own.solve(right)] + own.of_pressure() + own.of_flux()
-                for f in range(9):
-                    put(out_ref, X_VEM + f, vem[f])
-    for out_ref, at in outs:
-        for k in range(8):
-            near, far = [y_halo(yn_ref, yp_ref, Y_FIELD + 2 * k, at(d)) for d in (1, 2)]
-            put(out_ref, X_CORNER + k, jnp.where(middle, turned(far, 4), near))
-        near, mid, far = [y_halo(yn_ref, yp_ref, 0, at(d)) for d in (1, 2, 3)]
-        put(out_ref, X_CELL13, jnp.where(middle, turned(far, 4), near))
-        put(out_ref, X_CELL2, mid)
     sums = coarse_sums(cell_ref, lambda i: right_ref[0, i] + right_ref[1, i] + right_ref[2, i])
     terms = coarse_terms(sums, columns_ref, scratch_ref, group)
     terms_ref[...] = terms
-    for out_ref, _ in outs:
-        out_ref[8 * X_COARSE :, :128] = terms
-        out_ref[8 * X_COARSE :, 128:] = jnp.zeros((16, 128), F32)
+    for out_ref, at in ((fore_ref, lambda d: 4 - d), (back_ref, lambda d: d - 1)):
+        for k in range(8):
+            near, far = [y_halo(yn_ref, yp_ref, Y_FIELD + 2 * k, at(d)) for d in (1, 2)]
+            put(out_ref, k, jnp.where(middle, turned(far, 4), near))
+        near, mid, far = [y_halo(yn_ref, yp_ref, 0, at(d)) for d in (1, 2, 3)]
+        put(out_ref, C_CELL13, jnp.where(middle, turned(far, 4), near))
+        put(out_ref, C_CELL2, mid)
+        out_ref[8 * C_COARSE :, :128] = terms
+        out_ref[8 * C_COARSE :, 128:] = jnp.zeros((16, 128), F32)
 
 
 def write_slots(group, slots_ref, three):
@@ -263,7 +257,7 @@
 
 
 def slots_kernel(group, terms_ref, next_ref, previous_ref, slots_ref):
-    write_slots(group, slots_ref, three_groups(terms_ref, next_ref, previous_ref, 0))
+    write_slots(group, slots_ref, three_groups(terms_ref, next_ref, previous_ref, 8 * C_COARSE))
 
 
 def forward_kernel(group, terms_ref, source_ref, solved_ref, next_ref, previous_ref, slots_ref, up_ref, down_ref):
@@ -286,21 +280,23 @@
 
 
 class Fields:
-    def __init__(self, trans_ref, xn_ref, xp_ref, yn_ref, yp_ref, own):
-        self.trans_ref, self.x, self.y, self.own = trans_ref, (xn_ref, xp_ref), (yn_ref, yp_ref), own
-
-    def side(self, place):
-        return (self.x[0], place - 3) if place < 8 else (self.x[1], 12 - place)
+    def __init__(self, trans_ref, xn_ref, xp_ref, cn_ref, cp_ref, yn_ref, yp_ref, own):
+        self.trans_ref, self.own = trans_ref, own
+        self.x, self.corner, self.y = (xn_ref, xp_ref), (cn_ref, cp_ref), (yn_ref, yp_ref)
+
+    def side(self, place, tile):
+        refs = self.corner if tile else self.x
+        return (refs[0], place - 3) if place < 8 else (refs[1], 12 - place)
 
     def field(self, k, place, tile):
         if place < 4:
             if tile:
                 return y_halo(self.y[0], self.y[1], Y_FIELD + 2 * k, place)
             return self.trans_ref[k, place] if k < 6 else self.own(k, place)
-        ref, d = self.side(place)
+        ref, d = self.side(place, tile)
         if tile == 0:
             return get(ref, X_FIELD + 3 * k + d - 1)
-        corner = get(ref, X_CORNER + k)
+        corner = get(ref, k)
         return corner if d == 1 else turned(corner, 4)
 
     def trans(self, face, place, tile):
@@ -309,23 +305,26 @@
     def cells(self, place, tile, own_cells):
         if place < 4:
             return y_halo(self.y[0], self.y[1], 0, place) if tile else own_cells(place)
-        ref, d = self.side(place)
+        ref, d = self.side(place, tile)
         if tile == 0:
             return get(ref, d - 1)
         if d == 2:
-            return get(ref, X_CELL2)
-        corner = get(ref, X_CELL13)
+            return get(ref, C_CELL2)
+        corner = get(ref, C_CELL13)
         return corner if d == 1 else turned(corner, 4)
 
     def vem(self, f, place, tile):
         if tile == 0:
             return get(self.x[0] if place == 4 else self.x[1], X_VEM + f)
-        return edge_rows(self.y[0], self.y[1], 8 * Y_VEM + 4 * f + place)
-
-
-def edge_rows(next_ref, previous_ref, spot):
-    after = jnp.broadcast_to(next_ref[spot : spot + 1, :], (ROWS, 256))
-    before = jnp.broadcast_to(previous_ref[spot : spot + 1, :], (ROWS, 256))
+        if f == 8:
+            return edge_rows(self.y[0], self.y[1], 8 * Y_LAST + place, 8 * Y_LAST + place)
+        spot = 8 * (Y_FIELD + 2 * f + place // 2) + 4 * (place % 2)
+        return edge_rows(self.y[0], self.y[1], spot + 3, spot)
+
+
+def edge_rows(next_ref, previous_ref, next_spot, previous_spot):
+    after = jnp.broadcast_to(next_ref[next_spot : next_spot + 1, :], (ROWS, 256))
+    before = jnp.broadcast_to(previous_ref[previous_spot : previous_spot + 1, :], (ROWS, 256))
     return jnp.where(row_index() < 4, after, before)
 
 
@@ -398,7 +397,7 @@
 
 def first_kernel(
     group, right_ref, block_ref, mobility_ref, trans_ref, mask_ref, cell_ref, columns_ref,
-    xn_ref, xp_ref, yn_ref, yp_ref, slots_ref,
+    xn_ref, xp_ref, cn_ref, cp_ref, yn_ref, yp_ref, slots_ref,
     zo_ref, w_ref, fore_ref, back_ref, terms_ref, source_ref, solved_ref,
     p_ref, q_ref, z_ref, scratch_ref, kappa_ref,
 ):
@@ -417,7 +416,7 @@
         for c in range(3):
             solved_ref[c, place] = v[c]
     fields = Fields(
-        trans_ref, xn_ref, xp_ref, yn_ref, yp_ref,
+        trans_ref, xn_ref, xp_ref, cn_ref, cp_ref, yn_ref, yp_ref,
         lambda k, place: kappa_ref[place] if k == 6 else source_ref[place],
     )
 
@@ -454,7 +453,7 @@
 
 def second_kernel(
     group, right_ref, block_ref, mobility_ref, trans_ref, mask_ref, cell_ref,
-    xn_ref, xp_ref, yn_ref, yp_ref, slots_ref, w1_ref, source_ref, xn2_ref, xp2_ref, yn2_ref, yp2_ref,
+    xn_ref, xp_ref, cn_ref, cp_ref, yn_ref, yp_ref, slots_ref, w1_ref, source_ref, xn2_ref, xp2_ref, yn2_ref, yp2_ref,
     zo_ref, sums_ref,
     w_ref, p_ref, q_ref, z_ref, kappa_ref,
 ):
@@ -463,7 +462,7 @@
 
     for place in range(4):
         kappa_ref[place] = owns(place).kappa()
-    fields = Fields(trans_ref, xn_ref, xp_ref, yn_ref, yp_ref, lambda k, place: kappa_ref[place])
+    fields = Fields(trans_ref, xn_ref, xp_ref, cn_ref, cp_ref, yn_ref, yp_ref, lambda k, place: kappa_ref[place])
 
     def source(place, tile):
         if tile:
@@ -475,7 +474,8 @@
 
     def solved(place, tile):
         if tile:
-            return [edge_rows(yn2_ref, yp2_ref, 8 * Y2_V + 4 * c + place) for c in range(3)]
+            spots = [8 * Y2_V + 4 * c + place for c in range(3)]
+            return [edge_rows(yn2_ref, yp2_ref, spot, spot) for spot in spots]
         if place < 4:
             return owns(place).solve([w1_ref[c, place] for c in range(3)])
         return [get(xn2_ref if place == 4 else xp2_ref, c) for c in range(3)]
@@ -514,22 +514,97 @@
             out_ref[c, place] = c1 * z1_ref[c, place] + c2 * z2_ref[c, place]
 
 
+class Sent:
+    def __init__(self, axis, tiles, swap=False):
+        self.axis, self.shape, self.swap = axis, (8 * tiles, 256), swap
+
+    def exchanged(self, pair):
+        count = lax.axis_size(self.axis)
+        if self.swap:
+            links = [[(i, i + 1) for i in range(start, count - 1, 2)] for start in (1, 0)]
+            links = [way + [(j, i) for i, j in way] for way in links]
+            second = lax.ppermute(pair[1], self.axis, links[1])
+            first = lax.ppermute(pair[0], self.axis, links[0])
+            return Received(self.axis, (first, second), True)
+        from_previous = lax.ppermute(pair[0], self.axis, [(i, i + 1) for i in range(count - 1)])
+        from_next = lax.ppermute(pair[1], self.axis, [(i + 1, i) for i in range(count - 1)])
+        return Received(self.axis, (from_next, from_previous), False)
+
+
+class Received:
+    def __init__(self, axis, pair, swap):
+        self.axis, self.pair, self.swap = axis, pair, swap
+
+
+def copied(axis, even, odd):
+    def body(pairs):
+        def copy():
+            for from_ref, to_ref in pairs:
+                to_ref[...] = from_ref[...]
+
+        return copy
+
+    is_odd = lax.axis_index(axis) % 2
+    pl.when(is_odd == 1)(body(odd))
+    pl.when(is_odd == 0)(body(even))
+
+
 def call(kernel, outs, scratch, *args, smem=0, space=pltpu.VMEM):
     vmem = pl.BlockSpec(memory_space=pltpu.VMEM)
-    return pl.pallas_call(
-        kernel,
-        out_shape=[jax.ShapeDtypeStruct(shape, F32) for shape in outs],
-        in_specs=[pl.BlockSpec(memory_space=pltpu.SMEM)] * smem + [pl.BlockSpec(memory_space=space)] * (len(args) - smem),
-        out_specs=[vmem] * len(outs),
-        scratch_shapes=[pltpu.VMEM(shape, F32) if isinstance(shape, tuple) else shape for shape in scratch],
-        compiler_params=pltpu.CompilerParams(vmem_limit_bytes=40 * 2**20),
-    )(*args)
-
-
-def send(values, axis, step):
-    count = lax.axis_size(axis)
-    pairs = [(i, i + step) for i in range(count) if 0 <= i + step < count]
-    return lax.ppermute(values, axis, pairs)
+    flat, specs, shapes, views = [], [], [], []
+    for i, arg in enumerate(args):
+        parts = arg.pair if isinstance(arg, Received) else [arg]
+        flat += parts
+        specs += [pl.BlockSpec(memory_space=pltpu.SMEM if i < smem else space)] * len(parts)
+        if isinstance(arg, Received) and arg.swap:
+            views += [arg.pair[0].shape] * 2
+    for out in outs:
+        shapes += [out.shape] * 2 if isinstance(out, Sent) else [out]
+        if isinstance(out, Sent) and out.swap:
+            views += [out.shape] * 2
+
+    def body(*refs):
+        refs = list(refs)
+        ins, results = refs[: len(flat)], refs[len(flat) : len(flat) + len(shapes)]
+        copies = refs[len(flat) + len(shapes) : len(flat) + len(shapes) + len(views)]
+        rest = refs[len(flat) + len(shapes) + len(views) :]
+        seen, after = [], []
+        for arg in args:
+            parts = [ins.pop(0) for _ in range(2 if isinstance(arg, Received) else 1)]
+            if isinstance(arg, Received) and arg.swap:
+                first, second = parts
+                parts = ahead, behind = copies.pop(0), copies.pop(0)
+                copied(arg.axis, [(second, ahead), (first, behind)], [(first, ahead), (second, behind)])
+            seen += parts
+        for out in outs:
+            parts = [results.pop(0) for _ in range(2 if isinstance(out, Sent) else 1)]
+            if isinstance(out, Sent) and out.swap:
+                first, second = parts
+                parts = ahead, behind = copies.pop(0), copies.pop(0)
+                after.append((out.axis, [(ahead, second), (behind, first)], [(ahead, first), (behind, second)]))
+            seen += parts
+        kernel(*seen, *rest)
+        for each in after:
+            copied(*each)
+
+    found = list(
+        pl.pallas_call(
+            body,
+            out_shape=[jax.ShapeDtypeStruct(shape, F32) for shape in shapes],
+            in_specs=specs,
+            out_specs=[vmem] * len(shapes),
+            scratch_shapes=[pltpu.VMEM(shape, F32) for shape in views]
+            + [pltpu.VMEM(shape, F32) if isinstance(shape, tuple) else shape for shape in scratch],
+            compiler_params=pltpu.CompilerParams(vmem_limit_bytes=40 * 2**20),
+        )(*flat)
+    )
+    results = []
+    for out in outs:
+        if isinstance(out, Sent):
+            results.append(out.exchanged([found.pop(0), found.pop(0)]))
+        else:
+            results.append(found.pop(0))
+    return results
 
 
 def on_device(
@@ -539,9 +614,9 @@
     line = lax.axis_size("gx")
     local = (right_side, block_matrix, mobility, trans, active_mask, cell_map)
     field = (3, XO, ROWS, 256)
-    columns, up, down = call(
+    columns, y_halos, x_halos = call(
         functools.partial(pack_kernel, group),
-        [(group, 40, 128), (8 * Y_TILES, 256), (8 * Y_TILES, 256)],
+        [(group, 40, 128), Sent("gy", Y_TILES, True), Sent("gx", X_TILES, True)],
         [(ROWS, 256), coarse_rows.shape]
         + [pltpu.VMEM(arg.shape, arg.dtype) for arg in local]
         + [pltpu.SemaphoreType.DMA((7,))],
@@ -549,43 +624,34 @@
         smem=1, space=pltpu.HBM,
     )
     columns = lax.all_to_all(columns, "gy", 0, 0)
-    y_previous, y_next = send(up, "gy", 1), send(down, "gy", -1)
-    fore, back, terms = call(
+    corners, terms = call(
         functools.partial(sides_kernel, group),
-        [(8 * X_TILES, 256), (8 * X_TILES, 256), (16, 128)],
+        [Sent("gx", C_TILES, True), (16, 128)],
         [(16, 128)],
-        *local, columns, y_next, y_previous,
-    )
-    x_previous, x_next = send(fore, "gx", 1), send(back, "gx", -1)
-    (slots,) = call(
-        functools.partial(slots_kernel, group),
-        [(group, 8, 128)],
-        [],
-        terms, x_next[8 * X_COARSE :], x_previous[8 * X_COARSE :],
-    )
+        right_side, cell_map, columns, y_halos,
+    )
+    (slots,) = call(functools.partial(slots_kernel, group), [(group, 8, 128)], [], terms, corners)
     slots = lax.all_to_all(slots, "gy", 0, 0)
-    halos = (x_next, x_previous, y_next, y_previous)
+    halos = (x_halos, corners, y_halos)
     work = [(24, ROWS, 256), (24, ROWS, 256), (3, 24, ROWS, 256)]
-    first_z, first_w, fore, back, terms, source, solved = call(
+    first_z, first_w, x2_halos, terms, source, solved = call(
         functools.partial(first_kernel, group),
-        [field, field, (8 * X2_TILES, 256), (8 * X2_TILES, 256), (16, 128), (XO, ROWS, 256), field],
+        [field, field, Sent("gx", X2_TILES, True), (16, 128), (XO, ROWS, 256), field],
         work + [(16, 128), (XO, ROWS, 256)],
         *local, columns, *halos, slots,
     )
-    x2_previous, x2_next = send(fore, "gx", 1), send(back, "gx", -1)
-    slots, up, down = call(
+    slots, y2_halos = call(
         functools.partial(forward_kernel, group),
-        [(group, 8, 128), (8 * Y2_TILES, 256), (8 * Y2_TILES, 256)],
+        [(group, 8, 128), Sent("gy", Y2_TILES, True)],
         [],
-        terms, source, solved, x2_next, x2_previous,
+        terms, source, solved, x2_halos,
     )
     slots = lax.all_to_all(slots, "gy", 0, 0)
-    y2_previous, y2_next = send(up, "gy", 1), send(down, "gy", -1)
     second_z, sums = call(
         functools.partial(second_kernel, group),
         [field, (line, 1, 128)],
         [field] + work + [(XO, ROWS, 256)],
-        *local, *halos, slots, first_w, source, x2_next, x2_previous, y2_next, y2_previous,
+        *local, *halos, slots, first_w, source, x2_halos, y2_halos,
     )
     sums = lax.all_to_all(sums, "gx", 0, 0)
     (sums,) = call(regroup_kernel, [(group, 1, 128)], [], sums)

time: 129 us -> 122 us (0.946)
  blocking collectives: 55.6 us -> 37.5 us
  starting transfers between devices: 47.3 us -> 60.6 us
  waiting for transfers between devices: 18.6 us -> 15 us
    all_to_all x1 -> x0, blocking collectives: 15 us -> none  [on_device(): slots = lax.all_to_all(slots, 'gy', 0, 0)]
    ppermute x8 -> x10, waiting for transfers between devices: 15.5 us -> 4.33 us  [the longest x5 3.96 us: exchanged(): second = lax.ppermute(pair[1], self.axis, links[1])]
    ppermute x8 -> x10, starting transfers between devices: 28 us -> 35.8 us  [the longest x5 18.7 us: exchanged(): first = lax.ppermute(pair[0], self.axis, links[0])]
    all_to_all x1 -> x2, waiting for transfers between devices: 3.15 us -> 10.7 us  [on_device(): slots = lax.all_to_all(slots, 'gy', 0, 0)]
    all_to_all x1 -> x2, starting transfers between devices: 3.5 us -> 8.96 us  [on_device(): slots = lax.all_to_all(slots, 'gy', 0, 0)]
    all_to_all x1, blocking collectives: 23.9 us -> 21.8 us  [on_device(): sums = lax.all_to_all(sums, 'gx', 0, 0)]
  transfers between devices with their start and end apart: 10 -> 13, of which waited for: 6 -> 6; matrix products, arithmetic and copies ran while one was open for 0% -> 0% of each run, Pallas kernels for 0% -> 1%
where the time goes in v4:
time: 122 us
  starting transfers between devices  60.6 us (50%)
  blocking collectives  37.5 us (31%)
  waiting for transfers between devices  15 us (12%)
  Pallas kernels  7.4 us (6%)
    all_to_all x1, blocking collectives, on_device(): sums = lax.all_to_all(sums, 'gx', 0, 0)  21.8 us
    ppermute x5, starting transfers between devices, exchanged(): first = lax.ppermute(pair[0], self.axis, links[0])  18.7 us
    ppermute x5, starting transfers between devices, exchanged(): second = lax.ppermute(pair[1], self.axis, links[1])  17.1 us
    all_to_all x1, starting transfers between devices, on_device(): columns = lax.all_to_all(columns, 'gy', 0, 0)  15.8 us
    all_to_all x1, blocking collectives, on_device(): sums = lax.all_to_all(sums, 'gy', 0, 0)  15.7 us
    all_to_all x2, waiting for transfers between devices, on_device(): slots = lax.all_to_all(slots, 'gy', 0, 0)  10.7 us
    all_to_all x2, starting transfers between devices, on_device(): slots = lax.all_to_all(slots, 'gy', 0, 0)  8.96 us
    pallas_call x8, Pallas kernels, call(): pl.pallas_call(body, out_shape=[jax.ShapeDtypeStruct(shape, F32) for shap...  7.4 us
  transfers between devices with their start and end apart: 13, of which 6 were waited for; matrix products, arithmetic and copies ran while one was open for 0% of the time, Pallas kernels for 1%

profile of v4, /device:TPU:1, one launch (start us, length us, event | category | flops | bytes accessed | tf_op | source)
XLA Modules:
  0.0 121.5 jit_solution(18046571647689725241)
XLA Ops:
  0.7 2.3 %shard_map.82 = (f32[12,40,128]{2,1,0:T(8,128)}, f32[152,256]{1,0:T(8,128)S(1)}, f32[152,256]{1,0:T(8,128)S(1)}, f32[296,256]{1,0:T(8,128)S(1)}, f32[296,256]{1,0:T(8,128)S(1)}) custom-call(s32[1,1]{1,0:T(1,128)S(6)} %copy.9.refs_0_, f32[64,768]{1,0:T(8,128)} %refs_1_.4, f32[3,4,8,256]{3,2,1,0:T(8,128)} %refs_0_.6, f32[3,3,4,8,256]{4,3,2,1,0:T(8,128)} %refs_1_.7, ...), custom_call_target="tpu_custom_call" | custom-call | tf_op jit(solution)/shard_map/pallas_call | solution.py:591
  2.9 0.0 copy-start.2
  2.9 0.0 copy-start.4
  2.9 15.8 %all-to-all-start = ((f32[12,40,128]{2,1,0:T(8,128)}), f32[12,40,128]{2,1,0:T(8,128)S(1)}, u32[]{:S(2)}, u32[]{:S(2)}) async-start(f32[12,40,128]{2,1,0:T(8,128)} %get-tuple-element.27), calls=%async_computation | async-start | bytes 491520 | tf_op jit(solution)/shard_map/all_to_all | solution.py:626
  18.8 0.7 collective-permute-start.2
  19.5 5.7 %collective-permute-start.3 = (f32[152,256]{1,0:T(8,128)S(1)}, f32[152,256]{1,0:T(8,128)S(1)}, u32[]{:S(2)}, u32[]{:S(2)}) collective-permute-start(f32[152,256]{1,0:T(8,128)S(1)} %get-tuple-element.29), channel_id=1, source_target_pairs={{0,1},{2,3},{4,5},{6,7},{8,9},{10,11},{1,0},{3,2},{5,4},{7,6},{9,8... | collective-permute-start | bytes 466952 | tf_op jit(solution)/shard_map/ppermute | solution.py:526
  25.2 4.9 %collective-permute-start = (f32[296,256]{1,0:T(8,128)S(1)}, f32[296,256]{1,0:T(8,128)S(1)}, u32[]{:S(2)}, u32[]{:S(2)}) collective-permute-start(f32[296,256]{1,0:T(8,128)S(1)} %get-tuple-element.25), channel_id=1, source_target_pairs={{12,24},{36,48},{60,72},{84,96},{108,120},{132,144},{156,168},{180... | collective-permute-start | bytes 909320 | tf_op jit(solution)/shard_map/ppermute | solution.py:527
  30.1 1.9 %collective-permute-start.1 = (f32[296,256]{1,0:T(8,128)S(1)}, f32[296,256]{1,0:T(8,128)S(1)}, u32[]{:S(2)}, u32[]{:S(2)}) collective-permute-start(f32[296,256]{1,0:T(8,128)S(1)} %get-tuple-element.26), channel_id=1, source_target_pairs={{0,12},{24,36},{48,60},{72,84},{96,108},{120,132},{144,156},{168,1... | collective-permute-start | bytes 909320 | tf_op jit(solution)/shard_map/ppermute | solution.py:526
  32.1 0.5 shard_map.83
  32.6 7.6 %collective-permute-start.4 = (f32[96,256]{1,0:T(8,128)S(1)}, f32[96,256]{1,0:T(8,128)S(1)}, u32[]{:S(2)}, u32[]{:S(2)}) collective-permute-start(f32[96,256]{1,0:T(8,128)S(1)} %get-tuple-element.30), channel_id=1, source_target_pairs={{12,24},{36,48},{60,72},{84,96},{108,120},{132,144},{156,168},{180... | collective-permute-start | bytes 294920 | tf_op jit(solution)/shard_map/ppermute | solution.py:527
  40.3 1.9 %collective-permute-start.5 = (f32[96,256]{1,0:T(8,128)S(1)}, f32[96,256]{1,0:T(8,128)S(1)}, u32[]{:S(2)}, u32[]{:S(2)}) collective-permute-start(f32[96,256]{1,0:T(8,128)S(1)} %get-tuple-element.31), channel_id=1, source_target_pairs={{0,12},{24,36},{48,60},{72,84},{96,108},{120,132},{144,156},{168,1... | collective-permute-start | bytes 294920 | tf_op jit(solution)/shard_map/ppermute | solution.py:526
  42.2 0.4 collective-permute-done.4.refs_1_.refs_9_.refs_8_
  42.5 0.9 collective-permute-done.5.refs_2_.refs_10_.refs_9_
  43.5 0.6 shard_map.84
  44.1 5.5 %all-to-all-start.1 = ((f32[12,8,128]{2,1,0:T(8,128)}), f32[12,8,128]{2,1,0:T(8,128)S(1)}, u32[]{:S(2)}, u32[]{:S(2)}) async-start(f32[12,8,128]{2,1,0:T(8,128)} %shard_map.84), calls=%async_computation.1 | async-start | bytes 98304 | tf_op jit(solution)/shard_map/all_to_all | solution.py:634
  49.6 9.5 %all-to-all-done.1.refs_13_ = f32[12,8,128]{2,1,0:T(8,128)S(1)} async-done(((f32[12,8,128]{2,1,0:T(8,128)}), f32[12,8,128]{2,1,0:T(8,128)S(1)}, u32[]{:S(2)}, u32[]{:S(2)}) %all-to-all-start.1) | async-done | bytes 49184 | tf_op jit(solution)/shard_map/all_to_all | solution.py:634
  59.1 1.4 %shard_map.85 = (f32[3,4,8,256]{3,2,1,0:T(8,128)S(1)}, f32[3,4,8,256]{3,2,1,0:T(8,128)S(1)}, f32[64,256]{1,0:T(8,128)S(1)}, f32[64,256]{1,0:T(8,128)S(1)}, f32[1...) custom-call(f32[3,4,8,256]{3,2,1,0:T(8,128)S(1)} %copy-done.2, ...), custom_call_target="tpu_custom_call" | custom-call | tf_op jit(solution)/shard_map/pallas_call | solution.py:591
  60.5 4.8 %collective-permute-start.6 = (f32[64,256]{1,0:T(8,128)S(1)}, f32[64,256]{1,0:T(8,128)S(1)}, u32[]{:S(2)}, u32[]{:S(2)}) collective-permute-start(f32[64,256]{1,0:T(8,128)S(1)} %get-tuple-element.36), channel_id=1, source_target_pairs={{12,24},{36,48},{60,72},{84,96},{108,120},{132,144},{156,168},{180... | collective-permute-start | bytes 196616 | tf_op jit(solution)/shard_map/ppermute | solution.py:527
  65.4 1.9 %collective-permute-start.7 = (f32[64,256]{1,0:T(8,128)S(1)}, f32[64,256]{1,0:T(8,128)S(1)}, u32[]{:S(2)}, u32[]{:S(2)}) collective-permute-start(f32[64,256]{1,0:T(8,128)S(1)} %get-tuple-element.37), channel_id=1, source_target_pairs={{0,12},{24,36},{48,60},{72,84},{96,108},{120,132},{144,156},{168,1... | collective-permute-start | bytes 196616 | tf_op jit(solution)/shard_map/ppermute | solution.py:526
  67.3 0.0 collective-permute-done.6.refs_3_.refs_15_
  67.3 1.2 collective-permute-done.7.refs_4_.refs_16_
  68.5 0.7 shard_map.86
  69.2 3.5 %all-to-all-start.2 = ((f32[12,8,128]{2,1,0:T(8,128)}), f32[12,8,128]{2,1,0:T(8,128)S(1)}, u32[]{:S(2)}, u32[]{:S(2)}) async-start(f32[12,8,128]{2,1,0:T(8,128)} %get-tuple-element.38), calls=%async_computation.2 | async-start | bytes 98304 | tf_op jit(solution)/shard_map/all_to_all | solution.py:649
  72.7 0.7 collective-permute-start.8
  73.4 5.6 %collective-permute-start.9 = (f32[48,256]{1,0:T(8,128)S(1)}, f32[48,256]{1,0:T(8,128)S(1)}, u32[]{:S(2)}, u32[]{:S(2)}) collective-permute-start(f32[48,256]{1,0:T(8,128)S(1)} %get-tuple-element.41), channel_id=1, source_target_pairs={{0,1},{2,3},{4,5},{6,7},{8,9},{10,11},{1,0},{3,2},{5,4},{7,6},{9,8... | collective-permute-start | bytes 147464 | tf_op jit(solution)/shard_map/ppermute | solution.py:526
  79.0 1.8 %collective-permute-done.9.refs_18_ = f32[48,256]{1,0:T(8,128)S(1)} collective-permute-done((f32[48,256]{1,0:T(8,128)S(1)}, f32[48,256]{1,0:T(8,128)S(1)}, u32[]{:S(2)}, u32[]{:S(2)}) %collective-permute-start.9) | collective-permute-done | bytes 49184 | tf_op jit(solution)/shard_map/ppermute | solution.py:526
  80.9 1.2 all-to-all-done.2.refs_12_
  82.1 0.9 shard_map.87
  83.0 21.8 %all_to_all.25.refs_0_ = f32[64,1,128]{2,1,0:T(1,128)S(1)} all-to-all(f32[64,1,128]{2,1,0:T(1,128)S(1)} %get-tuple-element.42), channel_id=1, replica_groups=mesh['gx'=64,'gy'=12] {'gx'}, dimensions={0} | all-to-all | bytes 65536 | tf_op jit(solution)/shard_map/all_to_all | solution.py:656
  104.8 0.1 shard_map.88
  104.9 15.7 %all_to_all.26.refs_0_ = f32[12,1,128]{2,1,0:T(1,128)S(1)} all-to-all(f32[12,1,128]{2,1,0:T(1,128)S(1)} %shard_map.88), channel_id=1, replica_groups=mesh['gx'=64,'gy'=12] {'gy'}, dimensions={0} | all-to-all | bytes 12288 | tf_op jit(solution)/shard_map/all_to_all | solution.py:658
  120.6 0.9 shard_map.89
  (16 shorter events, 0.0 us)
Async XLA Ops:
  2.9 29.2 %copy-start.2 = (f32[3,4,8,256]{3,2,1,0:T(8,128)S(1)}, f32[3,4,8,256]{3,2,1,0:T(8,128)}, u32[]{:S(2)}) copy-start(f32[3,4,8,256]{3,2,1,0:T(8,128)} %refs_0_.6) | copy-start | bytes 294916
  2.9 29.2 %copy-start.4 = (s32[4,8,256]{2,1,0:T(8,128)S(1)}, s32[4,8,256]{2,1,0:T(8,128)}, u32[]{:S(2)}) copy-start(s32[4,8,256]{2,1,0:T(8,128)} %refs_5_.5) | copy-start | bytes 98308
  2.9 29.1 %all-to-all-start = ((f32[12,40,128]{2,1,0:T(8,128)}), f32[12,40,128]{2,1,0:T(8,128)S(1)}, u32[]{:S(2)}, u32[]{:S(2)}) async-start(f32[12,40,128]{2,1,0:T(8,128)} %get-tuple-element.27), calls=%async_computation | async-start | bytes 491520 | tf_op jit(solution)/shard_map/all_to_all | solution.py:626
  18.8 13.3 %collective-permute-start.2 = (f32[152,256]{1,0:T(8,128)S(1)}, f32[152,256]{1,0:T(8,128)S(1)}, u32[]{:S(2)}, u32[]{:S(2)}) collective-permute-start(f32[152,256]{1,0:T(8,128)S(1)} %get-tuple-element.28), channel_id=1, source_target_pairs={{1,2},{3,4},{5,6},{7,8},{9,10},{2,1},{4,3},{6,5},{8,7},{10,9},{13,... | collective-permute-start | bytes 466952 | tf_op jit(solution)/shard_map/ppermute | solution.py:527
  19.5 12.6 %collective-permute-start.3 = (f32[152,256]{1,0:T(8,128)S(1)}, f32[152,256]{1,0:T(8,128)S(1)}, u32[]{:S(2)}, u32[]{:S(2)}) collective-permute-start(f32[152,256]{1,0:T(8,128)S(1)} %get-tuple-element.29), channel_id=1, source_target_pairs={{0,1},{2,3},{4,5},{6,7},{8,9},{10,11},{1,0},{3,2},{5,4},{7,6},{9,8... | collective-permute-start | bytes 466952 | tf_op jit(solution)/shard_map/ppermute | solution.py:526
  25.2 24.4 %collective-permute-start = (f32[296,256]{1,0:T(8,128)S(1)}, f32[296,256]{1,0:T(8,128)S(1)}, u32[]{:S(2)}, u32[]{:S(2)}) collective-permute-start(f32[296,256]{1,0:T(8,128)S(1)} %get-tuple-element.25), channel_id=1, source_target_pairs={{12,24},{36,48},{60,72},{84,96},{108,120},{132,144},{156,168},{180... | collective-permute-start | bytes 909320 | tf_op jit(solution)/shard_map/ppermute | solution.py:527
  30.1 19.5 %collective-permute-start.1 = (f32[296,256]{1,0:T(8,128)S(1)}, f32[296,256]{1,0:T(8,128)S(1)}, u32[]{:S(2)}, u32[]{:S(2)}) collective-permute-start(f32[296,256]{1,0:T(8,128)S(1)} %get-tuple-element.26), channel_id=1, source_target_pairs={{0,12},{24,36},{48,60},{72,84},{96,108},{120,132},{144,156},{168,1... | collective-permute-start | bytes 909320 | tf_op jit(solution)/shard_map/ppermute | solution.py:526
  32.1 27.0 %copy-start.1 = (f32[6,4,8,256]{3,2,1,0:T(8,128)S(1)}, f32[6,4,8,256]{3,2,1,0:T(8,128)}, u32[]{:S(2)}) copy-start(f32[6,4,8,256]{3,2,1,0:T(8,128)} %refs_3_.5) | copy-start | bytes 589828
  32.1 27.0 %copy-start.3 = (f32[3,4,8,256]{3,2,1,0:T(8,128)S(1)}, f32[3,4,8,256]{3,2,1,0:T(8,128)}, u32[]{:S(2)}) copy-start(f32[3,4,8,256]{3,2,1,0:T(8,128)} %refs_2_.5) | copy-start | bytes 294916
  32.6 26.5 %copy-start = (f32[3,3,4,8,256]{4,3,2,1,0:T(8,128)S(1)}, f32[3,3,4,8,256]{4,3,2,1,0:T(8,128)}, u32[]{:S(2)}) copy-start(f32[3,3,4,8,256]{4,3,2,1,0:T(8,128)} %refs_1_.7) | copy-start | bytes 884740
  32.6 9.9 %collective-permute-start.4 = (f32[96,256]{1,0:T(8,128)S(1)}, f32[96,256]{1,0:T(8,128)S(1)}, u32[]{:S(2)}, u32[]{:S(2)}) collective-permute-start(f32[96,256]{1,0:T(8,128)S(1)} %get-tuple-element.30), channel_id=1, source_target_pairs={{12,24},{36,48},{60,72},{84,96},{108,120},{132,144},{156,168},{180... | collective-permute-start | bytes 294920 | tf_op jit(solution)/shard_map/ppermute | solution.py:527
  40.3 3.2 %collective-permute-start.5 = (f32[96,256]{1,0:T(8,128)S(1)}, f32[96,256]{1,0:T(8,128)S(1)}, u32[]{:S(2)}, u32[]{:S(2)}) collective-permute-start(f32[96,256]{1,0:T(8,128)S(1)} %get-tuple-element.31), channel_id=1, source_target_pairs={{0,12},{24,36},{48,60},{72,84},{96,108},{120,132},{144,156},{168,1... | collective-permute-start | bytes 294920 | tf_op jit(solution)/shard_map/ppermute | solution.py:526
  44.1 15.0 %copy-start.5 = (s32[4,8,256]{2,1,0:T(8,128)S(1)}, s32[4,8,256]{2,1,0:T(8,128)}, u32[]{:S(2)}) copy-start(s32[4,8,256]{2,1,0:T(8,128)} %refs_4_.5) | copy-start | bytes 98308
  44.1 15.0 %all-to-all-start.1 = ((f32[12,8,128]{2,1,0:T(8,128)}), f32[12,8,128]{2,1,0:T(8,128)S(1)}, u32[]{:S(2)}, u32[]{:S(2)}) async-start(f32[12,8,128]{2,1,0:T(8,128)} %shard_map.84), calls=%async_computation.1 | async-start | bytes 98304 | tf_op jit(solution)/shard_map/all_to_all | solution.py:634
  60.5 6.8 %collective-permute-start.6 = (f32[64,256]{1,0:T(8,128)S(1)}, f32[64,256]{1,0:T(8,128)S(1)}, u32[]{:S(2)}, u32[]{:S(2)}) collective-permute-start(f32[64,256]{1,0:T(8,128)S(1)} %get-tuple-element.36), channel_id=1, source_target_pairs={{12,24},{36,48},{60,72},{84,96},{108,120},{132,144},{156,168},{180... | collective-permute-start | bytes 196616 | tf_op jit(solution)/shard_map/ppermute | solution.py:527
  65.4 3.1 %collective-permute-start.7 = (f32[64,256]{1,0:T(8,128)S(1)}, f32[64,256]{1,0:T(8,128)S(1)}, u32[]{:S(2)}, u32[]{:S(2)}) collective-permute-start(f32[64,256]{1,0:T(8,128)S(1)} %get-tuple-element.37), channel_id=1, source_target_pairs={{0,12},{24,36},{48,60},{72,84},{96,108},{120,132},{144,156},{168,1... | collective-permute-start | bytes 196616 | tf_op jit(solution)/shard_map/ppermute | solution.py:526
  69.2 12.9 %all-to-all-start.2 = ((f32[12,8,128]{2,1,0:T(8,128)}), f32[12,8,128]{2,1,0:T(8,128)S(1)}, u32[]{:S(2)}, u32[]{:S(2)}) async-start(f32[12,8,128]{2,1,0:T(8,128)} %get-tuple-element.38), calls=%async_computation.2 | async-start | bytes 98304 | tf_op jit(solution)/shard_map/all_to_all | solution.py:649
  72.7 6.3 %collective-permute-start.8 = (f32[48,256]{1,0:T(8,128)S(1)}, f32[48,256]{1,0:T(8,128)S(1)}, u32[]{:S(2)}, u32[]{:S(2)}) collective-permute-start(f32[48,256]{1,0:T(8,128)S(1)} %get-tuple-element.40), channel_id=1, source_target_pairs={{1,2},{3,4},{5,6},{7,8},{9,10},{2,1},{4,3},{6,5},{8,7},{10,9},{13,... | collective-permute-start | bytes 147464 | tf_op jit(solution)/shard_map/ppermute | solution.py:527
  73.4 7.5 %collective-permute-start.9 = (f32[48,256]{1,0:T(8,128)S(1)}, f32[48,256]{1,0:T(8,128)S(1)}, u32[]{:S(2)}, u32[]{:S(2)}) collective-permute-start(f32[48,256]{1,0:T(8,128)S(1)} %get-tuple-element.41), channel_id=1, source_target_pairs={{0,1},{2,3},{4,5},{6,7},{8,9},{10,11},{1,0},{3,2},{5,4},{7,6},{9,8... | collective-permute-start | bytes 147464 | tf_op jit(solution)/shard_map/ppermute | solution.py:526

commit v5 on v4

--- a/solution.py
+++ b/solution.py
@@ -90,6 +90,10 @@
     return jnp.sum(total[:, :128] + total[:, 128:], axis=1, keepdims=True)
 
 
+def segment(ref, j, k):
+    return ref[j, :, 128 * k : 128 * k + 128]
+
+
 def coarse_terms(sums, columns_ref, terms_ref, group):
     lane = lax.broadcasted_iota(jnp.int32, (NC // 2, 128), 1)
     weights = jnp.where(
@@ -99,10 +103,12 @@
     )
     result = jnp.zeros(terms_ref.shape, F32)
     for j in range(group):
-        terms_ref[j : j + 1, :] = columns_ref[j, NC // 2 : NC // 2 + 1, :]
+        terms_ref[j : j + 1, :] = segment(columns_ref, j, NC // 2)
     owners = terms_ref[...]
     for j in range(group):
-        line = jnp.sum(columns_ref[j, : NC // 2, :] * weights, axis=0, keepdims=True)
+        line = segment(columns_ref, j, 0) * weights[:1]
+        for k in range(1, NC // 2):
+            line = line + segment(columns_ref, j, k) * weights[k : k + 1]
         line = line + pltpu.roll(line, NC, axis=1)
         result = result + jnp.where(owners == float(j), jnp.broadcast_to(line, result.shape), 0.0)
     return result
@@ -166,14 +172,16 @@
         copy.start()
     copies[0].wait()
     lane = lax.broadcasted_iota(jnp.int32, (NC // 2, 128), 1)
-    owner = jnp.full((8, 128), owner_ref[0, 0], jnp.int32).astype(F32)
+    owner = jnp.full((1, 128), owner_ref[0, 0], jnp.int32).astype(F32)
     for pair in range(group // 2):
         part = rows_ref[:, 128 * pair : 128 * pair + 128]
         flipped = jnp.concatenate([part, part], axis=0).T
         for odd in range(2):
             block = flipped[NC * odd : NC * odd + NC]
-            columns_ref[2 * pair + odd, : NC // 2, :] = jnp.where(lane < NC, block[: NC // 2], block[NC // 2 :])
-            columns_ref[2 * pair + odd, NC // 2 :, :] = owner
+            block = jnp.where(lane < NC, block[: NC // 2], block[NC // 2 :])
+            for k in range(NC // 2):
+                columns_ref[2 * pair + odd, :, 128 * k : 128 * k + 128] = block[k : k + 1]
+            columns_ref[2 * pair + odd, :, 64 * NC :] = owner
     for copy in copies[1:]:
         copy.wait()
     for out_ref in (up_ref, down_ref):
@@ -240,12 +248,11 @@
     lane = lax.broadcasted_iota(jnp.int32, (1, 128), 1)
     zero = jnp.zeros((1, 128), F32)
     for b in range(group):
-        slots_ref[b, 6:8, :] = jnp.zeros((2, 128), F32)
         for i, line in enumerate(three):
             after = line(b + 1) if b + 1 < group else zero
             before = line(b - 1) if b > 0 else zero
-            slots_ref[b, i : i + 1, :] = line(b)
-            slots_ref[b, 3 + i : 4 + i, :] = jnp.where(lane < NC, after, before)
+            slots_ref[b, :, 128 * i : 128 * i + 128] = line(b)
+            slots_ref[b, :, 128 * i + 384 : 128 * i + 512] = jnp.where(lane < NC, after, before)
 
 
 def three_groups(terms_ref, next_ref, previous_ref, start):
@@ -333,7 +340,7 @@
     if tile:
         index = index + jnp.where(row_index() < 4, 0, NC)
     line = 3 * tile + group
-    table = jnp.broadcast_to(coarse[line : line + 1, :], (ROWS, 128))
+    table = jnp.broadcast_to(coarse[:, 128 * line : 128 * line + 128], (ROWS, 128))
     found = [jnp.take_along_axis(table, index[:, 128 * h : 128 * h + 128], axis=1) for h in range(2)]
     return jnp.where(code >= 0.0, jnp.concatenate(found, axis=1), 0.0)
 
@@ -401,6 +408,7 @@
     zo_ref, w_ref, fore_ref, back_ref, terms_ref, source_ref, solved_ref,
     p_ref, q_ref, z_ref, scratch_ref, kappa_ref,
 ):
+    @functools.cache
     def owns(place):
         return Own(place, block_ref, mobility_ref, mask_ref)
 
@@ -457,6 +465,7 @@
     zo_ref, sums_ref,
     w_ref, p_ref, q_ref, z_ref, kappa_ref,
 ):
+    @functools.cache
     def owns(place):
         return Own(place, block_ref, mobility_ref, mask_ref)
 
@@ -616,7 +625,7 @@
     field = (3, XO, ROWS, 256)
     columns, y_halos, x_halos = call(
         functools.partial(pack_kernel, group),
-        [(group, 40, 128), Sent("gy", Y_TILES, True), Sent("gx", X_TILES, True)],
+        [(group, 1, 64 * NC + 128), Sent("gy", Y_TILES, True), Sent("gx", X_TILES, True)],
         [(ROWS, 256), coarse_rows.shape]
         + [pltpu.VMEM(arg.shape, arg.dtype) for arg in local]
         + [pltpu.SemaphoreType.DMA((7,))],
@@ -630,7 +639,7 @@
         [(16, 128)],
         right_side, cell_map, columns, y_halos,
     )
-    (slots,) = call(functools.partial(slots_kernel, group), [(group, 8, 128)], [], terms, corners)
+    (slots,) = call(functools.partial(slots_kernel, group), [(group, 1, 768)], [], terms, corners)
     slots = lax.all_to_all(slots, "gy", 0, 0)
     halos = (x_halos, corners, y_halos)
     work = [(24, ROWS, 256), (24, ROWS, 256), (3, 24, ROWS, 256)]
@@ -642,7 +651,7 @@
     )
     slots, y2_halos = call(
         functools.partial(forward_kernel, group),
-        [(group, 8, 128), Sent("gy", Y2_TILES, True)],
+        [(group, 1, 768), Sent("gy", Y2_TILES, True)],
         [],
         terms, source, solved, x2_halos,
     )

time: 122 us -> 120 us (0.984)
  starting transfers between devices: 60.6 us -> 59 us
    ppermute x5, starting transfers between devices: 18.7 us -> 17.5 us  [exchanged(): first = lax.ppermute(pair[0], self.axis, links[0])]
where the time goes in v5:
time: 120 us
  starting transfers between devices  59 us (49%)
  blocking collectives  37.6 us (31%)
  waiting for transfers between devices  14.8 us (12%)
  Pallas kernels  7.4 us (6%)
    all_to_all x1, blocking collectives, on_device(): sums = lax.all_to_all(sums, 'gx', 0, 0)  21.8 us
    ppermute x5, starting transfers between devices, exchanged(): first = lax.ppermute(pair[0], self.axis, links[0])  17.5 us
    ppermute x5, starting transfers between devices, exchanged(): second = lax.ppermute(pair[1], self.axis, links[1])  17.1 us
    all_to_all x1, blocking collectives, on_device(): sums = lax.all_to_all(sums, 'gy', 0, 0)  15.9 us
    all_to_all x1, starting transfers between devices, on_device(): columns = lax.all_to_all(columns, 'gy', 0, 0)  15.8 us
    all_to_all x2, waiting for transfers between devices, on_device(): slots = lax.all_to_all(slots, 'gy', 0, 0)  10.5 us
    all_to_all x2, starting transfers between devices, on_device(): slots = lax.all_to_all(slots, 'gy', 0, 0)  8.57 us
    pallas_call x8, Pallas kernels, call(): pl.pallas_call(body, out_shape=[jax.ShapeDtypeStruct(shape, F32) for shap...  7.4 us
  transfers between devices with their start and end apart: 13, of which 6 were waited for; matrix products, arithmetic and copies ran while one was open for 0% of the time, Pallas kernels for 1%

profile of v5, /device:TPU:1, one launch (start us, length us, event | category | flops | bytes accessed | tf_op | source)
XLA Modules:
  0.0 119.8 jit_solution(11234434236558786179)
XLA Ops:
  0.7 2.2 %shard_map.82 = (f32[12,1,4224]{2,1,0:T(1,128)}, f32[152,256]{1,0:T(8,128)S(1)}, f32[152,256]{1,0:T(8,128)S(1)}, f32[296,256]{1,0:T(8,128)S(1)}, f32[296,256]{1,0:T(8,128)S(1)}) custom-call(s32[1,1]{1,0:T(1,128)S(6)} %copy.9.refs_0_, f32[64,768]{1,0:T(8,128)} %refs_1_.4, f32[3,4,8,256]{3,2,1,0:T(8,128)} %refs_0_.6, f32[3,3,4,8,256]{4,3,2,1,0:T(8,128)} %refs_1_.7, ...), custom_call_target="tpu_custom_call" | custom-call | tf_op jit(solution)/shard_map/pallas_call | solution.py:600
  2.9 0.0 copy-start.2
  2.9 15.8 %all-to-all-start = ((f32[12,1,4224]{2,1,0:T(1,128)}), f32[12,1,4224]{2,1,0:T(1,128)S(1)}, u32[]{:S(2)}, u32[]{:S(2)}) async-start(f32[12,1,4224]{2,1,0:T(1,128)} %get-tuple-element.27), calls=%async_computation | async-start | bytes 405504 | tf_op jit(solution)/shard_map/all_to_all | solution.py:635
  18.8 0.7 collective-permute-start.2
  19.5 5.7 %collective-permute-start.3 = (f32[152,256]{1,0:T(8,128)S(1)}, f32[152,256]{1,0:T(8,128)S(1)}, u32[]{:S(2)}, u32[]{:S(2)}) collective-permute-start(f32[152,256]{1,0:T(8,128)S(1)} %get-tuple-element.29), channel_id=1, source_target_pairs={{0,1},{2,3},{4,5},{6,7},{8,9},{10,11},{1,0},{3,2},{5,4},{7,6},{9,8... | collective-permute-start | bytes 466952 | tf_op jit(solution)/shard_map/ppermute | solution.py:535
  25.2 4.9 %collective-permute-start = (f32[296,256]{1,0:T(8,128)S(1)}, f32[296,256]{1,0:T(8,128)S(1)}, u32[]{:S(2)}, u32[]{:S(2)}) collective-permute-start(f32[296,256]{1,0:T(8,128)S(1)} %get-tuple-element.25), channel_id=1, source_target_pairs={{12,24},{36,48},{60,72},{84,96},{108,120},{132,144},{156,168},{180... | collective-permute-start | bytes 909320 | tf_op jit(solution)/shard_map/ppermute | solution.py:536
  30.1 1.9 %collective-permute-start.1 = (f32[296,256]{1,0:T(8,128)S(1)}, f32[296,256]{1,0:T(8,128)S(1)}, u32[]{:S(2)}, u32[]{:S(2)}) collective-permute-start(f32[296,256]{1,0:T(8,128)S(1)} %get-tuple-element.26), channel_id=1, source_target_pairs={{0,12},{24,36},{48,60},{72,84},{96,108},{120,132},{144,156},{168,1... | collective-permute-start | bytes 909320 | tf_op jit(solution)/shard_map/ppermute | solution.py:535
  32.1 0.0 copy-start.5
  32.1 0.5 shard_map.83
  32.7 6.5 %collective-permute-start.4 = (f32[96,256]{1,0:T(8,128)S(1)}, f32[96,256]{1,0:T(8,128)S(1)}, u32[]{:S(2)}, u32[]{:S(2)}) collective-permute-start(f32[96,256]{1,0:T(8,128)S(1)} %get-tuple-element.30), channel_id=1, source_target_pairs={{12,24},{36,48},{60,72},{84,96},{108,120},{132,144},{156,168},{180... | collective-permute-start | bytes 294920 | tf_op jit(solution)/shard_map/ppermute | solution.py:536
  39.2 1.9 %collective-permute-start.5 = (f32[96,256]{1,0:T(8,128)S(1)}, f32[96,256]{1,0:T(8,128)S(1)}, u32[]{:S(2)}, u32[]{:S(2)}) collective-permute-start(f32[96,256]{1,0:T(8,128)S(1)} %get-tuple-element.31), channel_id=1, source_target_pairs={{0,12},{24,36},{48,60},{72,84},{96,108},{120,132},{144,156},{168,1... | collective-permute-start | bytes 294920 | tf_op jit(solution)/shard_map/ppermute | solution.py:535
  41.1 0.4 collective-permute-done.4.refs_1_.refs_9_.refs_8_
  41.5 0.9 collective-permute-done.5.refs_2_.refs_10_.refs_9_
  42.4 0.6 shard_map.84
  43.0 5.1 %all-to-all-start.1 = ((f32[12,1,768]{2,1,0:T(1,128)}), f32[12,1,768]{2,1,0:T(1,128)S(1)}, u32[]{:S(2)}, u32[]{:S(2)}) async-start(f32[12,1,768]{2,1,0:T(1,128)} %shard_map.84), calls=%async_computation.1 | async-start | bytes 73728 | tf_op jit(solution)/shard_map/all_to_all | solution.py:643
  48.1 9.4 %all-to-all-done.1.refs_13_ = f32[12,1,768]{2,1,0:T(1,128)S(1)} async-done(((f32[12,1,768]{2,1,0:T(1,128)}), f32[12,1,768]{2,1,0:T(1,128)S(1)}, u32[]{:S(2)}, u32[]{:S(2)}) %all-to-all-start.1) | async-done | bytes 36896 | tf_op jit(solution)/shard_map/all_to_all | solution.py:643
  57.6 1.4 %shard_map.85 = (f32[3,4,8,256]{3,2,1,0:T(8,128)S(1)}, f32[3,4,8,256]{3,2,1,0:T(8,128)S(1)}, f32[64,256]{1,0:T(8,128)S(1)}, f32[64,256]{1,0:T(8,128)S(1)}, f32[1...) custom-call(f32[3,4,8,256]{3,2,1,0:T(8,128)S(1)} %copy-done.2, ...), custom_call_target="tpu_custom_call" | custom-call | tf_op jit(solution)/shard_map/pallas_call | solution.py:600
  58.9 4.7 %collective-permute-start.6 = (f32[64,256]{1,0:T(8,128)S(1)}, f32[64,256]{1,0:T(8,128)S(1)}, u32[]{:S(2)}, u32[]{:S(2)}) collective-permute-start(f32[64,256]{1,0:T(8,128)S(1)} %get-tuple-element.36), channel_id=1, source_target_pairs={{12,24},{36,48},{60,72},{84,96},{108,120},{132,144},{156,168},{180... | collective-permute-start | bytes 196616 | tf_op jit(solution)/shard_map/ppermute | solution.py:536
  63.7 1.9 %collective-permute-start.7 = (f32[64,256]{1,0:T(8,128)S(1)}, f32[64,256]{1,0:T(8,128)S(1)}, u32[]{:S(2)}, u32[]{:S(2)}) collective-permute-start(f32[64,256]{1,0:T(8,128)S(1)} %get-tuple-element.37), channel_id=1, source_target_pairs={{0,12},{24,36},{48,60},{72,84},{96,108},{120,132},{144,156},{168,1... | collective-permute-start | bytes 196616 | tf_op jit(solution)/shard_map/ppermute | solution.py:535
  65.6 0.0 collective-permute-done.6.refs_3_.refs_15_
  65.6 1.2 %collective-permute-done.7.refs_4_.refs_16_ = f32[64,256]{1,0:T(8,128)S(1)} collective-permute-done((f32[64,256]{1,0:T(8,128)S(1)}, f32[64,256]{1,0:T(8,128)S(1)}, u32[]{:S(2)}, u32[]{:S(2)}) %collective-permute-start.7) | collective-permute-done | bytes 65568 | tf_op jit(solution)/shard_map/ppermute | solution.py:535
  66.8 0.7 shard_map.86
  67.5 3.5 %all-to-all-start.2 = ((f32[12,1,768]{2,1,0:T(1,128)}), f32[12,1,768]{2,1,0:T(1,128)S(1)}, u32[]{:S(2)}, u32[]{:S(2)}) async-start(f32[12,1,768]{2,1,0:T(1,128)} %get-tuple-element.38), calls=%async_computation.2 | async-start | bytes 73728 | tf_op jit(solution)/shard_map/all_to_all | solution.py:658
  71.0 0.7 collective-permute-start.8
  71.7 5.6 %collective-permute-start.9 = (f32[48,256]{1,0:T(8,128)S(1)}, f32[48,256]{1,0:T(8,128)S(1)}, u32[]{:S(2)}, u32[]{:S(2)}) collective-permute-start(f32[48,256]{1,0:T(8,128)S(1)} %get-tuple-element.41), channel_id=1, source_target_pairs={{0,1},{2,3},{4,5},{6,7},{8,9},{10,11},{1,0},{3,2},{5,4},{7,6},{9,8... | collective-permute-start | bytes 147464 | tf_op jit(solution)/shard_map/ppermute | solution.py:535
  77.3 1.8 %collective-permute-done.9.refs_18_ = f32[48,256]{1,0:T(8,128)S(1)} collective-permute-done((f32[48,256]{1,0:T(8,128)S(1)}, f32[48,256]{1,0:T(8,128)S(1)}, u32[]{:S(2)}, u32[]{:S(2)}) %collective-permute-start.9) | collective-permute-done | bytes 49184 | tf_op jit(solution)/shard_map/ppermute | solution.py:535
  79.1 1.1 all-to-all-done.2.refs_12_
  80.2 1.0 shard_map.87
  81.2 21.8 %all_to_all.25.refs_0_ = f32[64,1,128]{2,1,0:T(1,128)S(1)} all-to-all(f32[64,1,128]{2,1,0:T(1,128)S(1)} %get-tuple-element.42), channel_id=1, replica_groups=mesh['gx'=64,'gy'=12] {'gx'}, dimensions={0} | all-to-all | bytes 65536 | tf_op jit(solution)/shard_map/all_to_all | solution.py:665
  103.0 0.1 shard_map.88
  103.0 15.9 %all_to_all.26.refs_0_ = f32[12,1,128]{2,1,0:T(1,128)S(1)} all-to-all(f32[12,1,128]{2,1,0:T(1,128)S(1)} %shard_map.88), channel_id=1, replica_groups=mesh['gx'=64,'gy'=12] {'gy'}, dimensions={0} | all-to-all | bytes 12288 | tf_op jit(solution)/shard_map/all_to_all | solution.py:667
  118.9 0.9 shard_map.89
  (16 shorter events, 0.0 us)
Async XLA Ops:
  2.9 29.2 %copy-start.2 = (f32[3,4,8,256]{3,2,1,0:T(8,128)S(1)}, f32[3,4,8,256]{3,2,1,0:T(8,128)}, u32[]{:S(2)}) copy-start(f32[3,4,8,256]{3,2,1,0:T(8,128)} %refs_0_.6) | copy-start | bytes 294916
  2.9 29.2 %copy-start.4 = (s32[4,8,256]{2,1,0:T(8,128)S(1)}, s32[4,8,256]{2,1,0:T(8,128)}, u32[]{:S(2)}) copy-start(s32[4,8,256]{2,1,0:T(8,128)} %refs_5_.5) | copy-start | bytes 98308
  2.9 29.1 %all-to-all-start = ((f32[12,1,4224]{2,1,0:T(1,128)}), f32[12,1,4224]{2,1,0:T(1,128)S(1)}, u32[]{:S(2)}, u32[]{:S(2)}) async-start(f32[12,1,4224]{2,1,0:T(1,128)} %get-tuple-element.27), calls=%async_computation | async-start | bytes 405504 | tf_op jit(solution)/shard_map/all_to_all | solution.py:635
  18.8 13.3 %collective-permute-start.2 = (f32[152,256]{1,0:T(8,128)S(1)}, f32[152,256]{1,0:T(8,128)S(1)}, u32[]{:S(2)}, u32[]{:S(2)}) collective-permute-start(f32[152,256]{1,0:T(8,128)S(1)} %get-tuple-element.28), channel_id=1, source_target_pairs={{1,2},{3,4},{5,6},{7,8},{9,10},{2,1},{4,3},{6,5},{8,7},{10,9},{13,... | collective-permute-start | bytes 466952 | tf_op jit(solution)/shard_map/ppermute | solution.py:536
  19.5 12.6 %collective-permute-start.3 = (f32[152,256]{1,0:T(8,128)S(1)}, f32[152,256]{1,0:T(8,128)S(1)}, u32[]{:S(2)}, u32[]{:S(2)}) collective-permute-start(f32[152,256]{1,0:T(8,128)S(1)} %get-tuple-element.29), channel_id=1, source_target_pairs={{0,1},{2,3},{4,5},{6,7},{8,9},{10,11},{1,0},{3,2},{5,4},{7,6},{9,8... | collective-permute-start | bytes 466952 | tf_op jit(solution)/shard_map/ppermute | solution.py:535
  25.2 22.9 %collective-permute-start = (f32[296,256]{1,0:T(8,128)S(1)}, f32[296,256]{1,0:T(8,128)S(1)}, u32[]{:S(2)}, u32[]{:S(2)}) collective-permute-start(f32[296,256]{1,0:T(8,128)S(1)} %get-tuple-element.25), channel_id=1, source_target_pairs={{12,24},{36,48},{60,72},{84,96},{108,120},{132,144},{156,168},{180... | collective-permute-start | bytes 909320 | tf_op jit(solution)/shard_map/ppermute | solution.py:536
  30.1 18.0 %collective-permute-start.1 = (f32[296,256]{1,0:T(8,128)S(1)}, f32[296,256]{1,0:T(8,128)S(1)}, u32[]{:S(2)}, u32[]{:S(2)}) collective-permute-start(f32[296,256]{1,0:T(8,128)S(1)} %get-tuple-element.26), channel_id=1, source_target_pairs={{0,12},{24,36},{48,60},{72,84},{96,108},{120,132},{144,156},{168,1... | collective-permute-start | bytes 909320 | tf_op jit(solution)/shard_map/ppermute | solution.py:535
  32.1 25.5 %copy-start.1 = (f32[6,4,8,256]{3,2,1,0:T(8,128)S(1)}, f32[6,4,8,256]{3,2,1,0:T(8,128)}, u32[]{:S(2)}) copy-start(f32[6,4,8,256]{3,2,1,0:T(8,128)} %refs_3_.5) | copy-start | bytes 589828
  32.1 25.5 %copy-start.3 = (f32[3,4,8,256]{3,2,1,0:T(8,128)S(1)}, f32[3,4,8,256]{3,2,1,0:T(8,128)}, u32[]{:S(2)}) copy-start(f32[3,4,8,256]{3,2,1,0:T(8,128)} %refs_2_.5) | copy-start | bytes 294916
  32.1 25.4 %copy-start.5 = (s32[4,8,256]{2,1,0:T(8,128)S(1)}, s32[4,8,256]{2,1,0:T(8,128)}, u32[]{:S(2)}) copy-start(s32[4,8,256]{2,1,0:T(8,128)} %refs_4_.5) | copy-start | bytes 98308
  32.6 24.9 %copy-start = (f32[3,3,4,8,256]{4,3,2,1,0:T(8,128)S(1)}, f32[3,3,4,8,256]{4,3,2,1,0:T(8,128)}, u32[]{:S(2)}) copy-start(f32[3,3,4,8,256]{4,3,2,1,0:T(8,128)} %refs_1_.7) | copy-start | bytes 884740
  32.7 8.8 %collective-permute-start.4 = (f32[96,256]{1,0:T(8,128)S(1)}, f32[96,256]{1,0:T(8,128)S(1)}, u32[]{:S(2)}, u32[]{:S(2)}) collective-permute-start(f32[96,256]{1,0:T(8,128)S(1)} %get-tuple-element.30), channel_id=1, source_target_pairs={{12,24},{36,48},{60,72},{84,96},{108,120},{132,144},{156,168},{180... | collective-permute-start | bytes 294920 | tf_op jit(solution)/shard_map/ppermute | solution.py:536
  39.2 3.2 %collective-permute-start.5 = (f32[96,256]{1,0:T(8,128)S(1)}, f32[96,256]{1,0:T(8,128)S(1)}, u32[]{:S(2)}, u32[]{:S(2)}) collective-permute-start(f32[96,256]{1,0:T(8,128)S(1)} %get-tuple-element.31), channel_id=1, source_target_pairs={{0,12},{24,36},{48,60},{72,84},{96,108},{120,132},{144,156},{168,1... | collective-permute-start | bytes 294920 | tf_op jit(solution)/shard_map/ppermute | solution.py:535
  43.0 14.5 %all-to-all-start.1 = ((f32[12,1,768]{2,1,0:T(1,128)}), f32[12,1,768]{2,1,0:T(1,128)S(1)}, u32[]{:S(2)}, u32[]{:S(2)}) async-start(f32[12,1,768]{2,1,0:T(1,128)} %shard_map.84), calls=%async_computation.1 | async-start | bytes 73728 | tf_op jit(solution)/shard_map/all_to_all | solution.py:643
  58.9 6.7 %collective-permute-start.6 = (f32[64,256]{1,0:T(8,128)S(1)}, f32[64,256]{1,0:T(8,128)S(1)}, u32[]{:S(2)}, u32[]{:S(2)}) collective-permute-start(f32[64,256]{1,0:T(8,128)S(1)} %get-tuple-element.36), channel_id=1, source_target_pairs={{12,24},{36,48},{60,72},{84,96},{108,120},{132,144},{156,168},{180... | collective-permute-start | bytes 196616 | tf_op jit(solution)/shard_map/ppermute | solution.py:536
  63.7 3.1 %collective-permute-start.7 = (f32[64,256]{1,0:T(8,128)S(1)}, f32[64,256]{1,0:T(8,128)S(1)}, u32[]{:S(2)}, u32[]{:S(2)}) collective-permute-start(f32[64,256]{1,0:T(8,128)S(1)} %get-tuple-element.37), channel_id=1, source_target_pairs={{0,12},{24,36},{48,60},{72,84},{96,108},{120,132},{144,156},{168,1... | collective-permute-start | bytes 196616 | tf_op jit(solution)/shard_map/ppermute | solution.py:535
  67.5 12.7 %all-to-all-start.2 = ((f32[12,1,768]{2,1,0:T(1,128)}), f32[12,1,768]{2,1,0:T(1,128)S(1)}, u32[]{:S(2)}, u32[]{:S(2)}) async-start(f32[12,1,768]{2,1,0:T(1,128)} %get-tuple-element.38), calls=%async_computation.2 | async-start | bytes 73728 | tf_op jit(solution)/shard_map/all_to_all | solution.py:658
  71.0 6.3 %collective-permute-start.8 = (f32[48,256]{1,0:T(8,128)S(1)}, f32[48,256]{1,0:T(8,128)S(1)}, u32[]{:S(2)}, u32[]{:S(2)}) collective-permute-start(f32[48,256]{1,0:T(8,128)S(1)} %get-tuple-element.40), channel_id=1, source_target_pairs={{1,2},{3,4},{5,6},{7,8},{9,10},{2,1},{4,3},{6,5},{8,7},{10,9},{13,... | collective-permute-start | bytes 147464 | tf_op jit(solution)/shard_map/ppermute | solution.py:536
  71.7 7.5 %collective-permute-start.9 = (f32[48,256]{1,0:T(8,128)S(1)}, f32[48,256]{1,0:T(8,128)S(1)}, u32[]{:S(2)}, u32[]{:S(2)}) collective-permute-start(f32[48,256]{1,0:T(8,128)S(1)} %get-tuple-element.41), channel_id=1, source_target_pairs={{0,1},{2,3},{4,5},{6,7},{8,9},{10,11},{1,0},{3,2},{5,4},{7,6},{9,8... | collective-permute-start | bytes 147464 | tf_op jit(solution)/shard_map/ppermute | solution.py:535

commit v6 on v5

--- a/solution.py
+++ b/solution.py
@@ -14,9 +14,9 @@
 NC = 64
 
 X_FIELD, X_VEM, X_TILES = 4, 28, 37
-C_CELL13, C_CELL2, C_COARSE, C_TILES = 8, 9, 10, 12
+C_CELL13, C_CELL2, C_COARSE, C_TILES = 8, 9, 10, 11
 Y_FIELD, Y_LAST, Y_TILES = 2, 18, 19
-X2_S, X2_COARSE, X2_TILES = 3, 6, 8
+X2_S, X2_COARSE, X2_TILES = 3, 6, 7
 Y2_V, Y2_TILES = 4, 6
 Y2_PLACES = (0, 1, 2, 3, 4, 5, 10, 11)
 
@@ -240,8 +240,8 @@
         near, mid, far = [y_halo(yn_ref, yp_ref, 0, at(d)) for d in (1, 2, 3)]
         put(out_ref, C_CELL13, jnp.where(middle, turned(far, 4), near))
         put(out_ref, C_CELL2, mid)
-        out_ref[8 * C_COARSE :, :128] = terms
-        out_ref[8 * C_COARSE :, 128:] = jnp.zeros((16, 128), F32)
+        out_ref[8 * C_COARSE :, :128] = terms[:8]
+        out_ref[8 * C_COARSE :, 128:] = terms[8:]
 
 
 def write_slots(group, slots_ref, three):
@@ -258,8 +258,8 @@
 def three_groups(terms_ref, next_ref, previous_ref, start):
     return (
         lambda b: terms_ref[b : b + 1, :],
-        lambda b: next_ref[start + b : start + b + 1, :128],
-        lambda b: previous_ref[start + b : start + b + 1, :128],
+        lambda b: next_ref[start + b % 8 : start + b % 8 + 1, 128 * (b // 8) : 128 * (b // 8) + 128],
+        lambda b: previous_ref[start + b % 8 : start + b % 8 + 1, 128 * (b // 8) : 128 * (b // 8) + 128],
     )
 
 
@@ -455,8 +455,8 @@
     terms = coarse_terms(sums, columns_ref, scratch_ref, group)
     terms_ref[...] = terms
     for out_ref in (fore_ref, back_ref):
-        out_ref[8 * X2_COARSE :, :128] = terms
-        out_ref[8 * X2_COARSE :, 128:] = jnp.zeros((16, 128), F32)
+        out_ref[8 * X2_COARSE :, :128] = terms[:8]
+        out_ref[8 * X2_COARSE :, 128:] = terms[8:]
 
 
 def second_kernel(

time: 120 us -> 120 us (level)
  no operation moved by 1% of the time
where the time goes in v6:
time: 120 us
  starting transfers between devices  59 us (49%)
  blocking collectives  37.5 us (31%)
  waiting for transfers between devices  14.8 us (12%)
  Pallas kernels  7.4 us (6%)
    all_to_all x1, blocking collectives, on_device(): sums = lax.all_to_all(sums, 'gx', 0, 0)  21.6 us
    ppermute x5, starting transfers between devices, exchanged(): first = lax.ppermute(pair[0], self.axis, links[0])  17.5 us
    ppermute x5, starting transfers between devices, exchanged(): second = lax.ppermute(pair[1], self.axis, links[1])  17.1 us
    all_to_all x1, blocking collectives, on_device(): sums = lax.all_to_all(sums, 'gy', 0, 0)  15.9 us
    all_to_all x1, starting transfers between devices, on_device(): columns = lax.all_to_all(columns, 'gy', 0, 0)  15.8 us
    all_to_all x2, waiting for transfers between devices, on_device(): slots = lax.all_to_all(slots, 'gy', 0, 0)  10.5 us
    all_to_all x2, starting transfers between devices, on_device(): slots = lax.all_to_all(slots, 'gy', 0, 0)  8.57 us
    pallas_call x8, Pallas kernels, call(): pl.pallas_call(body, out_shape=[jax.ShapeDtypeStruct(shape, F32) for shap...  7.4 us
  transfers between devices with their start and end apart: 13, of which 6 were waited for; matrix products, arithmetic and copies ran while one was open for 0% of the time, Pallas kernels for 1%

profile of v6, /device:TPU:1, one launch (start us, length us, event | category | flops | bytes accessed | tf_op | source)
XLA Modules:
  0.0 119.6 jit_solution(10732331335623672100)
XLA Ops:
  0.7 2.2 %shard_map.82 = (f32[12,1,4224]{2,1,0:T(1,128)}, f32[152,256]{1,0:T(8,128)S(1)}, f32[152,256]{1,0:T(8,128)S(1)}, f32[296,256]{1,0:T(8,128)S(1)}, f32[296,256]{1,0:T(8,128)S(1)}) custom-call(s32[1,1]{1,0:T(1,128)S(6)} %copy.9.refs_0_, f32[64,768]{1,0:T(8,128)} %refs_1_.4, f32[3,4,8,256]{3,2,1,0:T(8,128)} %refs_0_.6, f32[3,3,4,8,256]{4,3,2,1,0:T(8,128)} %refs_1_.7, ...), custom_call_target="tpu_custom_call" | custom-call | tf_op jit(solution)/shard_map/pallas_call | solution.py:600
  2.9 0.0 copy-start.4
  2.9 15.8 %all-to-all-start = ((f32[12,1,4224]{2,1,0:T(1,128)}), f32[12,1,4224]{2,1,0:T(1,128)S(1)}, u32[]{:S(2)}, u32[]{:S(2)}) async-start(f32[12,1,4224]{2,1,0:T(1,128)} %get-tuple-element.27), calls=%async_computation | async-start | bytes 405504 | tf_op jit(solution)/shard_map/all_to_all | solution.py:635
  18.8 0.7 collective-permute-start.2
  19.5 5.7 %collective-permute-start.3 = (f32[152,256]{1,0:T(8,128)S(1)}, f32[152,256]{1,0:T(8,128)S(1)}, u32[]{:S(2)}, u32[]{:S(2)}) collective-permute-start(f32[152,256]{1,0:T(8,128)S(1)} %get-tuple-element.29), channel_id=1, source_target_pairs={{0,1},{2,3},{4,5},{6,7},{8,9},{10,11},{1,0},{3,2},{5,4},{7,6},{9,8... | collective-permute-start | bytes 466952 | tf_op jit(solution)/shard_map/ppermute | solution.py:535
  25.2 4.9 %collective-permute-start = (f32[296,256]{1,0:T(8,128)S(1)}, f32[296,256]{1,0:T(8,128)S(1)}, u32[]{:S(2)}, u32[]{:S(2)}) collective-permute-start(f32[296,256]{1,0:T(8,128)S(1)} %get-tuple-element.25), channel_id=1, source_target_pairs={{12,24},{36,48},{60,72},{84,96},{108,120},{132,144},{156,168},{180... | collective-permute-start | bytes 909320 | tf_op jit(solution)/shard_map/ppermute | solution.py:536
  30.1 1.9 %collective-permute-start.1 = (f32[296,256]{1,0:T(8,128)S(1)}, f32[296,256]{1,0:T(8,128)S(1)}, u32[]{:S(2)}, u32[]{:S(2)}) collective-permute-start(f32[296,256]{1,0:T(8,128)S(1)} %get-tuple-element.26), channel_id=1, source_target_pairs={{0,12},{24,36},{48,60},{72,84},{96,108},{120,132},{144,156},{168,1... | collective-permute-start | bytes 909320 | tf_op jit(solution)/shard_map/ppermute | solution.py:535
  32.1 0.0 copy-start.3
  32.1 0.0 copy-start.5
  32.1 0.5 shard_map.83
  32.7 6.5 %collective-permute-start.4 = (f32[88,256]{1,0:T(8,128)S(1)}, f32[88,256]{1,0:T(8,128)S(1)}, u32[]{:S(2)}, u32[]{:S(2)}) collective-permute-start(f32[88,256]{1,0:T(8,128)S(1)} %get-tuple-element.30), channel_id=1, source_target_pairs={{12,24},{36,48},{60,72},{84,96},{108,120},{132,144},{156,168},{180... | collective-permute-start | bytes 270344 | tf_op jit(solution)/shard_map/ppermute | solution.py:536
  39.2 1.9 %collective-permute-start.5 = (f32[88,256]{1,0:T(8,128)S(1)}, f32[88,256]{1,0:T(8,128)S(1)}, u32[]{:S(2)}, u32[]{:S(2)}) collective-permute-start(f32[88,256]{1,0:T(8,128)S(1)} %get-tuple-element.31), channel_id=1, source_target_pairs={{0,12},{24,36},{48,60},{72,84},{96,108},{120,132},{144,156},{168,1... | collective-permute-start | bytes 270344 | tf_op jit(solution)/shard_map/ppermute | solution.py:535
  41.1 0.3 collective-permute-done.4.refs_1_.refs_9_.refs_8_
  41.4 1.0 collective-permute-done.5.refs_2_.refs_10_.refs_9_
  42.4 0.6 shard_map.84
  43.0 5.1 %all-to-all-start.1 = ((f32[12,1,768]{2,1,0:T(1,128)}), f32[12,1,768]{2,1,0:T(1,128)S(1)}, u32[]{:S(2)}, u32[]{:S(2)}) async-start(f32[12,1,768]{2,1,0:T(1,128)} %shard_map.84), calls=%async_computation.1 | async-start | bytes 73728 | tf_op jit(solution)/shard_map/all_to_all | solution.py:643
  48.1 9.4 %all-to-all-done.1.refs_13_ = f32[12,1,768]{2,1,0:T(1,128)S(1)} async-done(((f32[12,1,768]{2,1,0:T(1,128)}), f32[12,1,768]{2,1,0:T(1,128)S(1)}, u32[]{:S(2)}, u32[]{:S(2)}) %all-to-all-start.1) | async-done | bytes 36896 | tf_op jit(solution)/shard_map/all_to_all | solution.py:643
  57.5 1.4 %shard_map.85 = (f32[3,4,8,256]{3,2,1,0:T(8,128)S(1)}, f32[3,4,8,256]{3,2,1,0:T(8,128)S(1)}, f32[56,256]{1,0:T(8,128)S(1)}, f32[56,256]{1,0:T(8,128)S(1)}, f32[1...) custom-call(f32[3,4,8,256]{3,2,1,0:T(8,128)S(1)} %copy-done.2, ...), custom_call_target="tpu_custom_call" | custom-call | tf_op jit(solution)/shard_map/pallas_call | solution.py:600
  58.9 4.7 %collective-permute-start.6 = (f32[56,256]{1,0:T(8,128)S(1)}, f32[56,256]{1,0:T(8,128)S(1)}, u32[]{:S(2)}, u32[]{:S(2)}) collective-permute-start(f32[56,256]{1,0:T(8,128)S(1)} %get-tuple-element.36), channel_id=1, source_target_pairs={{12,24},{36,48},{60,72},{84,96},{108,120},{132,144},{156,168},{180... | collective-permute-start | bytes 172040 | tf_op jit(solution)/shard_map/ppermute | solution.py:536
  63.6 1.9 %collective-permute-start.7 = (f32[56,256]{1,0:T(8,128)S(1)}, f32[56,256]{1,0:T(8,128)S(1)}, u32[]{:S(2)}, u32[]{:S(2)}) collective-permute-start(f32[56,256]{1,0:T(8,128)S(1)} %get-tuple-element.37), channel_id=1, source_target_pairs={{0,12},{24,36},{48,60},{72,84},{96,108},{120,132},{144,156},{168,1... | collective-permute-start | bytes 172040 | tf_op jit(solution)/shard_map/ppermute | solution.py:535
  65.6 1.2 %collective-permute-done.7.refs_4_.refs_16_ = f32[56,256]{1,0:T(8,128)S(1)} collective-permute-done((f32[56,256]{1,0:T(8,128)S(1)}, f32[56,256]{1,0:T(8,128)S(1)}, u32[]{:S(2)}, u32[]{:S(2)}) %collective-permute-start.7) | collective-permute-done | bytes 57376 | tf_op jit(solution)/shard_map/ppermute | solution.py:535
  66.8 0.7 shard_map.86
  67.4 3.5 %all-to-all-start.2 = ((f32[12,1,768]{2,1,0:T(1,128)}), f32[12,1,768]{2,1,0:T(1,128)S(1)}, u32[]{:S(2)}, u32[]{:S(2)}) async-start(f32[12,1,768]{2,1,0:T(1,128)} %get-tuple-element.38), calls=%async_computation.2 | async-start | bytes 73728 | tf_op jit(solution)/shard_map/all_to_all | solution.py:658
  70.9 0.7 collective-permute-start.8
  71.6 5.6 %collective-permute-start.9 = (f32[48,256]{1,0:T(8,128)S(1)}, f32[48,256]{1,0:T(8,128)S(1)}, u32[]{:S(2)}, u32[]{:S(2)}) collective-permute-start(f32[48,256]{1,0:T(8,128)S(1)} %get-tuple-element.41), channel_id=1, source_target_pairs={{0,1},{2,3},{4,5},{6,7},{8,9},{10,11},{1,0},{3,2},{5,4},{7,6},{9,8... | collective-permute-start | bytes 147464 | tf_op jit(solution)/shard_map/ppermute | solution.py:535
  77.3 1.8 %collective-permute-done.9.refs_18_ = f32[48,256]{1,0:T(8,128)S(1)} collective-permute-done((f32[48,256]{1,0:T(8,128)S(1)}, f32[48,256]{1,0:T(8,128)S(1)}, u32[]{:S(2)}, u32[]{:S(2)}) %collective-permute-start.9) | collective-permute-done | bytes 49184 | tf_op jit(solution)/shard_map/ppermute | solution.py:535
  79.1 1.1 all-to-all-done.2.refs_12_
  80.1 1.0 shard_map.87
  81.1 21.6 %all_to_all.25.refs_0_ = f32[64,1,128]{2,1,0:T(1,128)S(1)} all-to-all(f32[64,1,128]{2,1,0:T(1,128)S(1)} %get-tuple-element.42), channel_id=1, replica_groups=mesh['gx'=64,'gy'=12] {'gx'}, dimensions={0} | all-to-all | bytes 65536 | tf_op jit(solution)/shard_map/all_to_all | solution.py:665
  102.8 0.1 shard_map.88
  102.9 15.9 %all_to_all.26.refs_0_ = f32[12,1,128]{2,1,0:T(1,128)S(1)} all-to-all(f32[12,1,128]{2,1,0:T(1,128)S(1)} %shard_map.88), channel_id=1, replica_groups=mesh['gx'=64,'gy'=12] {'gy'}, dimensions={0} | all-to-all | bytes 12288 | tf_op jit(solution)/shard_map/all_to_all | solution.py:667
  118.7 0.9 shard_map.89
  (16 shorter events, 0.0 us)
Async XLA Ops:
  2.9 29.2 %copy-start.2 = (f32[3,4,8,256]{3,2,1,0:T(8,128)S(1)}, f32[3,4,8,256]{3,2,1,0:T(8,128)}, u32[]{:S(2)}) copy-start(f32[3,4,8,256]{3,2,1,0:T(8,128)} %refs_0_.6) | copy-start | bytes 294916
  2.9 29.2 %copy-start.4 = (s32[4,8,256]{2,1,0:T(8,128)S(1)}, s32[4,8,256]{2,1,0:T(8,128)}, u32[]{:S(2)}) copy-start(s32[4,8,256]{2,1,0:T(8,128)} %refs_5_.5) | copy-start | bytes 98308
  2.9 29.1 %all-to-all-start = ((f32[12,1,4224]{2,1,0:T(1,128)}), f32[12,1,4224]{2,1,0:T(1,128)S(1)}, u32[]{:S(2)}, u32[]{:S(2)}) async-start(f32[12,1,4224]{2,1,0:T(1,128)} %get-tuple-element.27), calls=%async_computation | async-start | bytes 405504 | tf_op jit(solution)/shard_map/all_to_all | solution.py:635
  18.8 13.3 %collective-permute-start.2 = (f32[152,256]{1,0:T(8,128)S(1)}, f32[152,256]{1,0:T(8,128)S(1)}, u32[]{:S(2)}, u32[]{:S(2)}) collective-permute-start(f32[152,256]{1,0:T(8,128)S(1)} %get-tuple-element.28), channel_id=1, source_target_pairs={{1,2},{3,4},{5,6},{7,8},{9,10},{2,1},{4,3},{6,5},{8,7},{10,9},{13,... | collective-permute-start | bytes 466952 | tf_op jit(solution)/shard_map/ppermute | solution.py:536
  19.5 12.6 %collective-permute-start.3 = (f32[152,256]{1,0:T(8,128)S(1)}, f32[152,256]{1,0:T(8,128)S(1)}, u32[]{:S(2)}, u32[]{:S(2)}) collective-permute-start(f32[152,256]{1,0:T(8,128)S(1)} %get-tuple-element.29), channel_id=1, source_target_pairs={{0,1},{2,3},{4,5},{6,7},{8,9},{10,11},{1,0},{3,2},{5,4},{7,6},{9,8... | collective-permute-start | bytes 466952 | tf_op jit(solution)/shard_map/ppermute | solution.py:535
  25.2 22.9 %collective-permute-start = (f32[296,256]{1,0:T(8,128)S(1)}, f32[296,256]{1,0:T(8,128)S(1)}, u32[]{:S(2)}, u32[]{:S(2)}) collective-permute-start(f32[296,256]{1,0:T(8,128)S(1)} %get-tuple-element.25), channel_id=1, source_target_pairs={{12,24},{36,48},{60,72},{84,96},{108,120},{132,144},{156,168},{180... | collective-permute-start | bytes 909320 | tf_op jit(solution)/shard_map/ppermute | solution.py:536
  30.1 18.0 %collective-permute-start.1 = (f32[296,256]{1,0:T(8,128)S(1)}, f32[296,256]{1,0:T(8,128)S(1)}, u32[]{:S(2)}, u32[]{:S(2)}) collective-permute-start(f32[296,256]{1,0:T(8,128)S(1)} %get-tuple-element.26), channel_id=1, source_target_pairs={{0,12},{24,36},{48,60},{72,84},{96,108},{120,132},{144,156},{168,1... | collective-permute-start | bytes 909320 | tf_op jit(solution)/shard_map/ppermute | solution.py:535
  32.1 25.4 %copy-start.1 = (f32[6,4,8,256]{3,2,1,0:T(8,128)S(1)}, f32[6,4,8,256]{3,2,1,0:T(8,128)}, u32[]{:S(2)}) copy-start(f32[6,4,8,256]{3,2,1,0:T(8,128)} %refs_3_.5) | copy-start | bytes 589828
  32.1 25.4 %copy-start.3 = (f32[3,4,8,256]{3,2,1,0:T(8,128)S(1)}, f32[3,4,8,256]{3,2,1,0:T(8,128)}, u32[]{:S(2)}) copy-start(f32[3,4,8,256]{3,2,1,0:T(8,128)} %refs_2_.5) | copy-start | bytes 294916
  32.1 25.4 %copy-start.5 = (s32[4,8,256]{2,1,0:T(8,128)S(1)}, s32[4,8,256]{2,1,0:T(8,128)}, u32[]{:S(2)}) copy-start(s32[4,8,256]{2,1,0:T(8,128)} %refs_4_.5) | copy-start | bytes 98308
  32.6 24.9 %copy-start = (f32[3,3,4,8,256]{4,3,2,1,0:T(8,128)S(1)}, f32[3,3,4,8,256]{4,3,2,1,0:T(8,128)}, u32[]{:S(2)}) copy-start(f32[3,3,4,8,256]{4,3,2,1,0:T(8,128)} %refs_1_.7) | copy-start | bytes 884740
  32.7 8.7 %collective-permute-start.4 = (f32[88,256]{1,0:T(8,128)S(1)}, f32[88,256]{1,0:T(8,128)S(1)}, u32[]{:S(2)}, u32[]{:S(2)}) collective-permute-start(f32[88,256]{1,0:T(8,128)S(1)} %get-tuple-element.30), channel_id=1, source_target_pairs={{12,24},{36,48},{60,72},{84,96},{108,120},{132,144},{156,168},{180... | collective-permute-start | bytes 270344 | tf_op jit(solution)/shard_map/ppermute | solution.py:536
  39.2 3.2 %collective-permute-start.5 = (f32[88,256]{1,0:T(8,128)S(1)}, f32[88,256]{1,0:T(8,128)S(1)}, u32[]{:S(2)}, u32[]{:S(2)}) collective-permute-start(f32[88,256]{1,0:T(8,128)S(1)} %get-tuple-element.31), channel_id=1, source_target_pairs={{0,12},{24,36},{48,60},{72,84},{96,108},{120,132},{144,156},{168,1... | collective-permute-start | bytes 270344 | tf_op jit(solution)/shard_map/ppermute | solution.py:535
  43.0 14.5 %all-to-all-start.1 = ((f32[12,1,768]{2,1,0:T(1,128)}), f32[12,1,768]{2,1,0:T(1,128)S(1)}, u32[]{:S(2)}, u32[]{:S(2)}) async-start(f32[12,1,768]{2,1,0:T(1,128)} %shard_map.84), calls=%async_computation.1 | async-start | bytes 73728 | tf_op jit(solution)/shard_map/all_to_all | solution.py:643
  58.9 6.7 %collective-permute-start.6 = (f32[56,256]{1,0:T(8,128)S(1)}, f32[56,256]{1,0:T(8,128)S(1)}, u32[]{:S(2)}, u32[]{:S(2)}) collective-permute-start(f32[56,256]{1,0:T(8,128)S(1)} %get-tuple-element.36), channel_id=1, source_target_pairs={{12,24},{36,48},{60,72},{84,96},{108,120},{132,144},{156,168},{180... | collective-permute-start | bytes 172040 | tf_op jit(solution)/shard_map/ppermute | solution.py:536
  63.6 3.1 %collective-permute-start.7 = (f32[56,256]{1,0:T(8,128)S(1)}, f32[56,256]{1,0:T(8,128)S(1)}, u32[]{:S(2)}, u32[]{:S(2)}) collective-permute-start(f32[56,256]{1,0:T(8,128)S(1)} %get-tuple-element.37), channel_id=1, source_target_pairs={{0,12},{24,36},{48,60},{72,84},{96,108},{120,132},{144,156},{168,1... | collective-permute-start | bytes 172040 | tf_op jit(solution)/shard_map/ppermute | solution.py:535
  67.4 12.7 %all-to-all-start.2 = ((f32[12,1,768]{2,1,0:T(1,128)}), f32[12,1,768]{2,1,0:T(1,128)S(1)}, u32[]{:S(2)}, u32[]{:S(2)}) async-start(f32[12,1,768]{2,1,0:T(1,128)} %get-tuple-element.38), calls=%async_computation.2 | async-start | bytes 73728 | tf_op jit(solution)/shard_map/all_to_all | solution.py:658
  70.9 6.3 %collective-permute-start.8 = (f32[48,256]{1,0:T(8,128)S(1)}, f32[48,256]{1,0:T(8,128)S(1)}, u32[]{:S(2)}, u32[]{:S(2)}) collective-permute-start(f32[48,256]{1,0:T(8,128)S(1)} %get-tuple-element.40), channel_id=1, source_target_pairs={{1,2},{3,4},{5,6},{7,8},{9,10},{2,1},{4,3},{6,5},{8,7},{10,9},{13,... | collective-permute-start | bytes 147464 | tf_op jit(solution)/shard_map/ppermute | solution.py:536
  71.6 7.5 %collective-permute-start.9 = (f32[48,256]{1,0:T(8,128)S(1)}, f32[48,256]{1,0:T(8,128)S(1)}, u32[]{:S(2)}, u32[]{:S(2)}) collective-permute-start(f32[48,256]{1,0:T(8,128)S(1)} %get-tuple-element.41), channel_id=1, source_target_pairs={{0,1},{2,3},{4,5},{6,7},{8,9},{10,11},{1,0},{3,2},{5,4},{7,6},{9,8... | collective-permute-start | bytes 147464 | tf_op jit(solution)/shard_map/ppermute | solution.py:535
